TPU v7x, 32 devices: a whole 2x2x4 slice. The times are simulated.
32 devices in a mesh: exp: 8 (over y, x, core), fsdp: 4 (over z).
Axes of the slice: x: 2, y: 2, z: 4, core: 2. Of those that a mesh axis runs over, the one named last changes fastest.
Arguments:
- block_input: bfloat16 [2, 16, 4, 8, 48, 1024], P(None, 'exp', 'fsdp'), may hold values from -6 to 6
- expert_ids: int32 [2, 32, 512, 1], P(None, ('exp', 'fsdp')), may hold values from 0 to 15; in each aligned block of 512 rows (0 to 511, 512 to 1023, ..., all dimensions but the last counted through in order) at most 48 rows name the same one
- seq_lengths: int32 [2, 32], P(None, ('exp', 'fsdp')), may hold values from 64 to 512, as said below
- attn_norm_gain: bfloat16 [1024], P(('exp', 'fsdp')), may hold values from 0.5 to 1.5
- attn_norm_bias: bfloat16 [1024], P(('exp', 'fsdp')), may hold values from -1.25 to 1.25
- query_matrix: bfloat16 [1024, 1024], P(('exp', 'fsdp')), may hold values from -0.1875 to 0.1875
- query_offset_bias: bfloat16 [1024], P(('exp', 'fsdp')), may hold values from -1.25 to 1.25
- key_matrix: bfloat16 [1024, 1024], P(('exp', 'fsdp')), may hold values from -0.1875 to 0.1875
- value_matrix: bfloat16 [1024, 1024], P(('exp', 'fsdp')), may hold values from -0.1875 to 0.1875
- value_offset_bias: bfloat16 [1024], P(('exp', 'fsdp')), may hold values from -1.25 to 1.25
- output_matrix: bfloat16 [1024, 1024], P(('exp', 'fsdp')), may hold values from -0.75 to 0.75
- attention_output_bias: bfloat16 [1024], P(('exp', 'fsdp')), may hold values from -0.625 to 0.625
- ffn_norm_gain: bfloat16 [1024], P(('exp', 'fsdp')), may hold values from 0.5 to 1.5
- ffn_norm_bias: bfloat16 [1024], P(('exp', 'fsdp')), may hold values from -1.25 to 1.25
- expert_in: bfloat16 [16, 1024, 4096], P('exp', None, 'fsdp'), may hold values from -0.1875 to 0.1875
- expert_in_bias: bfloat16 [16, 4096], P('exp', 'fsdp'), may hold values from -0.625 to 0.625
- expert_out: bfloat16 [16, 4096, 1024], P('exp', 'fsdp'), may hold values from -0.09375 to 0.09375
- expert_out_bias: bfloat16 [16, 1024], P('exp', 'fsdp'), may hold values from -0.625 to 0.625
- out_cotangent: bfloat16 [2, 16, 4, 8, 48, 1024], P(None, 'exp', 'fsdp'), may hold values from -6 to 6
Outputs:
- block_output: bfloat16 [2, 16, 4, 8, 48, 1024], P(None, 'exp', 'fsdp')
- input_grad: bfloat16 [2, 16, 4, 8, 48, 1024], P(None, 'exp', 'fsdp')
- grad_attn_gain: float32 [1024], P(('exp', 'fsdp'))
- grad_attn_bias: float32 [1024], P(('exp', 'fsdp'))
- grad_query: float32 [1024, 1024], P(('exp', 'fsdp'))
- grad_query_bias: float32 [1024], P(('exp', 'fsdp'))
- grad_key: float32 [1024, 1024], P(('exp', 'fsdp'))
- grad_value: float32 [1024, 1024], P(('exp', 'fsdp'))
- grad_value_bias: float32 [1024], P(('exp', 'fsdp'))
- grad_output: float32 [1024, 1024], P(('exp', 'fsdp'))
- grad_output_bias: float32 [1024], P(('exp', 'fsdp'))
- grad_ffn_gain: float32 [1024], P(('exp', 'fsdp'))
- grad_ffn_bias: float32 [1024], P(('exp', 'fsdp'))
- grad_expert_in: float32 [16, 1024, 4096], P('exp', None, 'fsdp')
- grad_expert_in_bias: float32 [16, 4096], P('exp', 'fsdp')
- grad_expert_out: float32 [16, 4096, 1024], P('exp', 'fsdp')
- grad_expert_out_bias: float32 [16, 1024], P('exp', 'fsdp')
Inputs may be any that keep to these rules, and one draw needn't show every extreme that they name: `expert_ids`: in each sequence no expert is named by more than 48 positions, and in every draw some expert is named by exactly 48 positions of some sequence. `seq_lengths`: in each micro-batch one sequence, drawn from the seed, has length 512.
All inputs are finite; a program needn't handle non-finite values.
Results may differ from a plain program's by a relative error of at most 0.014.
Values may be sent and summed in bfloat16 or wider, within the bound.
No kernel may reach another device: no remote copies, remote signals or barrier semaphores. Data moves between devices by JAX's collectives and lax.ppermute only.
A program may use at most 384 MiB of HBM per device.

v0:
```python
import jax
import jax.numpy as jnp
from jax import lax
from jax.sharding import PartitionSpec as P

HEADS = 16


def norm_parts(inputs):
    average = jnp.mean(inputs, axis=-1, keepdims=True)
    centred = inputs - average
    variance = jnp.mean(centred * centred, axis=-1, keepdims=True)
    inverse = lax.rsqrt(variance + 1e-05)
    return (centred * inverse, inverse)


def norm_back(grad_normed, normal, inverse, norm_gain):
    scaled = grad_normed * norm_gain
    return inverse * (
        scaled
        - jnp.mean(scaled, axis=-1, keepdims=True)
        - normal * jnp.mean(scaled * normal, axis=-1, keepdims=True)
    )


def smooth_gate(inputs):
    return jax.nn.gelu(inputs, approximate=True)


def slot_table(expert_row, expert_total, capacity):
    onehot = (expert_row[:, None] == jnp.arange(expert_total, dtype=jnp.int32)[None, :]).astype(
        jnp.int32
    )
    before = jnp.cumsum(onehot, axis=0) - onehot
    rank_in = jnp.sum(before * onehot, axis=1)
    counts = jnp.sum(onehot, axis=0)
    filled = (jnp.arange(capacity, dtype=jnp.int32)[None, :] < counts[:, None]).astype(jnp.bfloat16)
    return (expert_row * capacity + rank_in, filled)


def split_heads(tensor):
    return tensor.reshape(tensor.shape[0], HEADS, tensor.shape[1] // HEADS)


def block_scores(query_heads, key_heads, length, row_start, block_rows, scaling):
    key_pos = jnp.arange(key_heads.shape[0], dtype=jnp.int32)[None, None, :]
    query_pos = row_start + jnp.arange(block_rows, dtype=jnp.int32)[None, :, None]
    allowed = (key_pos <= query_pos) & (key_pos < length)
    scores = (
        jnp.einsum("qhd,khd->hqk", query_heads, key_heads, preferred_element_type=jnp.float32)
        * scaling
    )
    return jnp.where(allowed, scores, -1e30)


def attend_forward(query_rows, key_rows_total, value_rows_total, length):
    seq_len, model_width = query_rows.shape
    scaling = (model_width // HEADS) ** (-0.5)
    query_heads = split_heads(query_rows)
    key_heads = split_heads(key_rows_total)
    value_heads = split_heads(value_rows_total)
    block_rows = min(seq_len, 512)
    scores = block_scores(query_heads, key_heads, length, 0, block_rows, scaling)
    row_max = jnp.max(scores, axis=-1, keepdims=True)
    weights = jnp.exp(scores - row_max)
    row_total = jnp.sum(weights, axis=-1, keepdims=True)
    attn_probs = (weights / row_total).astype(jnp.bfloat16)
    outputs = jnp.einsum(
        "hqk,khd->qhd", attn_probs, value_heads, preferred_element_type=jnp.float32
    )
    totals = [row_max + jnp.log(row_total)]
    attention_result = outputs.reshape(seq_len, model_width).astype(jnp.bfloat16)
    return (attention_result, totals)


def attend_backward(query_rows, key_rows_total, value_rows_total, length, totals, grad_attended):
    seq_len, model_width = query_rows.shape
    scaling = (model_width // HEADS) ** (-0.5)
    query_heads = split_heads(query_rows)
    key_heads = split_heads(key_rows_total)
    value_heads = split_heads(value_rows_total)
    grad_heads = split_heads(grad_attended)
    block_rows = min(seq_len, 512)
    query_grads = []
    key_grad = jnp.zeros(key_heads.shape, jnp.float32)
    value_grad = jnp.zeros(value_heads.shape, jnp.float32)
    for block_idx, row_start in enumerate(range(0, seq_len, block_rows)):
        scores = block_scores(query_heads, key_heads, length, row_start, block_rows, scaling)
        attn_probs = jnp.exp(scores - totals[block_idx])
        grad_probs = jnp.einsum(
            "qhd,khd->hqk", grad_heads, value_heads, preferred_element_type=jnp.float32
        )
        inner_sum = jnp.sum(attn_probs * grad_probs, axis=-1, keepdims=True)
        grad_scores = (attn_probs * (grad_probs - inner_sum)).astype(jnp.bfloat16)
        query_grads.append(
            jnp.einsum("hqk,khd->qhd", grad_scores, key_heads, preferred_element_type=jnp.float32)
            * scaling
        )
        key_grad = (
            jnp.einsum("hqk,qhd->khd", grad_scores, query_heads, preferred_element_type=jnp.float32)
            * scaling
        )
        value_grad = jnp.einsum(
            "hqk,qhd->khd",
            attn_probs.astype(jnp.bfloat16),
            grad_heads,
            preferred_element_type=jnp.float32,
        )
    query_back = query_grads[0].reshape(seq_len, model_width).astype(jnp.bfloat16)
    key_back = key_grad.reshape(seq_len, model_width).astype(jnp.bfloat16)
    value_back = value_grad.reshape(seq_len, model_width).astype(jnp.bfloat16)
    return (query_back, key_back, value_back)


def add_up(total_parts, new_parts):
    if total_parts is None:
        return tuple(new_parts)
    return tuple((earlier + latest for earlier, latest in zip(total_parts, new_parts)))


def body(
    block_input,
    expert_ids,
    seq_lengths,
    attn_norm_gain,
    attn_norm_bias,
    query_matrix,
    query_offset_bias,
    key_matrix,
    value_matrix,
    value_offset_bias,
    output_matrix,
    attention_output_bias,
    ffn_norm_gain,
    ffn_norm_bias,
    expert_in,
    expert_in_bias,
    expert_out,
    expert_out_bias,
    out_cotangent,
):
    micro_count = block_input.shape[0]
    local_experts = block_input.shape[1]
    sources = block_input.shape[3]
    capacity = block_input.shape[4]
    model_width = block_input.shape[5]
    expert_total = local_experts * lax.axis_size("exp")
    group_count = lax.axis_size("fsdp")
    group_index = lax.axis_index("fsdp")
    slot_rows = sources * capacity
    width_share = model_width // group_count
    dense_total = None
    expert_grads = None
    outputs_all = []
    input_grads = []
    for micro_idx in range(micro_count):
        dense_full = (
            lax.all_gather(attn_norm_gain, ("exp", "fsdp"), axis=0, tiled=True),
            lax.all_gather(attn_norm_bias, ("exp", "fsdp"), axis=0, tiled=True),
            lax.all_gather(query_matrix, ("exp", "fsdp"), axis=0, tiled=True),
            lax.all_gather(query_offset_bias, ("exp", "fsdp"), axis=0, tiled=True),
            lax.all_gather(key_matrix, ("exp", "fsdp"), axis=0, tiled=True),
            lax.all_gather(value_matrix, ("exp", "fsdp"), axis=0, tiled=True),
            lax.all_gather(value_offset_bias, ("exp", "fsdp"), axis=0, tiled=True),
            lax.all_gather(output_matrix, ("exp", "fsdp"), axis=0, tiled=True),
            lax.all_gather(attention_output_bias, ("exp", "fsdp"), axis=0, tiled=True),
            lax.all_gather(ffn_norm_gain, ("exp", "fsdp"), axis=0, tiled=True),
            lax.all_gather(ffn_norm_bias, ("exp", "fsdp"), axis=0, tiled=True),
        )
        (
            gain_one,
            bias_one,
            w_query,
            b_query,
            w_key,
            w_value,
            b_value,
            w_output,
            b_output,
            gain_two,
            bias_two,
        ) = dense_full
        expert_row = expert_ids[micro_idx, 0, :, 0]
        length = seq_lengths[micro_idx, 0]
        slot_ids, filled = slot_table(expert_row, expert_total, capacity)
        local_rows = block_input[micro_idx, :, 0]
        arrived = lax.all_to_all(local_rows, "exp", split_axis=1, concat_axis=0, tiled=True)
        seq_rows = arrived.reshape(expert_total * capacity, model_width)[slot_ids]
        normal_one, inverse_one = norm_parts(seq_rows.astype(jnp.float32))
        normed_one = (
            normal_one * gain_one.astype(jnp.float32) + bias_one.astype(jnp.float32)
        ).astype(jnp.bfloat16)
        query_rows = (
            jnp.dot(normed_one, w_query, preferred_element_type=jnp.float32)
            + b_query.astype(jnp.float32)
        ).astype(jnp.bfloat16)
        key_rows_total = jnp.dot(normed_one, w_key, preferred_element_type=jnp.float32).astype(
            jnp.bfloat16
        )
        value_rows_total = (
            jnp.dot(normed_one, w_value, preferred_element_type=jnp.float32)
            + b_value.astype(jnp.float32)
        ).astype(jnp.bfloat16)
        attention_result, totals = attend_forward(
            query_rows, key_rows_total, value_rows_total, length
        )
        attention_output = (
            jnp.dot(attention_result, w_output, preferred_element_type=jnp.float32)
            + b_output.astype(jnp.float32)
        ).astype(jnp.bfloat16)
        placed = (
            jnp.zeros((expert_total * capacity, model_width), jnp.bfloat16)
            .at[slot_ids]
            .set(attention_output)
        )
        back_rows, back_filled = (
            lax.all_to_all(
                placed.reshape(expert_total, capacity, model_width),
                "exp",
                split_axis=0,
                concat_axis=1,
                tiled=True,
            ),
            lax.all_to_all(filled, "exp", split_axis=0, concat_axis=1, tiled=True),
        )
        fill_mask = back_filled.astype(jnp.float32)[:, :, None]
        mixed_rows = local_rows.reshape(local_experts, slot_rows, model_width).astype(
            jnp.float32
        ) + back_rows.astype(jnp.float32)
        normal_two, inverse_two = norm_parts(mixed_rows)
        normed_two = (
            normal_two * gain_two.astype(jnp.float32) + bias_two.astype(jnp.float32)
        ).astype(jnp.bfloat16)
        grad_rows = (
            out_cotangent[micro_idx, :, 0].reshape(local_experts, slot_rows, model_width)
            * back_filled[:, :, None]
        )
        gathered, bias_full = (
            lax.all_gather(normed_two, "fsdp", axis=1, tiled=True),
            lax.all_gather(expert_out_bias, "fsdp", axis=1, tiled=True),
        )
        inner_pre = (
            jnp.einsum("erd,edf->erf", gathered, expert_in, preferred_element_type=jnp.float32)
            + expert_in_bias.astype(jnp.float32)[:, None, :]
        )
        activated = smooth_gate(inner_pre).astype(jnp.bfloat16)
        partial_out = jnp.einsum(
            "erf,efd->erd", activated, expert_out, preferred_element_type=jnp.float32
        )
        ffn_out = (
            lax.psum_scatter(
                partial_out.astype(jnp.bfloat16), "fsdp", scatter_dimension=1, tiled=True
            ).astype(jnp.float32)
            + bias_full.astype(jnp.float32)[:, None, :]
        )
        grad_gathered = lax.all_gather(grad_rows, "fsdp", axis=1, tiled=True)
        grad_act = jnp.einsum(
            "erd,efd->erf", grad_gathered, expert_out, preferred_element_type=jnp.float32
        )
        grad_inner = jax.vjp(smooth_gate, inner_pre)[1](grad_act)[0].astype(jnp.bfloat16)
        column_grads = lax.dynamic_slice_in_dim(
            grad_gathered, group_index * width_share, width_share, 2
        )
        expert_parts = (
            jnp.einsum("erd,erf->edf", gathered, grad_inner, preferred_element_type=jnp.float32),
            jnp.sum(grad_inner.astype(jnp.float32), axis=1),
            jnp.einsum(
                "erf,erd->efd", activated, grad_gathered, preferred_element_type=jnp.float32
            ),
            jnp.sum(column_grads.astype(jnp.float32), axis=1),
        )
        grad_normed_two = lax.psum_scatter(
            jnp.einsum(
                "erf,edf->erd", grad_inner, expert_in, preferred_element_type=jnp.float32
            ).astype(jnp.bfloat16),
            "fsdp",
            scatter_dimension=1,
            tiled=True,
        ).astype(jnp.float32)
        block_rows_out = ((mixed_rows + ffn_out) * fill_mask).astype(jnp.bfloat16)
        outputs_all.append(block_rows_out.reshape(local_experts, 1, sources, capacity, model_width))
        grad_gain_two = jnp.sum(grad_normed_two * normal_two, axis=(0, 1))
        grad_bias_two = jnp.sum(grad_normed_two, axis=(0, 1))
        grad_mixed = grad_rows.astype(jnp.float32) + norm_back(
            grad_normed_two, normal_two, inverse_two, gain_two.astype(jnp.float32)
        )
        to_send = grad_mixed.astype(jnp.bfloat16).reshape(
            local_experts, sources, capacity, model_width
        )
        grad_arrived = lax.all_to_all(to_send, "exp", split_axis=1, concat_axis=0, tiled=True)
        grad_attn_out = grad_arrived.reshape(expert_total * capacity, model_width)[slot_ids]
        grad_w_output = jnp.einsum(
            "sd,se->de", attention_result, grad_attn_out, preferred_element_type=jnp.float32
        )
        grad_b_output = jnp.sum(grad_attn_out.astype(jnp.float32), axis=0)
        grad_attended = jnp.einsum(
            "se,de->sd", grad_attn_out, w_output, preferred_element_type=jnp.float32
        ).astype(jnp.bfloat16)
        query_back, key_back, value_back = attend_backward(
            query_rows, key_rows_total, value_rows_total, length, totals, grad_attended
        )
        grad_w_query = jnp.einsum(
            "sd,se->de", normed_one, query_back, preferred_element_type=jnp.float32
        )
        grad_b_query = jnp.sum(query_back.astype(jnp.float32), axis=0)
        grad_w_key = jnp.einsum(
            "sd,se->de", normed_one, key_back, preferred_element_type=jnp.float32
        )
        grad_w_value = jnp.einsum(
            "sd,se->de", normed_one, value_back, preferred_element_type=jnp.float32
        )
        grad_b_value = jnp.sum(value_back.astype(jnp.float32), axis=0)
        grad_normed_one = (
            jnp.einsum("se,de->sd", query_back, w_query, preferred_element_type=jnp.float32)
            + jnp.einsum("se,de->sd", key_back, w_key, preferred_element_type=jnp.float32)
            + jnp.einsum("se,de->sd", value_back, w_value, preferred_element_type=jnp.float32)
        )
        grad_gain_one = jnp.sum(grad_normed_one * normal_one, axis=0)
        grad_bias_one = jnp.sum(grad_normed_one, axis=0)
        seq_back = norm_back(
            grad_normed_one, normal_one, inverse_one, gain_one.astype(jnp.float32)
        ).astype(jnp.bfloat16)
        placed_back = (
            jnp.zeros((expert_total * capacity, model_width), jnp.bfloat16)
            .at[slot_ids]
            .set(seq_back)
        )
        returned = lax.all_to_all(
            placed_back.reshape(expert_total, capacity, model_width),
            "exp",
            split_axis=0,
            concat_axis=1,
            tiled=True,
        )
        input_grads.append(
            (grad_mixed + returned.astype(jnp.float32))
            .astype(jnp.bfloat16)
            .reshape(local_experts, 1, sources, capacity, model_width)
        )
        dense_parts = (
            grad_gain_one,
            grad_bias_one,
            grad_w_query,
            grad_b_query,
            grad_w_key,
            grad_w_value,
            grad_b_value,
            grad_w_output,
            grad_b_output,
            grad_gain_two,
            grad_bias_two,
        )
        dense_total = add_up(
            dense_total,
            (
                lax.psum_scatter(dense_parts[0], ("exp", "fsdp"), scatter_dimension=0, tiled=True),
                lax.psum_scatter(dense_parts[1], ("exp", "fsdp"), scatter_dimension=0, tiled=True),
                lax.psum_scatter(dense_parts[2], ("exp", "fsdp"), scatter_dimension=0, tiled=True),
                lax.psum_scatter(dense_parts[3], ("exp", "fsdp"), scatter_dimension=0, tiled=True),
                lax.psum_scatter(dense_parts[4], ("exp", "fsdp"), scatter_dimension=0, tiled=True),
                lax.psum_scatter(dense_parts[5], ("exp", "fsdp"), scatter_dimension=0, tiled=True),
                lax.psum_scatter(dense_parts[6], ("exp", "fsdp"), scatter_dimension=0, tiled=True),
                lax.psum_scatter(dense_parts[7], ("exp", "fsdp"), scatter_dimension=0, tiled=True),
                lax.psum_scatter(dense_parts[8], ("exp", "fsdp"), scatter_dimension=0, tiled=True),
                lax.psum_scatter(dense_parts[9], ("exp", "fsdp"), scatter_dimension=0, tiled=True),
                lax.psum_scatter(dense_parts[10], ("exp", "fsdp"), scatter_dimension=0, tiled=True),
            ),
        )
        expert_grads = add_up(expert_grads, expert_parts)
    return (
        jnp.stack(outputs_all),
        jnp.stack(input_grads),
        dense_total[0],
        dense_total[1],
        dense_total[2],
        dense_total[3],
        dense_total[4],
        dense_total[5],
        dense_total[6],
        dense_total[7],
        dense_total[8],
        dense_total[9],
        dense_total[10],
        expert_grads[0],
        expert_grads[1],
        expert_grads[2],
        expert_grads[3],
    )


def solution(mesh):
    placed = (
        P(None, "exp", "fsdp", None, None, None),
        P(None, ("exp", "fsdp"), None, None),
        P(None, ("exp", "fsdp")),
        P(("exp", "fsdp")),
        P(("exp", "fsdp")),
        P(("exp", "fsdp"), None),
        P(("exp", "fsdp")),
        P(("exp", "fsdp"), None),
        P(("exp", "fsdp"), None),
        P(("exp", "fsdp")),
        P(("exp", "fsdp"), None),
        P(("exp", "fsdp")),
        P(("exp", "fsdp")),
        P(("exp", "fsdp")),
        P("exp", None, "fsdp"),
        P("exp", "fsdp"),
        P("exp", "fsdp", None),
        P("exp", "fsdp"),
        P(None, "exp", "fsdp", None, None, None),
    )
    return jax.shard_map(
        body,
        mesh=mesh,
        in_specs=placed,
        out_specs=(
            P(None, "exp", "fsdp", None, None, None),
            P(None, "exp", "fsdp", None, None, None),
            P(("exp", "fsdp")),
            P(("exp", "fsdp")),
            P(("exp", "fsdp"), None),
            P(("exp", "fsdp")),
            P(("exp", "fsdp"), None),
            P(("exp", "fsdp"), None),
            P(("exp", "fsdp")),
            P(("exp", "fsdp"), None),
            P(("exp", "fsdp")),
            P(("exp", "fsdp")),
            P(("exp", "fsdp")),
            P("exp", None, "fsdp"),
            P("exp", "fsdp"),
            P("exp", "fsdp", None),
            P("exp", "fsdp"),
        ),
        check_vma=False,
    )
```

profile of v0, /device:TPU:0, one launch (start us, length us, event | category | flops | bytes accessed | tf_op | source)
XLA Modules:
  0.0 1817.5 jit_solution(16189499476329830308)
XLA Ops:
  37.8 15.1 all-to-all-done
  58.9 55.0 %all-reduce.15 = (bf16[1024]{0:T(1024)(128)(2,1)S(1)}, bf16[1024]{0:T(1024)(128)(2,1)S(1)}, bf16[1024]{0:T(1024)(128)(2,1)S(1)}, bf16[1024]{0:T(1024)(128)(2,1)S...) all-reduce(bf16[1024]{0:T(1024)(128)(2,1)S(1)} %dynamic-update-slic, ...), channel_id=1, replica_groups=mesh['exp'=8,'fsdp'=4] {'exp','fsdp'}, use_global_device_ids=true, to_apply=%add.2 | all-reduce | flops 7168 | bytes 28672
  149.3 46.0 %all-gather.9.cloned.1.call-done = bf16[1024,1024]{1,0:T(8,128)(2,1)} async-done(((bf16[32,1024]{1,0:T(8,128)(2,1)}), bf16[1024,1024]{1,0:T(8,128)(2,1)}) %all-gather.9.cloned.1.call-update) | async-done | bytes 2097168 | tf_op jit(solution)/shard_map/all_gather | solution.py:163
  206.8 9.0 fusion.141
  215.9 8.4 fusion.1
  224.3 7.7 fusion.76
  236.6 16.8 all-gather.15.cloned.1.call-done
  265.6 8.6 fusion.140
  274.1 8.4 fusion
  282.6 7.7 fusion.77
  307.8 13.9 all-to-all-done.1
  338.8 7.0 all_to_all.128
  347.8 21.2 %all-gather.23.cloned.1.call-done = bf16[2,1536,1024]{2,1,0:T(8,128)(2,1)} async-done(((bf16[2,384,1024]{2,1,0:T(8,128)(2,1)}), bf16[2,1536,1024]{2,1,0:T(8,128)(2,1)}) %all-gather.23.cloned.1.call-update) | async-done | bytes 6291472 | tf_op jit(solution)/shard_map/all_gather | solution.py:256
  369.0 12.8 fusion.146
  381.8 102.8 %all-gather.19.cloned.1.call-done = bf16[2,1536,1024]{2,1,0:T(8,128)(2,1)} async-done(((bf16[2,384,1024]{2,1,0:T(8,128)(2,1)}), bf16[2,1536,1024]{2,1,0:T(8,128)(2,1)}) %all-gather.19.cloned.1.call-update) | async-done | bytes 6291472 | tf_op jit(solution)/shard_map/all_gather | solution.py:239
  484.6 12.7 fusion.143
  497.3 103.0 %all-gather.17.cloned.1.call-done = bf16[2,1536,1024]{2,1,0:T(8,128)(2,1)} async-done(((bf16[2,384,1024]{2,1,0:T(8,128)(2,1)}), bf16[2,1536,1024]{2,1,0:T(8,128)(2,1)}) %all-gather.17.cloned.1.call-update) | async-done | bytes 6291472 | tf_op jit(solution)/shard_map/all_gather | solution.py:239
  600.3 12.6 fusion.142
  612.9 102.5 %all-gather.21.cloned.1.call-done = bf16[2,1536,1024]{2,1,0:T(8,128)(2,1)} async-done(((bf16[2,384,1024]{2,1,0:T(8,128)(2,1)}), bf16[2,1536,1024]{2,1,0:T(8,128)(2,1)}) %all-gather.21.cloned.1.call-update) | async-done | bytes 6291472 | tf_op jit(solution)/shard_map/all_gather | solution.py:256
  715.4 33.1 %convert_reduce_fusion.1 = (f32[2,1024]{1,0:T(2,128)}, bf16[2,1536,1024]{2,1,0:T(8,128)(2,1)}, f32[2,1024]{1,0:T(2,128)}, bf16[2,1536,1024]{2,1,0:T(8,128)(2,1)}) fusion(f32[2,1536,1024]{2,1,0:T(8,128)} %fusion.142, f32[2,1024]{1,0:T(2,128)S(1)} %convert_element_type.441, f32[2,1536,1024]{2,1,0:T(8,128)} %fusion.146, f32[2,1536,1024]{2,1,0:T(8,128)} %fusion.143, ...), kind=kOutput, calls=%fused_computation.43 | convolution fusion | flops 6587150336 | bytes 60841984 | tf_op jit(solution)/shard_map/erd,efd->erf/dot_general | solution.py:257
  748.5 11.7 convolution_convert_fusion.1
  760.3 11.9 convolution_convert_fusion
  772.4 13.9 convolution_convert_fusion.3
  787.7 81.7 %reduce-scatter.13.cloned.1.call-done = bf16[2,384,1024]{2,1,0:T(8,128)(2,1)} async-done(((bf16[2,1536,1024]{2,1,0:T(8,128)(2,1)}), bf16[2,384,1024]{2,1,0:T(8,128)(2,1)}) %reduce-scatter.13.cloned.1.call-update) | async-done | bytes 1572880 | tf_op jit(solution)/shard_map/reduce_scatter | solution.py:272
  879.4 14.3 convolution_convert_fusion.2
  893.7 6.6 all-to-all-done.6
  906.9 14.5 multiply_reduce_fusion.1
  923.7 8.3 multiply_convert_fusion.1
  945.4 9.5 convert_reduce_fusion.11
  965.9 11.6 all_gather.72
  977.5 9.3 all-to-all-done.7
  989.2 107.9 %reduce-scatter.9.cloned.1.call-done = bf16[2,384,1024]{2,1,0:T(8,128)(2,1)} async-done(((bf16[2,1536,1024]{2,1,0:T(8,128)(2,1)}), bf16[2,384,1024]{2,1,0:T(8,128)(2,1)}) %reduce-scatter.9.cloned.1.call-update) | async-done | bytes 1572880 | tf_op jit(solution)/shard_map/reduce_scatter | solution.py:251
  1097.2 8.0 fusion.45
  1116.1 16.5 all-to-all-done.8
  1134.7 6.2 convolution_add_fusion.2
  1151.4 9.6 convert_reduce_fusion.10
  1170.5 14.9 multiply_reduce_fusion
  1185.4 8.1 multiply_convert_fusion
  1208.3 14.4 fusion.118
  1230.5 12.7 fusion.150
  1243.2 15.6 convolution_add_fusion
  1266.2 5.5 scatter_custom_fusion.3
  1275.7 14.0 convolution_add_fusion.1
  1290.4 43.1 %all-reduce.14 = (f32[1024]{0:T(1024)S(1)}, f32[1024]{0:T(1024)S(1)}, f32[1024]{0:T(1024)S(1)}, f32[1024]{0:T(1024)S(1)}, f32[1024]{0:T(1024)S(1)}, /*index=5*/f32[1024]{0:T(1024)S(1)}, f32[1024]{0:T(1024)S(1)}) all-reduce(f32[1024]{0:T(1024)S(1)} %add.422, ...), channel_id=17, replica_groups=mesh['exp'=8,'fsdp'=4] {'exp','fsdp'}, use_global_device_ids=true, to_apply=%region_39.40.clone | all-reduce | flops 7168 | bytes 57344
  1349.3 12.9 reduce-scatter.23.cloned.1.call-done
  1362.2 150.3 %reduce-scatter.21.cloned.1.call-done = f32[32,1024]{1,0:T(8,128)} async-done(((f32[1024,1024]{1,0:T(8,128)}), f32[32,1024]{1,0:T(8,128)}) %reduce-scatter.21.cloned.1.call-update) | async-done | bytes 131088 | tf_op jit(solution)/shard_map/reduce_scatter | solution.py:361
  1512.4 148.7 %reduce-scatter.17.cloned.1.call-done = f32[32,1024]{1,0:T(8,128)} async-done(((f32[1024,1024]{1,0:T(8,128)}), f32[32,1024]{1,0:T(8,128)}) %reduce-scatter.17.cloned.1.call-update) | async-done | bytes 131088 | tf_op jit(solution)/shard_map/reduce_scatter | solution.py:358
  1661.1 149.6 %reduce-scatter.19.cloned.1.call-done = f32[32,1024]{1,0:T(8,128)} async-done(((f32[1024,1024]{1,0:T(8,128)}), f32[32,1024]{1,0:T(8,128)}) %reduce-scatter.19.cloned.1.call-update) | async-done | bytes 131088 | tf_op jit(solution)/shard_map/reduce_scatter | solution.py:360
  (556 shorter events, 265.7 us)
Async XLA Ops:
  7.2 119.1 %all-gather.13.cloned.1.call-start = ((), (), s32[]{:S(2)}) async-start(), calls=%async_computation.20 | async-start | bytes 2162688 | tf_op jit(solution)/shard_map/all_gather | solution.py:162
  7.9 129.0 %all-gather.11.cloned.1.call-start = ((), (), s32[]{:S(2)}) async-start(), calls=%async_computation.19 | async-start | bytes 2162688 | tf_op jit(solution)/shard_map/all_gather | solution.py:160
  8.7 186.6 %all-gather.9.cloned.1.call-start = ((), (), s32[]{:S(2)}) async-start(), calls=%async_computation.18 | async-start | bytes 2162688 | tf_op jit(solution)/shard_map/all_gather | solution.py:163
  9.4 244.0 %all-gather.15.cloned.1.call-start = ((), (), s32[]{:S(2)}) async-start(), calls=%async_computation.21 | async-start | bytes 2162688 | tf_op jit(solution)/shard_map/all_gather | solution.py:165
  13.0 12.8 all-to-all-start.5
  25.8 27.1 %all-to-all-start = ((bf16[2,8,48,1024]{3,2,0,1:T(8,128)(2,1)}), bf16[2,8,48,1024]{3,2,0,1:T(8,128)(2,1)S(1)}, u32[]{:S(2)}, u32[]{:S(2)}) async-start(bf16[2,8,48,1024]{3,2,0,1:T(8,128)(2,1)} %get-tuple-element.68), calls=%async_computation | async-start | bytes 3145728 | tf_op jit(solution)/shard_map/all_to_all | solution.py:187
  30.7 226.5 %copy-start.133 = (s32[512,1]{0,1:T(1,128)}, s32[512,1]{0,1:T(1,128)S(1)}, u32[]{:S(2)}) copy-start(s32[512,1]{0,1:T(1,128)S(1)} %get-tuple-element.80) | copy-start | bytes 6148
  30.7 261.9 %copy-start.134 = (s32[512,1]{0,1:T(1,128)}, s32[512,1]{0,1:T(1,128)S(1)}, u32[]{:S(2)}) copy-start(s32[512,1]{0,1:T(1,128)S(1)} %get-tuple-element.79) | copy-start | bytes 6148
  30.7 92.8 %copy-start.118 = (s32[1024]{0:T(1024)}, s32[1024]{0:T(1024)S(1)}, u32[]{:S(2)}) copy-start(s32[1024]{0:T(1024)S(1)} %pad_clamp_fusion) | copy-start | bytes 12292
  30.8 86.9 %copy-start.120 = (s32[1024]{0:T(1024)}, s32[1024]{0:T(1024)S(1)}, u32[]{:S(2)}) copy-start(s32[1024]{0:T(1024)S(1)} %pad_clamp_fusion.1) | copy-start | bytes 12292
  52.9 70.7 %all-to-all-start.3 = ((bf16[2,8,48,1024]{3,2,0,1:T(8,128)(2,1)}), bf16[2,8,48,1024]{3,2,0,1:T(8,128)(2,1)S(1)}, u32[]{:S(2)}, u32[]{:S(2)}) async-start(bf16[2,8,48,1024]{3,2,0,1:T(8,128)(2,1)} %get-tuple-element.70), calls=%async_computation.4 | async-start | bytes 3145728 | tf_op jit(solution)/shard_map/all_to_all | solution.py:187
  56.5 312.6 %all-gather.23.cloned.1.call-start = ((), (), s32[]{:S(2)}) async-start(), calls=%async_computation.28 | async-start | bytes 7864320 | tf_op jit(solution)/shard_map/all_gather | solution.py:256
  113.9 118.1 %copy-start.64 = (f32[1024]{0:T(1024)}, f32[1024]{0:T(1024)S(1)}, u32[]{:S(2)}) copy-start(f32[1024]{0:T(1024)S(1)} %convert_element_type.417) | copy-start | bytes 12292
  113.9 118.1 %copy-start.85 = (f32[1024]{0:T(1024)}, f32[1024]{0:T(1024)S(1)}, u32[]{:S(2)}) copy-start(f32[1024]{0:T(1024)S(1)} %convert_element_type.418) | copy-start | bytes 12292
  121.9 110.1 %copy-start.109 = (f32[512]{0:T(512)}, f32[512]{0:T(512)S(1)}, u32[]{:S(2)}) copy-start(f32[512]{0:T(512)S(1)} %broadcast_multiply_fusion.11) | copy-start | bytes 6148
  123.5 108.5 %copy-start.124 = (f32[512]{0:T(512)}, f32[512]{0:T(512)S(1)}, u32[]{:S(2)}) copy-start(f32[512]{0:T(512)S(1)} %add_rsqrt_fusion.1) | copy-start | bytes 6148
  125.6 75.8 %copy-start.3 = (bf16[512,1024]{1,0:T(8,128)(2,1)}, bf16[512,1024]{1,0:T(8,128)(2,1)S(1)}, u32[]{:S(2)}) copy-start(bf16[512,1024]{1,0:T(8,128)(2,1)S(1)} %gather_fusion.1) | copy-start | bytes 3145732
  132.1 133.4 %copy-start.22 = (bf16[512,1024]{0,1:T(8,128)(2,1)}, bf16[512,1024]{0,1:T(8,128)(2,1)S(1)}, u32[]{:S(2)}) copy-start(bf16[512,1024]{0,1:T(8,128)(2,1)S(1)} %copy.243) | copy-start | bytes 3145732
  261.7 34.8 %all-to-all-start.4 = ((bf16[16,48,1024]{2,1,0:T(8,128)(2,1)}), bf16[16,48,1024]{2,1,0:T(8,128)(2,1)S(1)}, u32[]{:S(2)}, u32[]{:S(2)}) async-start(bf16[16,48,1024]{2,1,0:T(8,128)(2,1)} %bitcast.291), calls=%async_computation.5 | async-start | bytes 3145728 | tf_op jit(solution)/shard_map/all_to_all | solution.py:217
  296.5 25.2 %all-to-all-start.1 = ((bf16[16,48,1024]{2,1,0:T(8,128)(2,1)}), bf16[16,48,1024]{2,1,0:T(8,128)(2,1)S(1)}, u32[]{:S(2)}, u32[]{:S(2)}) async-start(bf16[16,48,1024]{2,1,0:T(8,128)(2,1)} %bitcast.290), calls=%async_computation.1 | async-start | bytes 3145728 | tf_op jit(solution)/shard_map/all_to_all | solution.py:217
  300.7 183.9 %all-gather.19.cloned.1.call-start = ((), (), s32[]{:S(2)}) async-start(), calls=%async_computation.24 | async-start | bytes 7864320 | tf_op jit(solution)/shard_map/all_gather | solution.py:239
  337.9 262.5 %all-gather.17.cloned.1.call-start = ((), (), s32[]{:S(2)}) async-start(), calls=%async_computation.22 | async-start | bytes 7864320 | tf_op jit(solution)/shard_map/all_gather | solution.py:239
  338.6 376.8 %all-gather.21.cloned.1.call-start = ((), (), s32[]{:S(2)}) async-start(), calls=%async_computation.26 | async-start | bytes 7864320 | tf_op jit(solution)/shard_map/all_gather | solution.py:256
  347.3 522.1 %reduce-scatter.13.cloned.1.call-start = ((), (), s32[]{:S(2)}) async-start(), calls=%async_computation.27 | async-start | bytes 7864320 | tf_op jit(solution)/shard_map/reduce_scatter | solution.py:272
  347.8 531.6 %copy-start.131 = (f32[2,1024]{1,0:T(2,128)}, f32[2,1024]{1,0:T(2,128)S(1)}, u32[]{:S(2)}) copy-start(f32[2,1024]{1,0:T(2,128)S(1)} %convert_element_type.441) | copy-start | bytes 24580
  760.3 228.9 %reduce-scatter.15.cloned.1.call-start = ((), (), s32[]{:S(2)}) async-start(), calls=%async_computation.29 | async-start | bytes 7864320 | tf_op jit(solution)/shard_map/reduce_scatter | solution.py:272
  772.3 324.8 %reduce-scatter.9.cloned.1.call-start = ((), (), s32[]{:S(2)}) async-start(), calls=%async_computation.23 | async-start | bytes 7864320 | tf_op jit(solution)/shard_map/reduce_scatter | solution.py:251
  786.3 83.1 %copy-start.5 = (f32[2,384,1024]{2,1,0:T(8,128)S(1)}, f32[2,384,1024]{2,1,0:T(8,128)}, u32[]{:S(2)}) copy-start(f32[2,384,1024]{2,1,0:T(8,128)} %get-tuple-element.56) | copy-start | bytes 9437188
  786.3 83.1 %copy-start.62 = (f32[1024]{0:T(1024)S(1)}, f32[1024]{0:T(1024)}, u32[]{:S(2)}) copy-start(f32[1024]{0:T(1024)} %copy-done.61) | copy-start | bytes 12292
  786.3 83.1 %copy-start.71 = (f32[2,384]{1,0:T(2,128)S(1)}, f32[2,384]{1,0:T(2,128)}, u32[]{:S(2)}) copy-start(f32[2,384]{1,0:T(2,128)} %copy-done.70) | copy-start | bytes 9220
  786.3 83.1 %copy-start.73 = (f32[2,384]{1,0:T(2,128)S(1)}, f32[2,384]{1,0:T(2,128)}, u32[]{:S(2)}) copy-start(f32[2,384]{1,0:T(2,128)} %copy-done.72) | copy-start | bytes 9220
  787.0 86.0 %copy-start.91 = (bf16[2,384]{1,0:T(2,128)(2,1)S(1)}, bf16[2,384]{1,0:T(2,128)(2,1)}, u32[]{:S(2)}) copy-start(bf16[2,384]{1,0:T(2,128)(2,1)} %copy-done.90) | copy-start | bytes 4612
  875.7 24.7 %all-to-all-start.6 = ((bf16[2,8,48,1024]{3,2,0,1:T(8,128)(2,1)}), bf16[2,8,48,1024]{3,2,0,1:T(8,128)(2,1)S(1)}, u32[]{:S(2)}, u32[]{:S(2)}) async-start(bf16[2,8,48,1024]{3,2,0,1:T(8,128)(2,1)} %copy.264), calls=%async_computation.9 | async-start | bytes 3145728 | tf_op jit(solution)/shard_map/all_to_all | solution.py:290
  879.4 460.6 %reduce-scatter.11.cloned.1.call-start = ((), (), s32[]{:S(2)}) async-start(), calls=%async_computation.25 | async-start | bytes 7864320 | tf_op jit(solution)/shard_map/reduce_scatter | solution.py:251
  962.3 24.5 %all-to-all-start.7 = ((bf16[16,48,1024]{2,1,0:T(8,128)(2,1)}), bf16[16,48,1024]{2,1,0:T(8,128)(2,1)S(1)}, u32[]{:S(2)}, u32[]{:S(2)}) async-start(bf16[16,48,1024]{2,1,0:T(8,128)(2,1)} %bitcast.64), calls=%async_computation.10 | async-start | bytes 3145728 | tf_op jit(solution)/shard_map/all_to_all | solution.py:328
  977.5 119.6 %copy-start.81 = (f32[2,1024]{1,0:T(2,128)}, f32[2,1024]{1,0:T(2,128)S(1)}, u32[]{:S(2)}) copy-start(f32[2,1024]{1,0:T(2,128)S(1)} %convert_element_type.445) | copy-start | bytes 24580
  987.2 109.9 %copy-start.6 = (f32[2,384,1024]{2,1,0:T(8,128)S(1)}, f32[2,384,1024]{2,1,0:T(8,128)}, u32[]{:S(2)}) copy-start(f32[2,384,1024]{2,1,0:T(8,128)} %get-tuple-element.56) | copy-start | bytes 9437188
  987.2 109.9 %copy-start.74 = (f32[2,384]{1,0:T(2,128)S(1)}, f32[2,384]{1,0:T(2,128)}, u32[]{:S(2)}) copy-start(f32[2,384]{1,0:T(2,128)} %copy-done.72) | copy-start | bytes 9220
  987.2 109.9 %copy-start.76 = (f32[2,384]{1,0:T(2,128)S(1)}, f32[2,384]{1,0:T(2,128)}, u32[]{:S(2)}) copy-start(f32[2,384]{1,0:T(2,128)} %copy-done.75) | copy-start | bytes 9220
  987.2 109.9 %copy-start.79 = (f32[2,384]{1,0:T(2,128)S(1)}, f32[2,384]{1,0:T(2,128)}, u32[]{:S(2)}) copy-start(f32[2,384]{1,0:T(2,128)} %copy-done.78) | copy-start | bytes 9220
  987.3 109.9 %copy-start.102 = (f32[2,384]{1,0:T(2,128)S(1)}, f32[2,384]{1,0:T(2,128)}, u32[]{:S(2)}) copy-start(f32[2,384]{1,0:T(2,128)} %copy-done.101) | copy-start | bytes 9220
  987.3 109.9 %copy-start.104 = (f32[2,384]{1,0:T(2,128)S(1)}, f32[2,384]{1,0:T(2,128)}, u32[]{:S(2)}) copy-start(f32[2,384]{1,0:T(2,128)} %copy-done.103) | copy-start | bytes 9220
  1107.9 24.7 %all-to-all-start.8 = ((bf16[2,8,48,1024]{3,2,0,1:T(8,128)(2,1)}), bf16[2,8,48,1024]{3,2,0,1:T(8,128)(2,1)S(1)}, u32[]{:S(2)}, u32[]{:S(2)}) async-start(bf16[2,8,48,1024]{3,2,0,1:T(8,128)(2,1)} %copy.270), calls=%async_computation.12 | async-start | bytes 3145728 | tf_op jit(solution)/shard_map/all_to_all | solution.py:290
  1111.6 250.6 %reduce-scatter.23.cloned.1.call-start = ((), (), s32[]{:S(2)}) async-start(), calls=%async_computation.33 | async-start | bytes 4325376 | tf_op jit(solution)/shard_map/reduce_scatter | solution.py:363
  1140.9 371.5 %reduce-scatter.21.cloned.1.call-start = ((), (), s32[]{:S(2)}) async-start(), calls=%async_computation.32 | async-start | bytes 4325376 | tf_op jit(solution)/shard_map/reduce_scatter | solution.py:361
  1165.6 495.5 %reduce-scatter.17.cloned.1.call-start = ((), (), s32[]{:S(2)}) async-start(), calls=%async_computation.30 | async-start | bytes 4325376 | tf_op jit(solution)/shard_map/reduce_scatter | solution.py:358
  1202.4 608.3 %reduce-scatter.19.cloned.1.call-start = ((), (), s32[]{:S(2)}) async-start(), calls=%async_computation.31 | async-start | bytes 4325376 | tf_op jit(solution)/shard_map/reduce_scatter | solution.py:360
  1271.7 65.8 %all-to-all-start.9 = ((bf16[16,48,1024]{2,1,0:T(8,128)(2,1)}), bf16[16,48,1024]{2,1,0:T(8,128)(2,1)S(1)}, u32[]{:S(2)}, u32[]{:S(2)}) async-start(bf16[16,48,1024]{2,1,0:T(8,128)(2,1)} %bitcast.82), calls=%async_computation.13 | async-start | bytes 3145728 | tf_op jit(solution)/shard_map/all_to_all | solution.py:328
  (142 other events, 1348.9 us)
Sparse Core Ops, SparseCore 0:
  11.0 62.9 all-gather.12
  76.9 60.0 all-gather.10
  139.9 55.3 all-gather.8
  198.0 55.3 all-gather.14
  254.8 114.1 all-gather.22
  371.0 113.5 all-gather.18
  486.7 113.5 all-gather.16
  601.9 113.5 all-gather.20
  760.4 108.9 reduce-scatter.12
  871.5 111.3 reduce-scatter.14
  985.8 111.2 reduce-scatter.8
  1099.3 111.2 reduce-scatter.10
  1213.4 148.7 reduce-scatter.22
  1364.9 147.5 reduce-scatter.20
  1515.1 145.9 reduce-scatter.16
  1663.8 146.8 reduce-scatter.18
where the time goes:
time: 1820 us
  waiting for transfers between devices  1110 us (61%)
  matrix products  346 us (19%)
  blocking collectives  117 us (6%)
  other arithmetic  104 us (6%)
  local copies, waits for them, and re-layouts  84.4 us (5%)
  starting transfers between devices  37.1 us (2%)
    all_gather x2, waiting for transfers between devices, body(): lax.all_gather(normed_two, 'fsdp', axis=1, tiled=True)  206 us
    reduce_scatter x1, waiting for transfers between devices, body(): lax.psum_scatter(dense_parts[5], ('exp', 'fsdp'), scatter_dimension=0, ti...  150 us
    reduce_scatter x1, waiting for transfers between devices, body(): lax.psum_scatter(dense_parts[4], ('exp', 'fsdp'), scatter_dimension=0, ti...  150 us
    reduce_scatter x1, waiting for transfers between devices, body(): lax.psum_scatter(dense_parts[2], ('exp', 'fsdp'), scatter_dimension=0, ti...  149 us
    all_gather x2, waiting for transfers between devices, body(): grad_gathered = lax.all_gather(grad_rows, 'fsdp', axis=1, tiled=True)  124 us
    reduce_scatter x2, waiting for transfers between devices, body(): lax.psum_scatter(partial_out.astype(jnp.bfloat16), 'fsdp', scatter_dimens...  108 us
    unnamed x2, blocking collectives  98.1 us
    reduce_scatter x2, waiting for transfers between devices, body(): lax.psum_scatter(jnp.einsum('erf,edf->erd', grad_inner, expert_in, prefer...  81.7 us
  transfers between devices with their start and end apart: 25, of which 18 were waited for; matrix products, arithmetic and copies ran while one was open for 26% of the time, Pallas kernels for 0%

commit v1 on v0

v1 whole, which is shorter than its diff:
```python
import jax
import jax.numpy as jnp
from jax import lax
from jax.sharding import PartitionSpec as P

HEADS = 16
BF = jnp.bfloat16
F32 = jnp.float32


def norm_parts(inputs):
    average = jnp.mean(inputs, axis=-1, keepdims=True)
    centred = inputs - average
    variance = jnp.mean(centred * centred, axis=-1, keepdims=True)
    inverse = lax.rsqrt(variance + 1e-05)
    return (centred * inverse, inverse)


def norm_back(grad_normed, normal, inverse, norm_gain):
    scaled = grad_normed * norm_gain
    return inverse * (
        scaled
        - jnp.mean(scaled, axis=-1, keepdims=True)
        - normal * jnp.mean(scaled * normal, axis=-1, keepdims=True)
    )


def smooth_gate(inputs):
    return jax.nn.gelu(inputs, approximate=True)


def dot(a, b, dims):
    return lax.dot_general(a, b, (dims, ((), ())), preferred_element_type=F32)


def split_heads(tensor):
    return tensor.reshape(tensor.shape[0], HEADS, tensor.shape[1] // HEADS)


def block_scores(query_heads, key_heads, length, scaling):
    n = key_heads.shape[0]
    key_pos = jnp.arange(n, dtype=jnp.int32)[None, None, :]
    query_pos = jnp.arange(n, dtype=jnp.int32)[None, :, None]
    allowed = (key_pos <= query_pos) & (key_pos < length)
    scores = (
        jnp.einsum("qhd,khd->hqk", query_heads, key_heads, preferred_element_type=F32)
        * scaling
    )
    return jnp.where(allowed, scores, -1e30)


def attend_forward(q, k, v, length):
    seq_len, width = q.shape
    scaling = (width // HEADS) ** (-0.5)
    scores = block_scores(split_heads(q), split_heads(k), length, scaling)
    row_max = jnp.max(scores, axis=-1, keepdims=True)
    weights = jnp.exp(scores - row_max)
    row_total = jnp.sum(weights, axis=-1, keepdims=True)
    probs = (weights / row_total).astype(BF)
    out = jnp.einsum("hqk,khd->qhd", probs, split_heads(v), preferred_element_type=F32)
    return out.reshape(seq_len, width).astype(BF), row_max + jnp.log(row_total)


def attend_backward(q, k, v, length, lse, grad_attended):
    seq_len, width = q.shape
    scaling = (width // HEADS) ** (-0.5)
    qh, kh, vh, gh = (split_heads(a) for a in (q, k, v, grad_attended))
    probs = jnp.exp(block_scores(qh, kh, length, scaling) - lse)
    grad_probs = jnp.einsum("qhd,khd->hqk", gh, vh, preferred_element_type=F32)
    inner_sum = jnp.sum(probs * grad_probs, axis=-1, keepdims=True)
    grad_scores = (probs * (grad_probs - inner_sum)).astype(BF)
    dq = jnp.einsum("hqk,khd->qhd", grad_scores, kh, preferred_element_type=F32) * scaling
    dk = jnp.einsum("hqk,qhd->khd", grad_scores, qh, preferred_element_type=F32) * scaling
    dv = jnp.einsum("hqk,qhd->khd", probs.astype(BF), gh, preferred_element_type=F32)
    return tuple(a.reshape(seq_len, width).astype(BF) for a in (dq, dk, dv))


def attention_forward(arrived, slot_ids, length, dense, small):
    rows = arrived[slot_ids]
    normal, _ = norm_parts(rows.astype(F32))
    normed = (normal * small[0] + small[1]).astype(BF)
    q = (dot(normed, dense[0], ((1,), (0,))) + small[2]).astype(BF)
    k = dot(normed, dense[1], ((1,), (0,))).astype(BF)
    v = (dot(normed, dense[2], ((1,), (0,))) + small[3]).astype(BF)
    attended, lse = attend_forward(q, k, v, length)
    out = (dot(attended, dense[3], ((1,), (0,))) + small[4]).astype(BF)
    placed = jnp.zeros(arrived.shape, BF).at[slot_ids].set(out)
    return placed, (rows, q, k, v, attended, lse)


def attention_backward(grad_arrived, slot_ids, length, dense, small, saved):
    rows, q, k, v, attended, lse = saved
    normal, inverse = norm_parts(rows.astype(F32))
    normed = (normal * small[0] + small[1]).astype(BF)
    grad_out = grad_arrived[slot_ids]
    dwo = dot(attended, grad_out, ((0,), (0,)))
    dbo = jnp.sum(grad_out.astype(F32), axis=0)
    grad_attended = dot(grad_out, dense[3], ((1,), (1,))).astype(BF)
    dq, dk, dv = attend_backward(q, k, v, length, lse, grad_attended)
    dws = [dot(normed, a, ((0,), (0,))) for a in (dq, dk, dv)] + [dwo]
    grad_normed = sum(dot(a, w, ((1,), (1,))) for a, w in zip((dq, dk, dv), dense))
    smalls = [
        jnp.sum(grad_normed * normal, axis=0),
        jnp.sum(grad_normed, axis=0),
        jnp.sum(dq.astype(F32), axis=0),
        jnp.sum(dv.astype(F32), axis=0),
        dbo,
    ]
    back = norm_back(grad_normed, normal, inverse, small[0]).astype(BF)
    placed = jnp.zeros(grad_arrived.shape, BF).at[slot_ids].set(back)
    return placed, dws, smalls


def expert_step(x, g, w_in, b_in, w_out):
    inner = dot(x, w_in, ((1,), (0,))) + b_in[None, :]
    activated, pull = jax.vjp(smooth_gate, inner)
    activated = activated.astype(BF)
    out = dot(activated, w_out, ((1,), (0,))).astype(BF)
    grad_act = dot(g, w_out, ((1,), (1,)))
    grad_inner = pull(grad_act)[0].astype(BF)
    grad_x = dot(grad_inner, w_in, ((1,), (1,))).astype(BF)
    dw_in = dot(x, grad_inner, ((0,), (0,)))
    dw_out = dot(activated, g, ((0,), (0,)))
    db_in = jnp.sum(grad_inner.astype(F32), axis=0)
    return out, grad_x, dw_in, dw_out, db_in


def reduce_dense(parts, n_exp, n_f, ex, fi):
    rows, width = parts.shape[1:]
    chips = n_exp // 2
    chip, core = ex // 2, ex % 2
    view = parts.reshape(chips, 2, n_f * rows, width)
    keep = lax.dynamic_index_in_dim(view, core, 1, keepdims=False)
    give = lax.dynamic_index_in_dim(view, 1 - core, 1, keepdims=False)
    got = lax.ppermute(give, "exp", [(i, i ^ 1) for i in range(n_exp)])
    summed = keep + got
    low = summed.astype(BF)
    total = lax.dynamic_index_in_dim(summed, chip, 0, keepdims=False)
    for step in range(1, chips):
        block = lax.dynamic_index_in_dim(low, chip ^ step, 0, keepdims=False)
        total = total + lax.ppermute(
            block, "exp", [(i, i ^ (2 * step)) for i in range(n_exp)]
        ).astype(F32)
    total = total.reshape(n_f, rows, width)
    half = n_f // 2
    while half >= 1:
        pairs = total.reshape(2, half, rows, width)
        side = (fi // half) % 2
        give = lax.dynamic_index_in_dim(pairs, 1 - side, 0, keepdims=False)
        keep = lax.dynamic_index_in_dim(pairs, side, 0, keepdims=False)
        total = keep + lax.ppermute(
            give.astype(BF), "fsdp", [(i, i ^ half) for i in range(n_f)]
        ).astype(F32)
        half //= 2
    return total.reshape(rows, width)


def body(
    block_input,
    expert_ids,
    seq_lengths,
    attn_norm_gain,
    attn_norm_bias,
    query_matrix,
    query_offset_bias,
    key_matrix,
    value_matrix,
    value_offset_bias,
    output_matrix,
    attention_output_bias,
    ffn_norm_gain,
    ffn_norm_bias,
    expert_in,
    expert_in_bias,
    expert_out,
    expert_out_bias,
    out_cotangent,
):
    mb, le, _, sources, cap, width = block_input.shape
    n_exp, n_f = lax.axis_size("exp"), lax.axis_size("fsdp")
    ex, fi = lax.axis_index("exp"), lax.axis_index("fsdp")
    everyone = ("exp", "fsdp")
    experts = le * n_exp
    slots = experts * cap
    rows = sources * cap
    hidden = expert_in.shape[2]
    seq = expert_ids.shape[2]
    far = [(i, i ^ 2) for i in range(n_f)]
    near = [(i, i ^ 1) for i in range(n_f)]
    share = attn_norm_gain.shape[0]

    dense_full = lax.all_gather(
        jnp.stack([query_matrix, key_matrix, value_matrix, output_matrix]), everyone, axis=1, tiled=True
    )
    ids = expert_ids[:, 0, :, 0]
    onehot = ids[:, :, None] == jnp.arange(experts, dtype=jnp.int32)
    counts = jnp.sum(onehot.astype(F32), axis=1)
    position = jnp.arange(seq, dtype=jnp.int32)
    same = (ids[:, :, None] == ids[:, None, :]) & (position[None, None, :] < position[None, :, None])
    slot_ids = ids * cap + jnp.sum(same.astype(jnp.int32), axis=2)

    packed = jnp.concatenate(
        [
            attn_norm_gain,
            attn_norm_bias,
            query_offset_bias,
            value_offset_bias,
            attention_output_bias,
            ffn_norm_gain,
            ffn_norm_bias,
            expert_out_bias.reshape(-1),
            expert_in_bias.reshape(-1),
            counts.astype(BF).reshape(-1),
        ]
    )
    table = lax.all_gather(packed[None], everyone, axis=0, tiled=True).astype(F32)
    small = [table[:, i * share : (i + 1) * share].reshape(-1) for i in range(7)]
    at = 7 * share
    table = table.reshape(n_exp, n_f, -1)
    mine = lax.dynamic_index_in_dim(table, ex, 0, keepdims=False)
    bias_out = mine[:, at : at + expert_out_bias.size].reshape(n_f, le, -1).transpose(1, 0, 2).reshape(le, width)
    at += expert_out_bias.size
    bias_in = mine[:, at : at + le * hidden].reshape(n_f, le, hidden)
    bias_in = jnp.concatenate(
        [
            lax.dynamic_index_in_dim(bias_in, fi, 0, keepdims=False),
            lax.dynamic_index_in_dim(bias_in, fi ^ 1, 0, keepdims=False),
        ],
        axis=1,
    )
    at += le * hidden
    all_counts = table[:, :, at:].reshape(n_exp, n_f, mb, n_exp, le)
    my_counts = lax.dynamic_index_in_dim(all_counts, ex, 3, keepdims=False)

    def fill(group):
        count = lax.dynamic_index_in_dim(my_counts, group, 1, keepdims=False)
        count = count.transpose(1, 2, 0)[:, :, :, None]
        return (jnp.arange(cap, dtype=F32) < count).astype(F32).reshape(mb, le, rows, 1)

    fill_own, fill_far = fill(fi), fill(fi ^ 2)

    arrived_all = lax.all_to_all(
        block_input[:, :, 0], "exp", split_axis=2, concat_axis=1, tiled=True
    ).reshape(mb, slots, width)

    w_in = jnp.concatenate([expert_in, lax.ppermute(expert_in, "fsdp", near)], axis=2)
    w_out = jnp.concatenate([expert_out, lax.ppermute(expert_out, "fsdp", near)], axis=1)

    cot = out_cotangent[:, :, 0].reshape(mb, le, rows, width)
    cot_far = [lax.ppermute(cot[t], "fsdp", far) for t in range(mb)]

    outputs, input_grads = [], []
    dense_total, small_total, expert_total = None, None, None
    for t in range(mb):
        placed, saved = attention_forward(arrived_all[t], slot_ids[t], seq_lengths[t, 0], dense_full, small)
        back_rows = lax.all_to_all(
            placed.reshape(experts, cap, width), "exp", split_axis=0, concat_axis=1, tiled=True
        ).reshape(le, rows, width)
        mixed = block_input[t, :, 0].reshape(le, rows, width).astype(F32) + back_rows.astype(F32)
        normal_two, inverse_two = norm_parts(mixed)
        normed_two = (normal_two * small[5] + small[6]).astype(BF)
        normed_far = lax.ppermute(normed_two, "fsdp", far)
        grad_rows = cot[t] * fill_own[t].astype(BF)
        grad_far = cot_far[t] * fill_far[t].astype(BF)
        outs, gxs, dwi, dwo, dbi = [], [], [], [], []
        for j in range(le):
            x = jnp.concatenate([normed_two[j], normed_far[j]], axis=0)
            g = jnp.concatenate([grad_rows[j], grad_far[j]], axis=0)
            out, gx, a, b, c = expert_step(x, g, w_in[j], bias_in[j], w_out[j])
            outs.append(out)
            gxs.append(gx)
            dwi.append(a)
            dwo.append(b)
            dbi.append(c)
        gx_all = jnp.stack(gxs)
        grad_normed = gx_all[:, :rows].astype(F32) + lax.ppermute(gx_all[:, rows:], "fsdp", far).astype(F32)
        out_all = jnp.stack(outs)
        ffn_out = out_all[:, :rows].astype(F32) + lax.ppermute(out_all[:, rows:], "fsdp", far).astype(F32)
        ffn_out = ffn_out + bias_out[:, None, :]
        outputs.append(
            ((mixed + ffn_out) * fill_own[t]).astype(BF).reshape(le, 1, sources, cap, width)
        )
        dbo = jnp.sum(grad_rows.astype(F32), axis=1) + jnp.sum(grad_far.astype(F32), axis=1)
        grad_mixed = grad_rows.astype(F32) + norm_back(grad_normed, normal_two, inverse_two, small[5])
        grad_arrived = lax.all_to_all(
            grad_mixed.astype(BF).reshape(le, sources, cap, width), "exp", split_axis=1, concat_axis=0, tiled=True
        ).reshape(slots, width)
        placed_back, dws, smalls = attention_backward(
            grad_arrived, slot_ids[t], seq_lengths[t, 0], dense_full, small, saved
        )
        returned = lax.all_to_all(
            placed_back.reshape(experts, cap, width), "exp", split_axis=0, concat_axis=1, tiled=True
        ).reshape(le, rows, width)
        input_grads.append(
            (grad_mixed + returned.astype(F32)).astype(BF).reshape(le, 1, sources, cap, width)
        )
        smalls = smalls + [
            jnp.sum(grad_normed * normal_two, axis=(0, 1)),
            jnp.sum(grad_normed, axis=(0, 1)),
        ]
        expert_parts = [jnp.stack(dwi), jnp.stack(dwo), jnp.stack(dbi), dbo]
        if t == 0:
            dense_total, small_total, expert_total = dws, smalls, expert_parts
        else:
            dense_total = [a + b for a, b in zip(dense_total, dws)]
            small_total = [a + b for a, b in zip(small_total, smalls)]
            expert_total = [a + b for a, b in zip(expert_total, expert_parts)]

    dwi, dwo, dbi, dbo = expert_total
    grad_in = dwi[:, :, :hidden] + lax.ppermute(dwi[:, :, hidden:].astype(BF), "fsdp", near).astype(F32)
    grad_out = dwo[:, :hidden] + lax.ppermute(dwo[:, hidden:].astype(BF), "fsdp", near).astype(F32)
    vectors = lax.ppermute(jnp.concatenate([dbi[:, hidden:], dbo], axis=1), "fsdp", near)
    grad_in_bias = dbi[:, :hidden] + vectors[:, :hidden]
    dbo = dbo + vectors[:, hidden:]
    grad_out_bias = lax.dynamic_slice_in_dim(dbo, fi * (width // n_f), width // n_f, 1)

    blocks = jnp.stack(
        [a.reshape(n_exp * n_f, share, width) for a in dense_total], axis=1
    ).reshape(n_exp * n_f, 4 * share, width)
    dense = reduce_dense(blocks, n_exp, n_f, ex, fi)
    dense = dense.reshape(4, share, width)
    smalls = lax.all_gather(jnp.stack(small_total)[None], everyone, axis=0, tiled=True)
    smalls = jnp.sum(smalls, axis=0)
    smalls = lax.dynamic_slice_in_dim(smalls, (ex * n_f + fi) * share, share, 1)
    return (
        jnp.stack(outputs),
        jnp.stack(input_grads),
        smalls[0],
        smalls[1],
        dense[0],
        smalls[2],
        dense[1],
        dense[2],
        smalls[3],
        dense[3],
        smalls[4],
        smalls[5],
        smalls[6],
        grad_in,
        grad_in_bias,
        grad_out,
        grad_out_bias,
    )


def solution(mesh):
    rows, dense, vec = (
        P(None, "exp", "fsdp", None, None, None),
        P(("exp", "fsdp"), None),
        P(("exp", "fsdp")),
    )
    experts = (P("exp", None, "fsdp"), P("exp", "fsdp"), P("exp", "fsdp", None), P("exp", "fsdp"))
    return jax.shard_map(
        body,
        mesh=mesh,
        in_specs=(
            rows,
            P(None, ("exp", "fsdp"), None, None),
            P(None, ("exp", "fsdp")),
            vec,
            vec,
            dense,
            vec,
            dense,
            dense,
            vec,
            dense,
            vec,
            vec,
            vec,
        )
        + experts
        + (rows,),
        out_specs=(rows, rows, vec, vec, dense, vec, dense, dense, vec, dense, vec, vec, vec) + experts,
        check_vma=False,
    )
```

time: 1820 us -> 1530 us (0.84)
  waiting for transfers between devices: 1110 us -> 327 us
  blocking collectives: 117 us -> 480 us
  other arithmetic: 104 us -> 173 us
  local copies, waits for them, and re-layouts: 84.4 us -> 125 us
    reduce_scatter x8 -> x0, waiting for transfers between devices: 651 us -> none  [the longest x1 150 us: body(): lax.psum_scatter(dense_parts[5], ('exp', 'fsdp'), scatter_dimension=0, ti...]
    all_gather x1 -> x2, blocking collectives: 11.6 us -> 480 us  [the longest x1 345 us: body(): lax.all_gather(packed[None], everyone, axis=0, tiled=True).astype(F32)]
    all_gather x8 -> x1, waiting for transfers between devices: 397 us -> 0.02 us  [body(): lax.all_gather(jnp.stack([query_matrix, key_matrix, value_matrix, output_...]
    ppermute x0 -> x19, waiting for transfers between devices: none -> 304 us  [the longest x2 154 us: body(): lax.ppermute(gx_all[:, rows:], 'fsdp', far).astype(F32)]
    unnamed x2 -> x0, blocking collectives: 98.1 us -> none
    add x11 -> x20, other arithmetic: 2.47 us -> 47.2 us  [the longest x4 19.9 us: body(): expert_total = [a + b for a, b in zip(expert_total, expert_parts)]]
    all_to_all x9 -> x7, waiting for transfers between devices: 61.4 us -> 23 us  [the longest x2 15.7 us: body(): lax.all_to_all(placed.reshape(experts, cap, width), 'exp', split_axis=0,...]
    ppermute x0 -> x19, starting transfers between devices: none -> 19 us  [the longest x3 3.49 us: reduce_dense(): lax.ppermute(block, 'exp', [(i, i ^ 2 * step) for i in range(n_exp)])]
  transfers between devices with their start and end apart: 25 -> 27, of which waited for: 18 -> 9; matrix products, arithmetic and copies ran while one was open for 26% -> 35% of each run, Pallas kernels for 0% -> 0%
where the time goes in v1:
time: 1530 us; the launch traced here: 1520 us
  blocking collectives  480 us (31%)
  matrix products  349 us (23%)
  waiting for transfers between devices  327 us (21%)
  other arithmetic  173 us (11%)
  local copies, waits for them, and re-layouts  125 us (8%)
  starting transfers between devices  51.2 us (3%)
  between operations  17.4 us (1%)
    all_gather x1, blocking collectives, body(): lax.all_gather(packed[None], everyone, axis=0, tiled=True).astype(F32)  345 us
    dot_general x48, matrix products, dot(): return lax.dot_general(a, b, (dims, ((), ())), preferred_element_type=F32)  245 us
    ppermute x2, waiting for transfers between devices, body(): lax.ppermute(gx_all[:, rows:], 'fsdp', far).astype(F32)  154 us
    all_gather x1, blocking collectives, body(): lax.all_gather(jnp.stack(small_total)[None], everyone, axis=0, tiled=True)  134 us
    ppermute x2, waiting for transfers between devices, body(): normed_far = lax.ppermute(normed_two, 'fsdp', far)  89.9 us
    ppermute x3, waiting for transfers between devices, reduce_dense(): lax.ppermute(block, 'exp', [(i, i ^ 2 * step) for i in range(n_exp)])  36 us
    unnamed x398, local copies, waits for them, and re-layouts  34.8 us
    dot_general x2, matrix products, attend_backward(): grad_probs = jnp.einsum('qhd,khd->hqk', gh, vh, preferred_element_type=F32)  31.1 us
  transfers between devices with their start and end apart: 27, of which 9 were waited for; matrix products, arithmetic and copies ran while one was open for 35% of the time, Pallas kernels for 0%

profile of v1, /device:TPU:0, one launch (start us, length us, event | category | flops | bytes accessed | tf_op | source)
XLA Modules:
  0.0 1522.5 jit_solution(9166103322090135530)
XLA Ops:
  27.7 345.5 %all-gather.2 = bf16[32,1,2816]{2,1,0:T(2,128)(2,1)S(1)} all-gather(bf16[1,1,2816]{2,1,0:T(2,128)(2,1)S(1)} %reshape.744), channel_id=2, replica_groups=mesh['exp'=8,'fsdp'=4] {'exp','fsdp'}, dimensions={0}, use_global_device_ids=true | all-gather | bytes 185856 | tf_op jit(solution)/shard_map/all_gather | solution.py:216
  449.3 9.3 fusion.206
  458.6 8.4 fusion
  467.0 7.5 fusion.119
  491.4 10.4 fusion.207
  501.8 8.3 fusion.1
  510.1 7.5 fusion.118
  535.4 15.7 %all-to-all-done.2 = bf16[16,48,1024]{2,1,0:T(8,128)(2,1)} async-done(((bf16[16,48,1024]{2,1,0:T(8,128)(2,1)}), bf16[16,48,1024]{2,1,0:T(8,128)(2,1)}, u32[]{:S(2)}, u32[]{:S(2)}) %all-to-all-start.2) | async-done | bytes 1572896 | tf_op jit(solution)/shard_map/all_to_all | solution.py:256
  582.4 89.9 %collective-permute-done = bf16[2,384,1024]{2,1,0:T(8,128)(2,1)S(1)} collective-permute-done((bf16[2,384,1024]{2,1,0:T(8,128)(2,1)S(1)}, bf16[2,384,1024]{2,1,0:T(8,128)(2,1)S(1)}, u32[]{:S(2)}, u32[]{:S(2)}) %collective-permute-start) | collective-permute-done | bytes 1572896 | tf_op jit(solution)/shard_map/ppermute | solution.py:262
  681.2 9.2 convert_reduce_fusion.2
  690.5 5.5 fusion.115
  705.0 10.7 convert_reduce_fusion.3
  719.2 5.8 convolution_bitcast_fusion.7
  725.0 8.1 fusion.113
  735.2 5.8 fusion.58
  741.1 8.2 fusion.116
  749.3 12.9 convert_reduce_fusion
  762.3 5.5 fusion.114
  767.8 5.9 convolution_bitcast_fusion.4
  773.7 5.6 fusion.50
  779.2 8.2 fusion.112
  787.5 12.9 convert_reduce_fusion.1
  805.8 8.2 convolution_bitcast_fusion.5
  825.0 9.7 maximum_add_fusion
  837.9 15.3 %convolution_bitcast_fusion.2 = f32[1,2048,1024]{2,1,0:T(8,128)} fusion(bf16[384,1024]{1,0:T(8,128)(2,1)} %get-tuple-element.63, bf16[384,1024]{1,0:T(8,128)(2,1)} %get-tuple-element.61, f32[768,2048]{1,0:T(8,128)} %copy-done.178, f32[2048]{0:T(1024)S(1)} %bitcast.559), kind=kOutput, calls=%fused_computation.85 | convolution fusion | flops 3240099840 | bytes 16261120 | tf_op jit(solution)/shard_map/dot_general | solution.py:33
  853.3 11.1 convolution_bitcast_fusion.3
  864.4 153.7 %collective-permute-done.7 = bf16[2,384,1024]{2,1,0:T(8,128)(2,1)S(1)} collective-permute-done((bf16[2,384,1024]{2,1,0:T(8,128)(2,1)}, bf16[2,384,1024]{2,1,0:T(8,128)(2,1)S(1)}, u32[]{:S(2)}, u32[]{:S(2)}) %collective-permute-start.7) | collective-permute-done | bytes 1572896 | tf_op jit(solution)/shard_map/ppermute | solution.py:276
  1021.2 6.8 multiply_reduce_fusion.2
  1038.0 10.9 convolution_bitcast_fusion
  1050.2 7.2 all-to-all-done.5
  1068.1 16.6 %multiply_reduce_fusion = (f32[16,512]{1,0:T(8,128)}, f32[16,512,512]{1,2,0:T(8,128)}) fusion(f32[16,512,512]{1,2,0:T(8,128)} %get-tuple-element.122, f32[16,512]{1,0:T(8,128)} %log_add_fusion, bf16[512,16,64]{0,2,1:T(8,128)(2,1)} %bitcast.494, bf16[512,16,64]{0,2,1:T(8,128)(2,1)} %bitcast.515), kind=kOutput, calls=%fused_computation.12 | convolution fusion | flops 549445632 | bytes 35717120 | tf_op jit(solution)/shard_map/qhd,khd->hqk/dot_general | solution.py:69
  1084.7 8.1 multiply_convert_fusion
  1098.6 7.1 multiply_convert_fusion.8
  1105.7 10.2 convert_reduce_fusion.12
  1125.0 10.4 convert_reduce_fusion.13
  1135.5 14.5 multiply_reduce_fusion.1
  1150.0 8.5 multiply_convert_fusion.1
  1163.4 6.4 multiply_convert_fusion.10
  1193.4 6.9 convolution_bitcast_fusion.1
  1200.3 9.6 maximum_add_fusion.1
  1232.3 5.6 scatter_custom_fusion.3
  1242.9 134.4 %all-gather.3 = f32[32,7,1024]{2,1,0:T(8,128)S(1)} all-gather(f32[1,7,1024]{2,1,0:T(8,128)S(1)} %bitcast.533), channel_id=3, replica_groups=mesh['exp'=8,'fsdp'=4] {'exp','fsdp'}, dimensions={0}, use_global_device_ids=true | all-gather | bytes 946176 | tf_op jit(solution)/shard_map/all_gather | solution.py:322
  1383.4 10.2 slice_add_fusion.1
  1398.2 10.3 slice_add_fusion
  1410.3 13.5 fusion.195
  1440.8 13.8 collective-permute-done.13
  1454.6 22.0 %collective-permute-done.12 = bf16[512,1024]{1,0:T(8,128)(2,1)} collective-permute-done((bf16[512,1024]{1,0:T(8,128)(2,1)}, bf16[512,1024]{1,0:T(8,128)(2,1)}, u32[]{:S(2)}, u32[]{:S(2)}) %collective-permute-start.12) | collective-permute-done | bytes 1048608 | tf_op jit(solution)/shard_map/ppermute | solution.py:141
  1485.8 20.1 %collective-permute-done.14 = bf16[2,128,1024]{2,1,0:T(8,128)(2,1)S(1)} collective-permute-done((bf16[2,128,1024]{2,1,0:T(8,128)(2,1)S(1)}, bf16[2,128,1024]{2,1,0:T(8,128)(2,1)S(1)}, u32[]{:S(2)}, u32[]{:S(2)}) %collective-permute-start.14) | collective-permute-done | bytes 524320 | tf_op jit(solution)/shard_map/ppermute | solution.py:151
  (648 shorter events, 347.3 us)
Async XLA Ops:
  7.2 411.9 %all-gather.6.cloned.1.call-start = ((), (), s32[]{:S(2)}) async-start(), calls=%async_computation.7 | async-start | bytes 8650752 | tf_op jit(solution)/shard_map/all_gather | solution.py:192
  13.0 395.4 %all-to-all-start = ((bf16[2,2,8,48,1024]{4,3,1,0,2:T(8,128)(2,1)}), bf16[2,2,8,48,1024]{4,3,1,0,2:T(8,128)(2,1)}, u32[]{:S(2)}, u32[]{:S(2)}) async-start(bf16[2,2,8,48,1024]{4,3,1,0,2:T(8,128)(2,1)} %bitcast.461), calls=%async_computation | async-start | bytes 6291456 | tf_op jit(solution)/shard_map/all_to_all | solution.py:242
  18.3 552.8 %collective-permute-start.1 = (bf16[2,1024,1024]{2,1,0:T(8,128)(2,1)}, bf16[2,1024,1024]{2,1,0:T(8,128)(2,1)}, u32[]{:S(2)}, u32[]{:S(2)}) collective-permute-start(bf16[2,1024,1024]{2,1,0:T(8,128)(2,1)} %param.33), channel_id=1, source_target_pairs={{0,1},{1,0},{2,3},{3,2},{4,5},{5,4},{6,7},{7,6},{8,9},{9,8},{10,11... | collective-permute-start | bytes 12582920 | tf_op jit(solution)/shard_map/ppermute | solution.py:246
  20.7 554.1 %collective-permute-start.2 = (bf16[2,1024,1024]{2,1,0:T(8,128)(2,1)}, bf16[2,1024,1024]{2,1,0:T(8,128)(2,1)}, u32[]{:S(2)}, u32[]{:S(2)}) collective-permute-start(bf16[2,1024,1024]{2,1,0:T(8,128)(2,1)} %param.35), channel_id=1, source_target_pairs={{0,1},{1,0},{2,3},{3,2},{4,5},{5,4},{6,7},{7,6},{8,9},{9,8},{10,11... | collective-permute-start | bytes 12582920 | tf_op jit(solution)/shard_map/ppermute | solution.py:247
  24.4 377.1 %copy-start.11 = (bf16[1,2,1,8,48,1024]{5,4,3,2,1,0:T(8,128)(2,1)}, bf16[1,2,1,8,48,1024]{5,4,3,2,1,0:T(8,128)(2,1)S(1)}, u32[]{:S(2)}) copy-start(bf16[1,2,1,8,48,1024]{5,4,3,2,1,0:T(8,128)(2,1)S(1)} %get-tuple-element.53) | copy-start | bytes 4718596
  24.4 382.3 %collective-permute-start.8 = (bf16[2,384,1024]{2,1,0:T(8,128)(2,1)S(1)}, bf16[2,384,1024]{2,1,0:T(8,128)(2,1)S(1)}, u32[]{:S(2)}, u32[]{:S(2)}) collective-permute-start(bf16[2,384,1024]{2,1,0:T(8,128)(2,1)S(1)} %bitcast.475), channel_id=1, source_target_pairs={{0,2},{1,3},{2,0},{3,1},{4,6},{5,7},{6,4},{7,5},{8,10},{9,11},{10,... | collective-permute-start | bytes 4718600 | tf_op jit(solution)/shard_map/ppermute | solution.py:250
  27.3 502.8 %collective-permute-start.6 = (bf16[2,384,1024]{2,1,0:T(8,128)(2,1)}, bf16[2,384,1024]{2,1,0:T(8,128)(2,1)}, u32[]{:S(2)}, u32[]{:S(2)}) collective-permute-start(bf16[2,384,1024]{2,1,0:T(8,128)(2,1)} %bitcast.74), channel_id=1, source_target_pairs={{0,2},{1,3},{2,0},{3,1},{4,6},{5,7},{6,4},{7,5},{8,10},{9,11},{10,... | collective-permute-start | bytes 4718600 | tf_op jit(solution)/shard_map/ppermute | solution.py:250
  378.6 107.3 %copy-start.116 = (f32[1024]{0:T(1024)}, f32[1024]{0:T(1024)S(1)}, u32[]{:S(2)}) copy-start(f32[1024]{0:T(1024)S(1)} %add.543) | copy-start | bytes 12292
  378.7 107.3 %copy-start.99 = (f32[1024]{0:T(1024)}, f32[1024]{0:T(1024)S(1)}, u32[]{:S(2)}) copy-start(f32[1024]{0:T(1024)S(1)} %mul.476) | copy-start | bytes 12292
  378.9 184.8 %copy-start.96 = (f32[1024]{0:T(1024)}, f32[1024]{0:T(1024)S(1)}, u32[]{:S(2)}) copy-start(f32[1024]{0:T(1024)S(1)} %mul.483) | copy-start | bytes 12292
  397.3 81.0 %copy-start.160 = (s32[512,1]{0,1:T(1,128)}, s32[512,1]{0,1:T(1,128)S(1)}, u32[]{:S(2)}) copy-start(s32[512,1]{0,1:T(1,128)S(1)} %get-tuple-element.115) | copy-start | bytes 6148
  397.3 124.1 %copy-start.161 = (s32[512,1]{0,1:T(1,128)}, s32[512,1]{0,1:T(1,128)S(1)}, u32[]{:S(2)}) copy-start(s32[512,1]{0,1:T(1,128)S(1)} %get-tuple-element.116) | copy-start | bytes 6148
  418.2 67.8 %copy-start.114 = (f32[512]{0:T(512)}, f32[512]{0:T(512)S(1)}, u32[]{:S(2)}) copy-start(f32[512]{0:T(512)S(1)} %broadcast_multiply_fusion.12) | copy-start | bytes 6148
  419.0 67.0 %copy-start.120 = (f32[512]{0:T(512)}, f32[512]{0:T(512)S(1)}, u32[]{:S(2)}) copy-start(f32[512]{0:T(512)S(1)} %add_rsqrt_fusion) | copy-start | bytes 6148
  482.2 43.2 %all-to-all-start.1 = ((bf16[16,48,1024]{2,1,0:T(8,128)(2,1)}), bf16[16,48,1024]{2,1,0:T(8,128)(2,1)S(1)}, u32[]{:S(2)}, u32[]{:S(2)}) async-start(bf16[16,48,1024]{2,1,0:T(8,128)(2,1)} %bitcast.509), calls=%async_computation.1 | async-start | bytes 3145728 | tf_op jit(solution)/shard_map/all_to_all | solution.py:256
  525.4 25.8 %all-to-all-start.2 = ((bf16[16,48,1024]{2,1,0:T(8,128)(2,1)}), bf16[16,48,1024]{2,1,0:T(8,128)(2,1)}, u32[]{:S(2)}, u32[]{:S(2)}) async-start(bf16[16,48,1024]{2,1,0:T(8,128)(2,1)} %bitcast.60), calls=%async_computation.2 | async-start | bytes 3145728 | tf_op jit(solution)/shard_map/all_to_all | solution.py:256
  570.5 101.8 %collective-permute-start = (bf16[2,384,1024]{2,1,0:T(8,128)(2,1)S(1)}, bf16[2,384,1024]{2,1,0:T(8,128)(2,1)S(1)}, u32[]{:S(2)}, u32[]{:S(2)}) collective-permute-start(bf16[2,384,1024]{2,1,0:T(8,128)(2,1)S(1)} %get-tuple-element.43), channel_id=1, source_target_pairs={{0,2},{1,3},{2,0},{3,1},{4,6},{5,7},{6,4},{7,5},{8,10},{9,11},{10,... | collective-permute-start | bytes 4718600 | tf_op jit(solution)/shard_map/ppermute | solution.py:262
  577.4 103.8 %copy-start.71 = (bf16[2,2048,1024]{2,1,0:T(8,128)(2,1)}, bf16[2,2048,1024]{2,1,0:T(8,128)(2,1)S(1)}, u32[]{:S(2)}) copy-start(bf16[2,2048,1024]{2,1,0:T(8,128)(2,1)S(1)} %constant_dynamic-update-slice_fusion.2) | copy-start | bytes 25165828
  579.3 153.8 %collective-permute-start.4 = (bf16[2,384,1024]{2,1,0:T(8,128)(2,1)S(1)}, bf16[2,384,1024]{2,1,0:T(8,128)(2,1)}, u32[]{:S(2)}, u32[]{:S(2)}) collective-permute-start(bf16[2,384,1024]{2,1,0:T(8,128)(2,1)S(1)} %get-tuple-element.101), channel_id=1, source_target_pairs={{0,2},{1,3},{2,0},{3,1},{4,6},{5,7},{6,4},{7,5},{8,10},{9,11},{10,... | collective-permute-start | bytes 4718600 | tf_op jit(solution)/shard_map/ppermute | solution.py:262
  582.3 153.0 %copy-start.89 = (bf16[384,1024]{1,0:T(8,128)(2,1)}, bf16[384,1024]{1,0:T(8,128)(2,1)S(1)}, u32[]{:S(2)}) copy-start(bf16[384,1024]{1,0:T(8,128)(2,1)S(1)} %get-tuple-element.73) | copy-start | bytes 2359300
  582.4 93.5 %copy-start.91 = (bf16[384,1024]{1,0:T(8,128)(2,1)}, bf16[384,1024]{1,0:T(8,128)(2,1)S(1)}, u32[]{:S(2)}) copy-start(bf16[384,1024]{1,0:T(8,128)(2,1)S(1)} %get-tuple-element.69) | copy-start | bytes 2359300
  696.0 119.2 %copy-start.55 = (bf16[1,768,1024]{2,1,0:T(8,128)(2,1)}, bf16[1,768,1024]{2,1,0:T(8,128)(2,1)S(1)}, u32[]{:S(2)}) copy-start(bf16[1,768,1024]{2,1,0:T(8,128)(2,1)S(1)} %fusion.115) | copy-start | bytes 4718596
  719.2 96.1 %copy-start.57 = (bf16[1,768,1024]{2,1,0:T(8,128)(2,1)}, bf16[1,768,1024]{2,1,0:T(8,128)(2,1)S(1)}, u32[]{:S(2)}) copy-start(bf16[1,768,1024]{2,1,0:T(8,128)(2,1)S(1)} %fusion.111) | copy-start | bytes 4718596
  733.1 87.7 %copy-start.45 = (bf16[1,768,1024]{2,1,0:T(8,128)(2,1)}, bf16[1,768,1024]{2,1,0:T(8,128)(2,1)S(1)}, u32[]{:S(2)}) copy-start(bf16[1,768,1024]{2,1,0:T(8,128)(2,1)S(1)} %fusion.113) | copy-start | bytes 4718596
  749.3 70.2 %copy-start.47 = (bf16[1,768,1024]{2,1,0:T(8,128)(2,1)}, bf16[1,768,1024]{2,1,0:T(8,128)(2,1)S(1)}, u32[]{:S(2)}) copy-start(bf16[1,768,1024]{2,1,0:T(8,128)(2,1)S(1)} %fusion.116) | copy-start | bytes 4718596
  815.2 205.8 %collective-permute-start.9 = (bf16[2,384,1024]{2,1,0:T(8,128)(2,1)}, bf16[2,384,1024]{2,1,0:T(8,128)(2,1)S(1)}, u32[]{:S(2)}, u32[]{:S(2)}) collective-permute-start(bf16[2,384,1024]{2,1,0:T(8,128)(2,1)} %pad_maximum_fusion.3), channel_id=1, source_target_pairs={{0,2},{1,3},{2,0},{3,1},{4,6},{5,7},{6,4},{7,5},{8,10},{9,11},{10,... | collective-permute-start | bytes 4718600 | tf_op jit(solution)/shard_map/ppermute | solution.py:276
  816.5 201.6 %collective-permute-start.7 = (bf16[2,384,1024]{2,1,0:T(8,128)(2,1)}, bf16[2,384,1024]{2,1,0:T(8,128)(2,1)S(1)}, u32[]{:S(2)}, u32[]{:S(2)}) collective-permute-start(bf16[2,384,1024]{2,1,0:T(8,128)(2,1)} %pad_maximum_fusion.4), channel_id=1, source_target_pairs={{0,2},{1,3},{2,0},{3,1},{4,6},{5,7},{6,4},{7,5},{8,10},{9,11},{10,... | collective-permute-start | bytes 4718600 | tf_op jit(solution)/shard_map/ppermute | solution.py:276
  820.8 612.8 %collective-permute-start.5 = (bf16[2,384,1024]{2,1,0:T(8,128)(2,1)}, bf16[2,384,1024]{2,1,0:T(8,128)(2,1)}, u32[]{:S(2)}, u32[]{:S(2)}) collective-permute-start(bf16[2,384,1024]{2,1,0:T(8,128)(2,1)} %pad_maximum_fusion.5), channel_id=1, source_target_pairs={{0,2},{1,3},{2,0},{3,1},{4,6},{5,7},{6,4},{7,5},{8,10},{9,11},{10,... | collective-permute-start | bytes 4718600 | tf_op jit(solution)/shard_map/ppermute | solution.py:278
  822.1 658.4 %collective-permute-start.3 = (bf16[2,384,1024]{2,1,0:T(8,128)(2,1)}, bf16[2,384,1024]{2,1,0:T(8,128)(2,1)}, u32[]{:S(2)}, u32[]{:S(2)}) collective-permute-start(bf16[2,384,1024]{2,1,0:T(8,128)(2,1)} %pad_maximum_fusion.6), channel_id=1, source_target_pairs={{0,2},{1,3},{2,0},{3,1},{4,6},{5,7},{6,4},{7,5},{8,10},{9,11},{10,... | collective-permute-start | bytes 4718600 | tf_op jit(solution)/shard_map/ppermute | solution.py:278
  837.9 545.5 %collective-permute-start.16 = (bf16[2,1024,1024]{2,1,0:T(8,128)(2,1)}, bf16[2,1024,1024]{2,1,0:T(8,128)(2,1)}, u32[]{:S(2)}, u32[]{:S(2)}) collective-permute-start(bf16[2,1024,1024]{2,1,0:T(8,128)(2,1)} %slice.574), channel_id=1, source_target_pairs={{0,1},{1,0},{2,3},{3,2},{4,5},{5,4},{6,7},{7,6},{8,9},{9,8},{10,11... | collective-permute-start | bytes 12582920 | tf_op jit(solution)/shard_map/ppermute | solution.py:310
  853.2 164.9 %copy-start.9 = (f32[2,384,1024]{2,1,0:T(8,128)S(1)}, f32[2,384,1024]{2,1,0:T(8,128)}, u32[]{:S(2)}) copy-start(f32[2,384,1024]{2,1,0:T(8,128)} %get-tuple-element.44) | copy-start | bytes 9437188
  853.2 164.9 %copy-start.56 = (bf16[1,768,1024]{2,1,0:T(8,128)(2,1)S(1)}, bf16[1,768,1024]{2,1,0:T(8,128)(2,1)}, u32[]{:S(2)}) copy-start(bf16[1,768,1024]{2,1,0:T(8,128)(2,1)} %copy-done.55) | copy-start | bytes 4718596
  853.2 164.9 %copy-start.58 = (bf16[1,768,1024]{2,1,0:T(8,128)(2,1)S(1)}, bf16[1,768,1024]{2,1,0:T(8,128)(2,1)}, u32[]{:S(2)}) copy-start(bf16[1,768,1024]{2,1,0:T(8,128)(2,1)} %copy-done.57) | copy-start | bytes 4718596
  853.2 164.9 %copy-start.97 = (f32[1024]{0:T(1024)S(1)}, f32[1024]{0:T(1024)}, u32[]{:S(2)}) copy-start(f32[1024]{0:T(1024)} %copy-done.96) | copy-start | bytes 12292
  853.2 164.9 %copy-start.108 = (f32[2,384]{1,0:T(2,128)S(1)}, f32[2,384]{1,0:T(2,128)}, u32[]{:S(2)}) copy-start(f32[2,384]{1,0:T(2,128)} %copy-done.107) | copy-start | bytes 9220
  853.3 164.9 %copy-start.111 = (f32[2,384]{1,0:T(2,128)S(1)}, f32[2,384]{1,0:T(2,128)}, u32[]{:S(2)}) copy-start(f32[2,384]{1,0:T(2,128)} %copy-done.110) | copy-start | bytes 9220
  1031.2 26.3 %all-to-all-start.5 = ((bf16[2,8,48,1024]{3,2,0,1:T(8,128)(2,1)}), bf16[2,8,48,1024]{3,2,0,1:T(8,128)(2,1)S(1)}, u32[]{:S(2)}, u32[]{:S(2)}) async-start(bf16[2,8,48,1024]{3,2,0,1:T(8,128)(2,1)} %copy.299), calls=%async_computation.5 | async-start | bytes 3145728 | tf_op jit(solution)/shard_map/all_to_all | solution.py:285
  1037.1 176.0 %collective-permute-start.17 = (f32[2,2048]{1,0:T(2,128)}, f32[2,2048]{1,0:T(2,128)}, u32[]{:S(2)}, u32[]{:S(2)}) collective-permute-start(f32[2,2048]{1,0:T(2,128)} %pad_maximum_fusion.32), channel_id=1, source_target_pairs={{0,1},{1,0},{2,3},{3,2},{4,5},{5,4},{6,7},{7,6},{8,9},{9,8},{10,11... | collective-permute-start | bytes 49160 | tf_op jit(solution)/shard_map/ppermute | solution.py:312
  1057.4 58.4 %all-to-all-start.3 = ((bf16[2,8,48,1024]{3,2,0,1:T(8,128)(2,1)}), bf16[2,8,48,1024]{3,2,0,1:T(8,128)(2,1)}, u32[]{:S(2)}, u32[]{:S(2)}) async-start(bf16[2,8,48,1024]{3,2,0,1:T(8,128)(2,1)} %copy.293), calls=%async_computation.3 | async-start | bytes 3145728 | tf_op jit(solution)/shard_map/all_to_all | solution.py:285
  1193.0 217.3 %collective-permute-start.10 = (f32[4,512,1024]{2,1,0:T(8,128)}, f32[4,512,1024]{2,1,0:T(8,128)}, u32[]{:S(2)}, u32[]{:S(2)}) collective-permute-start(f32[4,512,1024]{2,1,0:T(8,128)} %dynamic-slice_bitcast_fusion), channel_id=1, source_target_pairs={{0,4},{4,0},{8,12},{12,8},{16,20},{20,16},{24,28},{28,24},{1,5},{5... | collective-permute-start | bytes 25165832 | tf_op jit(solution)/shard_map/ppermute | solution.py:135
  1213.1 185.1 %collective-permute-start.18 = (bf16[2,1024,1024]{2,1,0:T(8,128)(2,1)}, bf16[2,1024,1024]{2,1,0:T(8,128)(2,1)}, u32[]{:S(2)}, u32[]{:S(2)}) collective-permute-start(bf16[2,1024,1024]{2,1,0:T(8,128)(2,1)} %slice.573), channel_id=1, source_target_pairs={{0,1},{1,0},{2,3},{3,2},{4,5},{5,4},{6,7},{7,6},{8,9},{9,8},{10,11... | collective-permute-start | bytes 12582920 | tf_op jit(solution)/shard_map/ppermute | solution.py:311
  1237.9 155.7 %all-to-all-start.6 = ((bf16[16,48,1024]{2,1,0:T(8,128)(2,1)}), bf16[16,48,1024]{2,1,0:T(8,128)(2,1)}, u32[]{:S(2)}, u32[]{:S(2)}) async-start(bf16[16,48,1024]{2,1,0:T(8,128)(2,1)} %bitcast.511), calls=%async_computation.6 | async-start | bytes 3145728 | tf_op jit(solution)/shard_map/all_to_all | solution.py:291
  1393.6 37.3 %all-to-all-start.4 = ((bf16[16,48,1024]{2,1,0:T(8,128)(2,1)}), bf16[16,48,1024]{2,1,0:T(8,128)(2,1)}, u32[]{:S(2)}, u32[]{:S(2)}) async-start(bf16[16,48,1024]{2,1,0:T(8,128)(2,1)} %bitcast.94), calls=%async_computation.4 | async-start | bytes 3145728 | tf_op jit(solution)/shard_map/all_to_all | solution.py:291
  1427.4 27.2 %collective-permute-start.13 = (bf16[512,1024]{1,0:T(8,128)(2,1)}, bf16[512,1024]{1,0:T(8,128)(2,1)}, u32[]{:S(2)}, u32[]{:S(2)}) collective-permute-start(bf16[512,1024]{1,0:T(8,128)(2,1)} %get-tuple-element.48), channel_id=1, source_target_pairs={{0,24},{4,28},{8,16},{12,20},{16,8},{20,12},{24,0},{28,4},{1,25},{... | collective-permute-start | bytes 3145736 | tf_op jit(solution)/shard_map/ppermute | solution.py:141
  1430.3 46.3 %collective-permute-start.12 = (bf16[512,1024]{1,0:T(8,128)(2,1)}, bf16[512,1024]{1,0:T(8,128)(2,1)}, u32[]{:S(2)}, u32[]{:S(2)}) collective-permute-start(bf16[512,1024]{1,0:T(8,128)(2,1)} %get-tuple-element.49), channel_id=1, source_target_pairs={{0,16},{4,20},{8,24},{12,28},{16,0},{20,4},{24,8},{28,12},{1,17},{... | collective-permute-start | bytes 3145736 | tf_op jit(solution)/shard_map/ppermute | solution.py:141
  1430.8 46.0 %collective-permute-start.11 = (bf16[512,1024]{1,0:T(8,128)(2,1)}, bf16[512,1024]{1,0:T(8,128)(2,1)}, u32[]{:S(2)}, u32[]{:S(2)}) collective-permute-start(bf16[512,1024]{1,0:T(8,128)(2,1)} %get-tuple-element.47), channel_id=1, source_target_pairs={{0,8},{4,12},{8,0},{12,4},{16,24},{20,28},{24,16},{28,20},{1,9},{5... | collective-permute-start | bytes 3145736 | tf_op jit(solution)/shard_map/ppermute | solution.py:141
  1480.4 25.4 %collective-permute-start.14 = (bf16[2,128,1024]{2,1,0:T(8,128)(2,1)S(1)}, bf16[2,128,1024]{2,1,0:T(8,128)(2,1)S(1)}, u32[]{:S(2)}, u32[]{:S(2)}) collective-permute-start(bf16[2,128,1024]{2,1,0:T(8,128)(2,1)S(1)} %fusion.152), channel_id=1, source_target_pairs={{0,2},{1,3},{2,0},{3,1},{4,6},{5,7},{6,4},{7,5},{8,10},{9,11},{10,... | collective-permute-start | bytes 1572872 | tf_op jit(solution)/shard_map/ppermute | solution.py:151
  1506.1 8.3 collective-permute-start.15
  (174 other events, 1289.6 us)
Sparse Core Ops, SparseCore 0:
  11.1 175.1 all-gather.5

commit v2 on v1

v2 whole, which is shorter than its diff:
```python
import functools
import math

import jax
import jax.numpy as jnp
from jax import lax
from jax.experimental import pallas as pl
from jax.experimental.pallas import tpu as pltpu
from jax.sharding import PartitionSpec as P

HEADS = 16
BF = jnp.bfloat16
F32 = jnp.float32


def dot(a, b, dims):
    return lax.dot_general(a, b, (dims, ((), ())), preferred_element_type=F32)


LIGHT = pl.CostEstimate(flops=1_000_000, bytes_accessed=100_000, transcendentals=0)
NN, NT, TN = ((1,), (0,)), ((1,), (1,)), ((0,), (0,))


def iota(shape, dim):
    return lax.broadcasted_iota(jnp.int32, shape, dim)


def chosen(condition):
    return jnp.where(condition, 1.0, 0.0).astype(BF)


def half_lanes(block, sub):
    lane = iota(block.shape, 1)
    width = block.shape[1] // 2
    inside = (lane < width) if sub == 0 else (lane >= width)
    return jnp.where(inside, block.astype(F32), 0.0).astype(BF)


def normal_of(rows):
    average = jnp.mean(rows, axis=-1, keepdims=True)
    centred = rows - average
    inverse = lax.rsqrt(jnp.mean(centred * centred, axis=-1, keepdims=True) + 1e-05)
    return centred * inverse, inverse


def fill_bias(bias, length):
    seq = bias.shape[0]
    query, key = iota((seq, seq), 0), iota((seq, seq), 1)
    bias[...] = jnp.where((key <= query) & (key < length), 0.0, -1e30)


def query_blocks(seq):
    block = 256 if seq % 256 == 0 else seq
    return [(start, block, start + block) for start in range(0, seq, block)]


def forward_kernel(
    length, column, row, arrived, w, small, placed, rows_out, q_out, k_out, v_out, att_out, lse_out, bias, normed
):
    slots, width = arrived.shape
    seq = column.shape[0]
    head = width // HEADS
    scale = head**-0.5
    fill_bias(bias, length[0, 0])
    chunk, tile = 128, 256

    @pl.loop(0, seq // chunk)
    def _(c):
        at = pl.ds(pl.multiple_of(c * chunk, chunk), chunk)
        pick = chosen(column[at, :] == iota((chunk, slots), 1))
        rows = dot(pick, arrived[...], NN)
        rows_out[at, :] = rows.astype(BF)
        normal, _ = normal_of(rows)
        normed[at, :] = (normal * small[0:1, :] + small[1:2, :]).astype(BF)

    @pl.loop(0, width // tile)
    def _(n):
        at = pl.ds(pl.multiple_of(n * tile, tile), tile)
        x = normed[...]
        q_out[:, at] = (dot(x, w[0, :, at], NN) + small[2:3, at]).astype(BF)
        k_out[:, at] = dot(x, w[1, :, at], NN).astype(BF)
        v_out[:, at] = (dot(x, w[2, :, at], NN) + small[3:4, at]).astype(BF)

    @pl.loop(0, HEADS // 2)
    def _(pair):
        at = pl.ds(pl.multiple_of(pair * 2 * head, 2 * head), 2 * head)
        k2, v2 = k_out[:, at], v_out[:, at]
        values = [half_lanes(v2, sub) for sub in (0, 1)]
        for start, size, reach in query_blocks(seq):
            q2 = q_out[start : start + size, at]
            total = None
            lse_block = lse_out[start : start + size, :]
            lane = iota(lse_block.shape, 1)
            for sub in (0, 1):
                s = dot(half_lanes(q2, sub), k2[:reach], NT) * scale + bias[start : start + size, :reach]
                top = jnp.max(s, axis=-1, keepdims=True)
                p = jnp.exp(s - top)
                l = jnp.sum(p, axis=-1, keepdims=True)
                out = dot((p * (1.0 / l)).astype(BF), values[sub][:reach], NN)
                total = out if sub == 0 else total + out
                lse_block = jnp.where(lane == 2 * pair + sub, top + jnp.log(l), lse_block)
            att_out[start : start + size, at] = total.astype(BF)
            lse_out[start : start + size, :] = lse_block

    @pl.loop(0, width // tile)
    def _(n):
        at = pl.ds(pl.multiple_of(n * tile, tile), tile)
        normed[:, at] = (dot(att_out[...], w[3, :, at], NN) + small[4:5, at]).astype(BF)

    @pl.loop(0, slots // chunk)
    def _(c):
        at = pl.ds(pl.multiple_of(c * chunk, chunk), chunk)
        put = chosen(row[...] == iota((chunk, seq), 0) + c * chunk)
        placed[at, :] = dot(put, normed[...], NN).astype(BF)


def attention_forward(arrived, slot_ids, length, w, small):
    slots, width = arrived.shape
    seq = slot_ids.shape[0]
    wide = jax.ShapeDtypeStruct((seq, width), BF)
    vm = pl.BlockSpec(memory_space=pltpu.VMEM)
    out = pl.pallas_call(
        forward_kernel,
        in_specs=[pl.BlockSpec(memory_space=pltpu.SMEM)] + [vm] * 5,
        out_specs=[vm] * 7,
        out_shape=[jax.ShapeDtypeStruct((slots, width), BF)]
        + [wide] * 5
        + [jax.ShapeDtypeStruct((seq, 128), F32)],
        scratch_shapes=[pltpu.VMEM((seq, seq), F32), pltpu.VMEM((seq, width), BF)],
        compiler_params=pltpu.CompilerParams(vmem_limit_bytes=48 << 20),
        cost_estimate=LIGHT,
    )(length.reshape(1, 1), slot_ids.reshape(seq, 1), slot_ids.reshape(1, seq), arrived, w, small)
    return out[0], tuple(out[1:])


def backward_kernel(
    groups, length, core, column, row, arrived, w, small, rows_in, q, k, v, att, lse,
    placed, *rest,
):
    keep, give, sums = rest[:4], rest[4:8], rest[8]
    bias, normed, grad_out, grad_att, dq, dk, dv, grad_normed = rest[9:]
    slots, width = arrived.shape
    seq = column.shape[0]
    head = width // HEADS
    scale = head**-0.5
    fill_bias(bias, length[0, 0])
    chunk, tile = 128, 256
    sums[...] = jnp.zeros_like(sums)

    @pl.loop(0, seq // chunk)
    def _(c):
        at = pl.ds(pl.multiple_of(c * chunk, chunk), chunk)
        pick = chosen(column[at, :] == iota((chunk, slots), 1))
        rows = dot(pick, arrived[...], NN)
        grad_out[at, :] = rows.astype(BF)
        sums[4:5, :] += jnp.sum(rows, axis=0, keepdims=True)
        normal, _ = normal_of(rows_in[at, :].astype(F32))
        normed[at, :] = (normal * small[0:1, :] + small[1:2, :]).astype(BF)

    @pl.loop(0, width // tile)
    def _(n):
        at = pl.ds(pl.multiple_of(n * tile, tile), tile)
        grad_att[:, at] = dot(grad_out[...], w[3, at, :], NT).astype(BF)

    @pl.loop(0, HEADS // 2)
    def _(pair):
        at = pl.ds(pl.multiple_of(pair * 2 * head, 2 * head), 2 * head)
        k2, v2 = k[:, at], v[:, at]
        keys = [half_lanes(k2, sub) for sub in (0, 1)]
        dks, dvs = [], []
        for start, size, reach in query_blocks(seq):
            span = slice(start, start + size)
            q2, g2, lse_block = q[span, at], grad_att[span, at], lse[span, :]
            lane = iota(lse_block.shape, 1)
            dq_total = dk_total = dv_total = None
            for sub in (0, 1):
                qs, gs = half_lanes(q2, sub), half_lanes(g2, sub)
                level = jnp.sum(jnp.where(lane == 2 * pair + sub, lse_block, 0.0), axis=-1, keepdims=True)
                s = dot(qs, k2[:reach], NT) * scale + bias[span, :reach]
                p = jnp.exp(s - level)
                dp = dot(gs, v2[:reach], NT)
                mean = jnp.sum(p * dp, axis=-1, keepdims=True)
                ds = (p * (dp - mean)).astype(BF)
                parts = (dot(ds, keys[sub][:reach], NN), dot(ds, qs, TN), dot(p.astype(BF), gs, TN))
                if sub == 0:
                    dq_total, dk_total, dv_total = parts
                else:
                    dq_total, dk_total, dv_total = (
                        dq_total + parts[0], dk_total + parts[1], dv_total + parts[2]
                    )
            dq[span, at] = (dq_total * scale).astype(BF)
            dks.append((reach, dk_total))
            dvs.append((reach, dv_total))
        for ref, pieces, factor in ((dk, dks, scale), (dv, dvs, 1.0)):
            before = 0
            for index, (reach, _) in enumerate(pieces):
                total = sum(piece[before:reach] for _, piece in pieces[index:])
                ref[before:reach, at] = (total * factor).astype(BF)
                before = reach

    for m, (left, right) in enumerate(((normed, dq), (normed, dk), (normed, dv), (att, grad_out))):
        write_dense(groups, keep[m], give[m], core, left, right)

    @pl.loop(0, width // tile)
    def _(n):
        at = pl.ds(pl.multiple_of(n * tile, tile), tile)
        grad_normed[:, at] = (
            dot(dq[...], w[0, at, :], NT) + dot(dk[...], w[1, at, :], NT) + dot(dv[...], w[2, at, :], NT)
        )

    @pl.loop(0, seq // chunk)
    def _(c):
        at = pl.ds(pl.multiple_of(c * chunk, chunk), chunk)
        normal, inverse = normal_of(rows_in[at, :].astype(F32))
        g = grad_normed[at, :]
        sums[0:1, :] += jnp.sum(g * normal, axis=0, keepdims=True)
        sums[1:2, :] += jnp.sum(g, axis=0, keepdims=True)
        sums[2:3, :] += jnp.sum(dq[at, :].astype(F32), axis=0, keepdims=True)
        sums[3:4, :] += jnp.sum(dv[at, :].astype(F32), axis=0, keepdims=True)
        u = g * small[0:1, :]
        back = inverse * (
            u - jnp.mean(u, axis=-1, keepdims=True) - normal * jnp.mean(u * normal, axis=-1, keepdims=True)
        )
        grad_out[at, :] = back.astype(BF)

    @pl.loop(0, slots // chunk)
    def _(c):
        at = pl.ds(pl.multiple_of(c * chunk, chunk), chunk)
        put = chosen(row[...] == iota((chunk, seq), 0) + c * chunk)
        placed[at, :] = dot(put, grad_out[...], NN).astype(BF)


def write_dense(groups, keep, give, core, left, right):
    width = right.shape[1]
    share = width // (2 * keep.shape[0])
    side = share * groups
    pieces = max(2 * side, 128) // side

    @pl.loop(0, width // (side * pieces))
    def _(step):
        at = pl.ds(pl.multiple_of(step * side * pieces, side * pieces), side * pieces)
        block = dot(left[:, at], right[...], TN).astype(BF).reshape(pieces, groups, share, width)
        for i in range(pieces):
            to = pl.ds((step * (pieces // 2) + i // 2) * groups, groups)

            @pl.when(core[0, 0] == i % 2)
            def _():
                keep[to] = block[i]

            @pl.when(core[0, 0] != i % 2)
            def _():
                give[to] = block[i]


def attention_backward(arrived, slot_ids, length, core, w, small, saved, owners, groups):
    slots, width = arrived.shape
    seq = slot_ids.shape[0]
    vm = pl.BlockSpec(memory_space=pltpu.VMEM)
    sm = pl.BlockSpec(memory_space=pltpu.SMEM)
    half = jax.ShapeDtypeStruct((owners // 2, width // owners, width), BF)
    out = pl.pallas_call(
        functools.partial(backward_kernel, groups),
        in_specs=[sm, sm] + [vm] * 11,
        out_specs=[vm] * 10,
        out_shape=[jax.ShapeDtypeStruct((slots, width), BF)] + [half] * 8 + [jax.ShapeDtypeStruct((8, width), F32)],
        scratch_shapes=[pltpu.VMEM((seq, seq), F32)]
        + [pltpu.VMEM((seq, width), BF)] * 6
        + [pltpu.VMEM((seq, width), F32)],
        compiler_params=pltpu.CompilerParams(vmem_limit_bytes=60 << 20),
        cost_estimate=LIGHT,
    )(
        length.reshape(1, 1), core.reshape(1, 1), slot_ids.reshape(seq, 1), slot_ids.reshape(1, seq),
        arrived, w, small, *saved,
    )
    return out[0], out[1:5], out[5:9], out[9]


def place_kernel(n_f, share, place, *refs):
    pieces, dense, table = refs[:-2], refs[-2], refs[-1]
    chips = len(pieces) // 2
    ex, fi = place[0, 0], place[0, 1]
    for c in range(2):
        for k in range(chips):
            for r in range(n_f):
                owner = jnp.bitwise_xor(ex, 2 * k + c) * n_f + jnp.bitwise_xor(fi, r)
                piece = pieces[c * chips + k]
                rows = pl.ds(pl.multiple_of(owner * share, share), share)
                for m in range(4):
                    dense[m, rows, :] = piece[r, m * share : (m + 1) * share, :]
                table[owner] = piece[r, 4 * share :, :]


def place_rows(pieces, ex, fi, share):
    n_f, lines, width = pieces[0].shape
    owners = len(pieces) * n_f
    vm = pl.BlockSpec(memory_space=pltpu.VMEM)
    return pl.pallas_call(
        functools.partial(place_kernel, n_f, share),
        in_specs=[pl.BlockSpec(memory_space=pltpu.SMEM)] + [vm] * len(pieces),
        out_specs=[vm] * 2,
        out_shape=[
            jax.ShapeDtypeStruct((4, owners * share, width), BF),
            jax.ShapeDtypeStruct((owners, lines - 4 * share, width), BF),
        ],
        compiler_params=pltpu.CompilerParams(vmem_limit_bytes=40 << 20),
        cost_estimate=LIGHT,
    )(jnp.stack([ex, fi]).astype(jnp.int32).reshape(1, 2), *pieces)


def add_dense_kernel(*refs):
    terms, vector, out = refs[:-2], refs[-2], refs[-1]
    share = terms[0].shape[1]
    for m in range(4):
        total = sum(ref[...].astype(F32) for ref in terms[m::4])
        out[:, m * share : (m + 1) * share, :] = total.astype(BF)
    out[:, 4 * share :, :] = vector[...].astype(BF)


def add_dense(terms, vector):
    count, share, width = terms[0].shape
    lines = vector.shape[1]
    block = pl.BlockSpec((2, share, width), lambda o: (o, 0, 0))
    return pl.pallas_call(
        add_dense_kernel,
        grid=(count // 2,),
        in_specs=[block] * len(terms) + [pl.BlockSpec((2, lines, width), lambda o: (o, 0, 0))],
        out_specs=pl.BlockSpec((2, 4 * share + lines, width), lambda o: (o, 0, 0)),
        out_shape=jax.ShapeDtypeStruct((count, 4 * share + lines, width), BF),
        cost_estimate=LIGHT,
    )(*terms, vector)


def add_near_kernel(a, c, got, out_in, out_out):
    out_in[0] = a[0] + jnp.transpose(got[0, 0].astype(F32))
    out_out[0] = c[0] + got[0, 1].astype(F32)


def add_near(dwi_own, dwo_own, got):
    le, width, hidden = dwi_own.shape
    tile = 256
    turned = pl.BlockSpec((1, width, tile), lambda j, c: (j, 0, c))
    plain = pl.BlockSpec((1, tile, width), lambda j, c: (j, c, 0))
    both = pl.BlockSpec((1, 2, tile, width), lambda j, c: (j, 0, c, 0))
    return pl.pallas_call(
        add_near_kernel,
        grid=(le, hidden // tile),
        in_specs=[turned, plain, both],
        out_specs=[turned, plain],
        out_shape=[jax.ShapeDtypeStruct(dwi_own.shape, F32), jax.ShapeDtypeStruct(dwo_own.shape, F32)],
        input_output_aliases={0: 0, 1: 1},
        cost_estimate=LIGHT,
    )(dwi_own, dwo_own, got)


def mixed_norm_kernel(rows, back, gain, shift, out):
    normal, _ = normal_of(rows[0].astype(F32) + back[0].astype(F32))
    out[0] = (normal * gain[...] + shift[...]).astype(BF)


def mixed_norm(rows, back, gain, shift):
    le, n, width = rows.shape
    block = pl.BlockSpec((1, 128, width), lambda j, c: (j, c, 0))
    line = pl.BlockSpec((1, width), lambda j, c: (0, 0))
    return pl.pallas_call(
        mixed_norm_kernel,
        grid=(le, n // 128),
        in_specs=[block, block, line, line],
        out_specs=block,
        out_shape=jax.ShapeDtypeStruct((le, n, width), BF),
        cost_estimate=LIGHT,
    )(rows, back, gain, shift)


def mixed_back_kernel(rows, back, gx, gx_far, cot, fill, gain, exact, low, sums):
    @pl.when((pl.program_id(0) == 0) & (pl.program_id(1) == 0))
    def _():
        sums[...] = jnp.zeros_like(sums)

    normal, inverse = normal_of(rows[0].astype(F32) + back[0].astype(F32))
    g = gx[0].astype(F32) + gx_far[0].astype(F32)
    sums[0:1, :] += jnp.sum(g * normal, axis=0, keepdims=True)
    sums[1:2, :] += jnp.sum(g, axis=0, keepdims=True)
    u = g * gain[...]
    total = cot[0].astype(F32) * fill[0] + inverse * (
        u - jnp.mean(u, axis=-1, keepdims=True) - normal * jnp.mean(u * normal, axis=-1, keepdims=True)
    )
    exact[0] = total
    low[0] = total.astype(BF)


def mixed_back(rows, back, gx, gx_far, cot, fill, gain):
    le, n, width = rows.shape
    block = pl.BlockSpec((1, 128, width), lambda j, c: (j, c, 0))
    mark = pl.BlockSpec((1, 128, 1), lambda j, c: (j, c, 0))
    return pl.pallas_call(
        mixed_back_kernel,
        grid=(le, n // 128),
        in_specs=[block] * 5 + [mark, pl.BlockSpec((1, width), lambda j, c: (0, 0))],
        out_specs=[block, block, pl.BlockSpec((8, width), lambda j, c: (0, 0))],
        out_shape=[
            jax.ShapeDtypeStruct((le, n, width), F32),
            jax.ShapeDtypeStruct((le, n, width), BF),
            jax.ShapeDtypeStruct((8, width), F32),
        ],
        cost_estimate=LIGHT,
    )(rows, back, gx, gx_far, cot, fill, gain)


def gelu_parts(v):
    a, b = 0.7978845608028654, 0.044715
    square = v * v
    t = jnp.tanh(a * v * (1.0 + b * square))
    half = 0.5 * (1.0 + t)
    slope = half + 0.5 * v * (1.0 - t * t) * (a * (1.0 + 3.0 * b * square))
    return v * half, slope


def expert_kernel(first, tiles, *refs):
    (x_own, x_far, g_own, g_far, fill_own, fill_far, wi_own, wi_near, wo_own, wo_near, bias) = refs[:11]
    before = [None] * 5 if first else refs[11:16]
    (out_own, out_far, gx_own, gx_far, dwi_own, dwo_own, dw_near, db, dbo,
     xs, gs, out_sum, gx_sum) = refs[11 if first else 16 :]
    h = pl.program_id(1)
    rows = x_own.shape[1]

    @pl.when(h == 0)
    def _():
        xs[:rows, :] = x_own[0]
        xs[rows:, :] = x_far[0]
        total = None
        for start, ref, fill in ((0, g_own, fill_own), (rows, g_far, fill_far)):
            g = ref[0].astype(F32) * fill[0]
            gs[start : start + rows, :] = g.astype(BF)
            part = jnp.sum(g, axis=0, keepdims=True)
            total = part if total is None else total + part
        dbo[0] = total if first else total + before[4][0]

    def tile_step(wi, wo, mine):
        x, g = xs[...], gs[...]
        inner = dot(x, wi, NN) + bias[0]
        act, slope = gelu_parts(inner)
        act = act.astype(BF)
        grad_inner = (dot(g, wo, NT) * slope).astype(BF)
        out = dot(act, wo, NN)
        gx = dot(grad_inner, wi, NT)
        dwi = dot(x, grad_inner, TN) if mine else dot(grad_inner, x, TN)
        dwo = dot(act, g, TN)
        column = jnp.sum(grad_inner.astype(F32), axis=0, keepdims=True)
        if mine:
            dwi_own[0] = dwi if first else dwi + before[0][0]
            dwo_own[0] = dwo if first else dwo + before[1][0]
        else:
            dw_near[0, 0] = (dwi if first else dwi + before[2][0, 0]).astype(dw_near.dtype)
            dw_near[0, 1] = (dwo if first else dwo + before[2][0, 1]).astype(dw_near.dtype)
        db[0] = column if first else column + before[3][0]

        @pl.when(h == 0)
        def _():
            out_sum[...] = out
            gx_sum[...] = gx

        @pl.when(h != 0)
        def _():
            out_sum[...] += out
            gx_sum[...] += gx

    @pl.when(h < tiles)
    def _():
        tile_step(wi_own[0], wo_own[0], True)

    @pl.when(h >= tiles)
    def _():
        tile_step(wi_near[0], wo_near[0], False)

    @pl.when(h == 2 * tiles - 1)
    def _():
        out_own[0] = out_sum[:rows, :].astype(BF)
        out_far[0] = out_sum[rows:, :].astype(BF)
        gx_own[0] = gx_sum[:rows, :].astype(BF)
        gx_far[0] = gx_sum[rows:, :].astype(BF)


def expert_step(x_own, x_far, g_own, g_far, fills, wi_own, wo_own, w_near, bias, before, tile=256):
    le, rows, width = x_own.shape
    hidden = wi_own.shape[2]
    tiles = hidden // tile
    first = before is None
    row = pl.BlockSpec((1, rows, width), lambda j, h: (j, 0, 0))
    mark = pl.BlockSpec((1, rows, 1), lambda j, h: (j, 0, 0))
    own_in = pl.BlockSpec((1, width, tile), lambda j, h: (j, 0, jnp.minimum(h, tiles - 1)))
    near_in = pl.BlockSpec((1, width, tile), lambda j, h: (j, 0, jnp.maximum(h - tiles, 0)))
    own_out = pl.BlockSpec((1, tile, width), lambda j, h: (j, jnp.minimum(h, tiles - 1), 0))
    near_out = pl.BlockSpec((1, tile, width), lambda j, h: (le + j, jnp.maximum(h - tiles, 0), 0))
    near_grads = pl.BlockSpec((1, 2, tile, width), lambda j, h: (j, 0, jnp.maximum(h - tiles, 0), 0))
    column = pl.BlockSpec((1, 1, tile), lambda j, h: (j, 0, h))
    line = pl.BlockSpec((1, 1, width), lambda j, h: (j, 0, 0))
    shapes = [jax.ShapeDtypeStruct((le, rows, width), BF)] * 4 + [
        jax.ShapeDtypeStruct((le, width, hidden), F32),
        jax.ShapeDtypeStruct((le, hidden, width), F32),
        jax.ShapeDtypeStruct((le, 2, hidden, width), F32 if first else BF),
        jax.ShapeDtypeStruct((le, 1, 2 * hidden), F32),
        jax.ShapeDtypeStruct((le, 1, width), F32),
    ]
    grads = [own_in, own_out, near_grads, column, line]
    operands = [x_own, x_far, g_own, g_far, *fills, wi_own, w_near, wo_own, w_near, bias]
    in_specs = [row] * 4 + [mark] * 2 + [own_in, near_in, own_out, near_out, column]
    if not first:
        operands += list(before)
        in_specs += grads
    return pl.pallas_call(
        functools.partial(expert_kernel, first, tiles),
        grid=(le, 2 * tiles),
        in_specs=in_specs,
        out_specs=[row] * 4 + grads,
        out_shape=shapes,
        scratch_shapes=[pltpu.VMEM((2 * rows, width), BF)] * 2 + [pltpu.VMEM((2 * rows, width), F32)] * 2,
        compiler_params=pltpu.CompilerParams(vmem_limit_bytes=60 << 20),
        cost_estimate=LIGHT,
    )(*operands)


def pick(array, index, dim):
    return lax.dynamic_index_in_dim(array, index, dim, keepdims=False)


def after(array, *others):
    return lax.optimization_barrier((array,) + others)[0]


def crossed(n, step):
    return [(i, i ^ step) for i in range(n)]


def gather_all(shard, first, n_exp, n_f, ex, fi, share):
    block, step = shard[None], 1
    while step < n_f:
        block = jnp.concatenate([block, lax.ppermute(block, "fsdp", crossed(n_f, step))])
        if step == 1:
            block = after(block, first)
        step *= 2
    pieces = [block] + [lax.ppermute(block, "exp", crossed(n_exp, 2 * k)) for k in range(1, n_exp // 2)]
    pieces += [lax.ppermute(piece, "exp", crossed(n_exp, 1)) for piece in pieces]
    return block, place_rows(pieces, ex, fi, share)


def reduce_plane(low, n_exp, chip):
    chips = n_exp // 2
    view = low.reshape(chips, -1, low.shape[1], low.shape[2])
    total = pick(view, chip, 0).astype(F32)
    for step in range(1, chips):
        block = pick(view, chip ^ step, 0)
        total = total + lax.ppermute(block, "exp", crossed(n_exp, 2 * step)).astype(F32)
    return total


def reduce_groups(total, n_f, fi):
    half = n_f // 2
    while half >= 1:
        pairs = total.reshape(2, half, *total.shape[1:])
        side = (fi // half) % 2
        got = lax.ppermute(pick(pairs, 1 - side, 0).astype(BF), "fsdp", crossed(n_f, half))
        total = pick(pairs, side, 0) + got.astype(F32)
        half //= 2
    return total[0]


def body(
    block_input,
    expert_ids,
    seq_lengths,
    attn_norm_gain,
    attn_norm_bias,
    query_matrix,
    query_offset_bias,
    key_matrix,
    value_matrix,
    value_offset_bias,
    output_matrix,
    attention_output_bias,
    ffn_norm_gain,
    ffn_norm_bias,
    expert_in,
    expert_in_bias,
    expert_out,
    expert_out_bias,
    out_cotangent,
):
    mb, le, _, sources, cap, width = block_input.shape
    n_exp, n_f = lax.axis_size("exp"), lax.axis_size("fsdp")
    ex, fi = lax.axis_index("exp"), lax.axis_index("fsdp")
    chip, core = ex // 2, ex % 2
    everyone = ("exp", "fsdp")
    owners = n_exp * n_f
    experts = le * n_exp
    slots = experts * cap
    rows = sources * cap
    hidden = expert_in.shape[2]
    seq = expert_ids.shape[2]
    far, near = crossed(n_f, 2), crossed(n_f, 1)
    share = attn_norm_gain.shape[0]

    ids = expert_ids[:, 0, :, 0]
    onehot = ids[:, :, None] == jnp.arange(experts, dtype=jnp.int32)
    counts = jnp.sum(onehot.astype(F32), axis=1)
    position = jnp.arange(seq, dtype=jnp.int32)
    same = (ids[:, :, None] == ids[:, None, :]) & (position[None, None, :] < position[None, :, None])
    slot_ids = ids * cap + jnp.sum(same.astype(jnp.int32), axis=2)
    packed = jnp.concatenate(
        [
            attn_norm_gain,
            attn_norm_bias,
            query_offset_bias,
            value_offset_bias,
            attention_output_bias,
            ffn_norm_gain,
            ffn_norm_bias,
            expert_out_bias.reshape(-1),
            expert_in_bias.reshape(-1),
            counts.astype(BF).reshape(-1),
        ]
    )
    lines = -(-packed.size // (16 * width)) * 16
    packed = jnp.pad(packed, (0, lines * width - packed.size)).reshape(lines, width)
    shipped = jnp.concatenate([query_matrix, key_matrix, value_matrix, output_matrix, packed])
    arrived_all = [
        lax.all_to_all(block_input[t, :, 0], "exp", split_axis=1, concat_axis=0, tiled=True).reshape(slots, width)
        for t in range(mb)
    ]
    ready, (dense_full, table) = gather_all(shipped, arrived_all[0], n_exp, n_f, ex, fi, share)
    table = table.reshape(owners, -1).astype(F32)
    cot = out_cotangent[:, :, 0].reshape(mb, le, rows, width)
    cot_far = lax.ppermute(after(cot, ready), "fsdp", far)
    w_near = lax.ppermute(after(jnp.concatenate([expert_in, expert_out]), ready), "fsdp", near)
    block_rows = block_input[:, :, 0].reshape(mb, le, rows, width)

    small = jnp.stack(
        [table[:, i * share : (i + 1) * share].reshape(-1) for i in range(7)] + [jnp.zeros((width,), F32)]
    )
    at = 7 * share
    table = table.reshape(n_exp, n_f, -1)
    mine = pick(table, ex, 0)
    bias_out = mine[:, at : at + expert_out_bias.size].reshape(n_f, le, -1).transpose(1, 0, 2).reshape(le, width)
    at += expert_out_bias.size
    bias_in = mine[:, at : at + le * hidden].reshape(n_f, le, hidden)
    bias_in = jnp.concatenate([pick(bias_in, fi, 0), pick(bias_in, fi ^ 1, 0)], axis=1)[:, None, :]
    at += le * hidden
    my_counts = table[:, :, at : at + counts.size].reshape(n_exp, n_f, mb, n_exp, le)
    my_counts = pick(my_counts, ex, 3)

    def fill(group):
        count = pick(my_counts, group, 1).transpose(1, 2, 0)[:, :, :, None]
        return (jnp.arange(cap, dtype=F32) < count).astype(F32).reshape(mb, le, rows, 1)

    fill_own, fill_far = fill(fi), fill(fi ^ 2)

    saved, back_rows, normed_two = [], [], []
    for t in range(mb):
        placed, kept = attention_forward(arrived_all[t], slot_ids[t], seq_lengths[t, 0], dense_full, small)
        saved.append(kept)
        back_rows.append(
            lax.all_to_all(
                placed.reshape(experts, cap, width), "exp", split_axis=0, concat_axis=1, tiled=True
            ).reshape(le, rows, width)
        )
        normed_two.append(mixed_norm(block_rows[t], back_rows[t], small[5:6], small[6:7]))
    normed_far = [lax.ppermute(normed_two[0], "fsdp", far)]
    for t in range(1, mb):
        rows_sent, cot_far = lax.optimization_barrier((normed_two[t], cot_far))
        normed_far.append(lax.ppermute(rows_sent, "fsdp", far))

    ffn, before = [], None
    for t in range(mb):
        ffn.append(
            expert_step(
                normed_two[t], normed_far[t], cot[t], cot_far[t], (fill_own[t], fill_far[t]),
                expert_in, expert_out, w_near, bias_in, before,
            )
        )
        before = ffn[t][4:]
    gx_far = [lax.ppermute(ffn[0][3], "fsdp", far)]
    for t in range(1, mb):
        gx_far.append(lax.ppermute(after(ffn[t][3], gx_far[t - 1]), "fsdp", far))
    dwi_own, dwo_own, dw_near, db, dbo = before
    dw_got = lax.ppermute(after(dw_near, gx_far[mb - 1]), "fsdp", near)
    out_far = lax.ppermute(after(jnp.stack([ffn[t][1] for t in range(mb)]), gx_far[mb - 1]), "fsdp", far)
    dbo = dbo[:, 0]
    vectors = lax.ppermute(jnp.concatenate([db[:, 0, hidden:], dbo], axis=1), "fsdp", near)

    input_grads, terms, small_total = [], [], None
    for t in range(mb):
        grad_mixed, to_send, norm_sums = mixed_back(
            block_rows[t], back_rows[t], ffn[t][2], gx_far[t], cot[t], fill_own[t], small[5:6]
        )
        grad_arrived = lax.all_to_all(
            to_send.reshape(le, sources, cap, width), "exp", split_axis=1, concat_axis=0, tiled=True
        ).reshape(slots, width)
        placed_back, keep, give, sums = attention_backward(
            grad_arrived, slot_ids[t], seq_lengths[t, 0], core, dense_full, small, saved[t], owners, n_f
        )
        returned = lax.all_to_all(
            placed_back.reshape(experts, cap, width), "exp", split_axis=0, concat_axis=1, tiled=True
        ).reshape(le, rows, width)
        input_grads.append(
            (grad_mixed + returned.astype(F32)).astype(BF).reshape(le, 1, sources, cap, width)
        )
        sums = jnp.concatenate([sums[:5], norm_sums[:2]])
        terms += list(keep) + [lax.ppermute(part, "exp", crossed(n_exp, 1)) for part in give]
        small_total = sums if t == 0 else small_total + sums

    vector = small_total.reshape(7, owners, share).transpose(1, 0, 2).reshape(owners, 7 * share)
    vector = jnp.pad(vector, ((0, 0), (0, width - 7 * share)))[:, None, :]
    vector = vector.reshape(n_exp // 2, 2, n_f, 1, width)
    vector = pick(vector, core, 1) + lax.ppermute(pick(vector, 1 - core, 1), "exp", crossed(n_exp, 1))
    vector = jnp.pad(vector.reshape(owners // 2, 1, width), ((0, 0), (0, 15), (0, 0)))
    grad_in, grad_out = add_near(dwi_own, dwo_own, dw_got)
    low, grad_in, grad_out, out_far = lax.optimization_barrier((add_dense(terms, vector), grad_in, grad_out, out_far))
    total = reduce_groups(reduce_plane(low, n_exp, chip), n_f, fi)
    dense = total[: 4 * share].reshape(4, share, width)
    smalls = total[4 * share, : 7 * share].reshape(7, share)

    outputs = []
    for t in range(mb):
        mixed = block_rows[t].astype(F32) + back_rows[t].astype(F32)
        ffn_out = ffn[t][0].astype(F32) + out_far[t].astype(F32) + bias_out[:, None, :]
        outputs.append(
            ((mixed + ffn_out) * fill_own[t]).astype(BF).reshape(le, 1, sources, cap, width)
        )
    grad_in_bias = db[:, 0, :hidden] + vectors[:, :hidden]
    grad_out_bias = lax.dynamic_slice_in_dim(
        dbo + vectors[:, hidden:], fi * (width // n_f), width // n_f, 1
    )
    return (
        jnp.stack(outputs),
        jnp.stack(input_grads),
        smalls[0],
        smalls[1],
        dense[0],
        smalls[2],
        dense[1],
        dense[2],
        smalls[3],
        dense[3],
        smalls[4],
        smalls[5],
        smalls[6],
        grad_in,
        grad_in_bias,
        grad_out,
        grad_out_bias,
    )


def solution(mesh):
    rows, dense, vec = (
        P(None, "exp", "fsdp", None, None, None),
        P(("exp", "fsdp"), None),
        P(("exp", "fsdp")),
    )
    experts = (P("exp", None, "fsdp"), P("exp", "fsdp"), P("exp", "fsdp", None), P("exp", "fsdp"))
    return jax.shard_map(
        body,
        mesh=mesh,
        in_specs=(
            rows,
            P(None, ("exp", "fsdp"), None, None),
            P(None, ("exp", "fsdp")),
            vec,
            vec,
            dense,
            vec,
            dense,
            dense,
            vec,
            dense,
            vec,
            vec,
            vec,
        )
        + experts
        + (rows,),
        out_specs=(rows, rows, vec, vec, dense, vec, dense, dense, vec, dense, vec, vec, vec) + experts,
        check_vma=False,
    )
```

time: 1530 us -> 1010 us (0.66)
  blocking collectives: 480 us -> 0 us
  matrix products: 349 us -> 0 us
  Pallas kernels: 0 us -> 339 us
  waiting for transfers between devices: 327 us -> 508 us
  other arithmetic: 173 us -> 26.1 us
  local copies, waits for them, and re-layouts: 125 us -> 64.6 us
  between operations: 17.4 us -> 1.98 us
    all_gather x2 -> x0, blocking collectives: 480 us -> none  [the longest x1 345 us: body(): lax.all_gather(packed[None], everyone, axis=0, tiled=True).astype(F32)]
    dot_general x60 -> x0, matrix products: 349 us -> none  [the longest x48 245 us: dot(): return lax.dot_general(a, b, (dims, ((), ())), preferred_element_type=F32)]
    pallas_call x0 -> x13, Pallas kernels: none -> 339 us  [the longest x2 136 us: expert_step(): pl.pallas_call(functools.partial(expert_kernel, first, tiles), grid=(le,...]
    ppermute x19 -> x32, waiting for transfers between devices: 304 us -> 471 us  [the longest x1 94.8 us: body(): normed_far = [lax.ppermute(normed_two[0], 'fsdp', far)]]
    add x19 -> x5, other arithmetic: 47.2 us -> 4.41 us  [the longest x1 3.48 us: reduce_plane(): total + lax.ppermute(block, 'exp', crossed(n_exp, 2 * step)).astype(F32)]
    convert_element_type x13 -> x3, other arithmetic: 45.2 us -> 3.66 us  [the longest x1 3.35 us: body(): ((mixed + ffn_out) * fill_own[t]).astype(BF)]
    reduce_sum x18 -> x0, other arithmetic: 40.3 us -> none  [the longest x2 16.6 us: attend_forward(): row_total = jnp.sum(weights, axis=-1, keepdims=True)]
    convert_element_type x17 -> x3, local copies, waits for them, and re-layouts: 22.3 us -> 2.78 us  [the longest x1 2.65 us: body(): table = table.reshape(owners, -1).astype(F32)]
  transfers between devices with their start and end apart: 27 -> 40, of which waited for: 9 -> 21; matrix products, arithmetic and copies ran while one was open for 35% -> 6% of each run, Pallas kernels for 0% -> 34%
where the time goes in v2:
time: 1010 us; the launch traced here: 1000 us
  waiting for transfers between devices  508 us (50%)
  Pallas kernels  339 us (34%)
  local copies, waits for them, and re-layouts  64.6 us (6%)
  starting transfers between devices  63.3 us (6%)
  other arithmetic  26.1 us (3%)
    pallas_call x2, Pallas kernels, expert_step(): pl.pallas_call(functools.partial(expert_kernel, first, tiles), grid=(le,...  136 us
    ppermute x1, waiting for transfers between devices, body(): normed_far = [lax.ppermute(normed_two[0], 'fsdp', far)]  94.8 us
    pallas_call x2, Pallas kernels, attention_backward(): pl.pallas_call(functools.partial(backward_kernel, groups), in_specs=[sm,...  91.8 us
    ppermute x1, waiting for transfers between devices, body(): dw_got = lax.ppermute(after(dw_near, gx_far[mb - 1]), 'fsdp', near)  83.3 us
    ppermute x1, waiting for transfers between devices, body(): gx_far.append(lax.ppermute(after(ffn[t][3], gx_far[t - 1]), 'fsdp', far))  68 us
    ppermute x1, waiting for transfers between devices, body(): cot_far = lax.ppermute(after(cot, ready), 'fsdp', far)  64 us
    ppermute x3, waiting for transfers between devices, gather_all(): lax.ppermute(block, 'exp', crossed(n_exp, 2 * k))  51.3 us
    pallas_call x2, Pallas kernels, attention_forward(): pl.pallas_call(forward_kernel, in_specs=[pl.BlockSpec(memory_space=pltpu....  51.1 us
  transfers between devices with their start and end apart: 40, of which 21 were waited for; matrix products, arithmetic and copies ran while one was open for 6% of the time, Pallas kernels for 34%

profile of v2, /device:TPU:0, one launch (start us, length us, event | category | flops | bytes accessed | tf_op | source)
XLA Modules:
  0.0 1002.7 jit_solution(12086101097415555881)
XLA Ops:
  0.7 3.4 fusion.20
  5.9 5.3 all-to-all-start
  13.4 7.8 collective-permute-done
  21.3 11.0 %all-to-all-done = bf16[2,8,48,1024]{3,2,0,1:T(8,128)(2,1)S(1)} async-done(((bf16[2,8,48,1024]{3,2,0,1:T(8,128)(2,1)}), bf16[2,8,48,1024]{3,2,0,1:T(8,128)(2,1)S(1)}, u32[]{:S(2)}, u32[]{:S(2)}) %all-to-all-start) | async-done | bytes 1572896 | tf_op jit(solution)/shard_map/all_to_all | solution.py:626
  34.9 7.6 pad_maximum_fusion
  42.5 15.6 %collective-permute-done.1 = bf16[2,144,1024]{2,1,0:T(8,128)(2,1)S(1)} collective-permute-done((bf16[2,144,1024]{2,1,0:T(8,128)(2,1)S(1)}, bf16[2,144,1024]{2,1,0:T(8,128)(2,1)S(1)}, u32[]{:S(2)}, u32[]{:S(2)}) %collective-permute-start.1) | collective-permute-done | bytes 589856 | tf_op jit(solution)/shard_map/ppermute | solution.py:537
  58.9 3.5 collective-permute-start.2
  63.9 25.4 %collective-permute-done.2.refs_1_ = bf16[4,144,1024]{2,1,0:T(8,128)(2,1)} collective-permute-done((bf16[4,144,1024]{2,1,0:T(8,128)(2,1)S(1)}, bf16[4,144,1024]{2,1,0:T(8,128)(2,1)}, u32[]{:S(2)}, u32[]{:S(2)}) %collective-permute-start.2) | collective-permute-done | bytes 1179680 | tf_op jit(solution)/shard_map/ppermute | solution.py:541
  89.3 25.8 %collective-permute-done.3.refs_2_ = bf16[4,144,1024]{2,1,0:T(8,128)(2,1)} collective-permute-done((bf16[4,144,1024]{2,1,0:T(8,128)(2,1)S(1)}, bf16[4,144,1024]{2,1,0:T(8,128)(2,1)}, u32[]{:S(2)}, u32[]{:S(2)}) %collective-permute-start.3) | collective-permute-done | bytes 1179680 | tf_op jit(solution)/shard_map/ppermute | solution.py:541
  117.0 4.5 all-to-all-start.2
  123.1 7.4 shard_map.314
  132.7 25.5 %shard_map.315 = (bf16[768,1024]{1,0:T(8,128)(2,1)}, bf16[512,1024]{1,0:T(8,128)(2,1)S(1)}, bf16[512,1024]{1,0:T(8,128)(2,1)S(1)}, bf16[512,1024]{1,0:T(8,128)(2...) custom-call(s32[1,1]{1,0:T(1,128)} %bitcast.119.length, ...), custom_call_target="tpu_custom_call" | custom-call | flops 1000000 | bytes 100000 | tf_op jit(solution)/shard_map/pallas_call | solution.py:122
  164.0 4.3 all-to-all-start.1
  168.5 3.4 collective-permute-start.10
  171.9 4.1 fusion.19
  178.7 25.5 %shard_map.317 = (bf16[768,1024]{1,0:T(8,128)(2,1)}, bf16[512,1024]{1,0:T(8,128)(2,1)S(1)}, bf16[512,1024]{1,0:T(8,128)(2,1)S(1)}, bf16[512,1024]{1,0:T(8,128)(2...) custom-call(s32[1,1]{1,0:T(1,128)} %bitcast.118.length, ...), custom_call_target="tpu_custom_call" | custom-call | flops 1000000 | bytes 100000 | tf_op jit(solution)/shard_map/pallas_call | solution.py:122
  209.9 4.3 all-to-all-start.3
  215.5 5.5 shard_map.316.refs_0_
  225.6 9.6 all-to-all-done.3
  238.0 5.5 shard_map.318.refs_0_
  243.4 64.0 %collective-permute-done.10 = bf16[2,2,384,1024]{3,2,1,0:T(8,128)(2,1)} collective-permute-done((bf16[2,2,384,1024]{3,2,1,0:T(8,128)(2,1)}, bf16[2,2,384,1024]{3,2,1,0:T(8,128)(2,1)}, u32[]{:S(2)}, u32[]{:S(2)}) %collective-permute-start.10) | collective-permute-done | bytes 3145760 | tf_op jit(solution)/shard_map/ppermute | solution.py:632
  307.5 3.4 collective-permute-start.17
  310.9 3.9 slice_bitcast_fusion.1
  314.9 94.8 %collective-permute-done.9.refs_1_ = bf16[2,384,1024]{2,1,0:T(8,128)(2,1)S(1)} collective-permute-done((bf16[2,384,1024]{2,1,0:T(8,128)(2,1)}, bf16[2,384,1024]{2,1,0:T(8,128)(2,1)S(1)}, u32[]{:S(2)}, u32[]{:S(2)}) %collective-permute-start.9) | collective-permute-done | bytes 1572896 | tf_op jit(solution)/shard_map/ppermute | solution.py:666
  410.8 67.0 %shard_map.319 = (bf16[2,384,1024]{2,1,0:T(8,128)(2,1)}, bf16[2,384,1024]{2,1,0:T(8,128)(2,1)}, bf16[2,384,1024]{2,1,0:T(8,128)(2,1)}, bf16[2,384,1024]{2,1,0:T(...) custom-call(bf16[2,384,1024]{2,1,0:T(8,128)(2,1)} %shard_map.316.ref, ...), custom_call_target="tpu_custom_call" | custom-call | flops 1000000 | bytes 100000 | tf_op jit(solution)/shard_map/pallas_call | solution.py:510
  480.9 68.7 %shard_map.322 = (bf16[2,384,1024]{2,1,0:T(8,128)(2,1)}, bf16[2,384,1024]{2,1,0:T(8,128)(2,1)}, bf16[2,384,1024]{2,1,0:T(8,128)(2,1)}, bf16[2,384,1024]{2,1,0:T(...) custom-call(bf16[2,384,1024]{2,1,0:T(8,128)(2,1)} %shard_map.318.ref, ...), custom_call_target="tpu_custom_call" | custom-call | flops 1000000 | bytes 100000 | tf_op jit(solution)/shard_map/pallas_call | solution.py:510
  552.5 68.0 %collective-permute-done.18.gx_far = bf16[2,384,1024]{2,1,0:T(8,128)(2,1)} collective-permute-done((bf16[2,384,1024]{2,1,0:T(8,128)(2,1)}, bf16[2,384,1024]{2,1,0:T(8,128)(2,1)}, u32[]{:S(2)}, u32[]{:S(2)}) %collective-permute-start.18) | collective-permute-done | bytes 1572896 | tf_op jit(solution)/shard_map/ppermute | solution.py:682
  620.6 8.0 shard_map.320
  631.4 3.6 all-to-all-start.4
  635.0 8.0 shard_map.323
  645.7 10.2 %all-to-all-done.4 = bf16[2,8,48,1024]{3,2,0,1:T(8,128)(2,1)S(1)} async-done(((bf16[2,8,48,1024]{3,2,0,1:T(8,128)(2,1)}), bf16[2,8,48,1024]{3,2,0,1:T(8,128)(2,1)S(1)}, u32[]{:S(2)}, u32[]{:S(2)}) %all-to-all-start.4) | async-done | bytes 1572896 | tf_op jit(solution)/shard_map/all_to_all | solution.py:694
  657.1 3.8 all-to-all-start.5
  660.9 46.0 %shard_map.321 = (bf16[768,1024]{1,0:T(8,128)(2,1)}, bf16[16,32,1024]{2,1,0:T(8,128)(2,1)}, bf16[16,32,1024]{2,1,0:T(8,128)(2,1)}, bf16[16,32,1024]{2,1,0:T(8,12...) custom-call(s32[1,1]{1,0:T(1,128)} %bitcast.119.length, ...), custom_call_target="tpu_custom_call" | custom-call | flops 1000000 | bytes 100000 | tf_op jit(solution)/shard_map/pallas_call | solution.py:261
  707.5 3.4 pad_maximum_fusion.1
  716.2 45.8 %shard_map.324 = (bf16[768,1024]{1,0:T(8,128)(2,1)}, bf16[16,32,1024]{2,1,0:T(8,128)(2,1)}, bf16[16,32,1024]{2,1,0:T(8,128)(2,1)}, bf16[16,32,1024]{2,1,0:T(8,12...) custom-call(s32[1,1]{1,0:T(1,128)} %bitcast.118.length, ...), custom_call_target="tpu_custom_call" | custom-call | flops 1000000 | bytes 100000 | tf_op jit(solution)/shard_map/pallas_call | solution.py:261
  762.2 4.6 all-to-all-start.6
  775.8 10.4 %shard_map.325 = bf16[16,144,1024]{2,1,0:T(8,128)(2,1)} custom-call(bf16[16,32,1024]{2,1,0:T(8,128)(2,1)} %get-tuple-element.109.refs_0_, bf16[16,32,1024]{2,1,0:T(8,128)(2,1)} %get-tuple-element.110.refs_1_, bf16[16,32,1024]{2,1,0:T(8,128)(2,1)} %get-tuple-element.111.refs_2_, bf16[16,32,1024]{2,1,0:T(8,128)(2,1)} %get-tuple-element.112.refs_3_, ...), custom_call_target="tpu_custom_call" | custom-call | flops 1000000 | bytes 100000 | tf_op jit(solution)/shard_map/pallas_call | solution.py:323
  786.3 83.3 %collective-permute-done.24.got = bf16[2,2,1024,1024]{3,2,1,0:T(8,128)(2,1)} collective-permute-done((bf16[2,2,1024,1024]{3,2,1,0:T(8,128)(2,1)}, bf16[2,2,1024,1024]{3,2,1,0:T(8,128)(2,1)}, u32[]{:S(2)}, u32[]{:S(2)}) %collective-permute-start.24) | collective-permute-done | bytes 8388640 | tf_op jit(solution)/shard_map/ppermute | solution.py:684
  869.5 15.5 %shard_map.326 = (f32[2,1024,1024]{2,1,0:T(8,128)}, f32[2,1024,1024]{2,1,0:T(8,128)}) custom-call(f32[2,1024,1024]{2,1,0:T(8,128)} %get-tuple-element.145.a, f32[2,1024,1024]{2,1,0:T(8,128)} %get-tuple-element.146.c, bf16[2,2,1024,1024]{3,2,1,0:T(8,128)(2,1)} %collective-permute-done.24.got), custom_call_target="tpu_custom_call", output_to_operand_aliasing={{0}: (0, {}), {1}: (1, {})} | custom-call | flops 1000000 | bytes 100000 | tf_op jit(solution)/shard_map/pallas_call | solution.py:344
  885.0 3.6 all-to-all-start.7
  888.6 3.9 dynamic-slice_bitcast_fusion.2
  896.4 3.4 collective-permute-done.31
  903.7 6.4 all-to-all-done.7
  910.5 24.1 %collective-permute-done.26 = bf16[4,144,1024]{2,1,0:T(8,128)(2,1)} collective-permute-done((bf16[4,144,1024]{2,1,0:T(8,128)(2,1)}, bf16[4,144,1024]{2,1,0:T(8,128)(2,1)}, u32[]{:S(2)}, u32[]{:S(2)}) %collective-permute-start.26) | collective-permute-done | bytes 1179680 | tf_op jit(solution)/shard_map/ppermute | solution.py:552
  934.5 25.7 %collective-permute-done.28 = bf16[4,144,1024]{2,1,0:T(8,128)(2,1)} collective-permute-done((bf16[4,144,1024]{2,1,0:T(8,128)(2,1)}, bf16[4,144,1024]{2,1,0:T(8,128)(2,1)}, u32[]{:S(2)}, u32[]{:S(2)}) %collective-permute-start.28) | collective-permute-done | bytes 1179680 | tf_op jit(solution)/shard_map/ppermute | solution.py:552
  960.3 3.5 fusion.11
  966.8 24.9 %collective-permute-done.29 = bf16[2,144,1024]{2,1,0:T(8,128)(2,1)S(1)} collective-permute-done((bf16[2,144,1024]{2,1,0:T(8,128)(2,1)S(1)}, bf16[2,144,1024]{2,1,0:T(8,128)(2,1)S(1)}, u32[]{:S(2)}, u32[]{:S(2)}) %collective-permute-start.29) | collective-permute-done | bytes 589856 | tf_op jit(solution)/shard_map/ppermute | solution.py:561
  997.5 3.6 collective-permute-done.30
  (266 shorter events, 84.1 us)
Async XLA Ops:
  5.9 26.3 %all-to-all-start = ((bf16[2,8,48,1024]{3,2,0,1:T(8,128)(2,1)}), bf16[2,8,48,1024]{3,2,0,1:T(8,128)(2,1)S(1)}, u32[]{:S(2)}, u32[]{:S(2)}) async-start(bf16[2,8,48,1024]{3,2,0,1:T(8,128)(2,1)} %bitcast.197), calls=%async_computation | async-start | bytes 3145728 | tf_op jit(solution)/shard_map/all_to_all | solution.py:626
  11.8 9.5 collective-permute-start
  32.3 25.8 %collective-permute-start.1 = (bf16[2,144,1024]{2,1,0:T(8,128)(2,1)S(1)}, bf16[2,144,1024]{2,1,0:T(8,128)(2,1)S(1)}, u32[]{:S(2)}, u32[]{:S(2)}) collective-permute-start(bf16[2,144,1024]{2,1,0:T(8,128)(2,1)S(1)} %pad_maximum_fusion.4), channel_id=1, source_target_pairs={{0,2},{1,3},{2,0},{3,1},{4,6},{5,7},{6,4},{7,5},{8,10},{9,11},{10,... | collective-permute-start | bytes 1769480 | tf_op jit(solution)/shard_map/ppermute | solution.py:537
  42.4 73.2 %copy-start.19 = (bf16[1,2,1,8,48,1024]{5,4,3,2,1,0:T(8,128)(2,1)S(1)}, bf16[1,2,1,8,48,1024]{5,4,3,2,1,0:T(8,128)(2,1)}, u32[]{:S(2)}) copy-start(bf16[1,2,1,8,48,1024]{5,4,3,2,1,0:T(8,128)(2,1)} %get-tuple-element.175) | copy-start | bytes 4718596
  58.1 351.5 %collective-permute-start.11 = (bf16[4,1024,1024]{2,1,0:T(8,128)(2,1)}, bf16[4,1024,1024]{2,1,0:T(8,128)(2,1)}, u32[]{:S(2)}, u32[]{:S(2)}) collective-permute-start(bf16[4,1024,1024]{2,1,0:T(8,128)(2,1)} %pad_maximum_fusion), channel_id=1, source_target_pairs={{0,1},{1,0},{2,3},{3,2},{4,5},{5,4},{6,7},{7,6},{8,9},{9,8},{10,11... | collective-permute-start | bytes 25165832 | tf_op jit(solution)/shard_map/ppermute | solution.py:633
  58.9 30.4 %collective-permute-start.2 = (bf16[4,144,1024]{2,1,0:T(8,128)(2,1)S(1)}, bf16[4,144,1024]{2,1,0:T(8,128)(2,1)}, u32[]{:S(2)}, u32[]{:S(2)}) collective-permute-start(bf16[4,144,1024]{2,1,0:T(8,128)(2,1)S(1)} %constant_dynamic-update-slice_fusion.5.refs_0_), channel_id=1, source_target_pairs={{0,8},{4,12},{8,0},{12,4},{16,24},{20,28},{24,16},{28,20},{1,9},{5... | collective-permute-start | bytes 3538952 | tf_op jit(solution)/shard_map/ppermute | solution.py:541
  62.4 52.7 %collective-permute-start.3 = (bf16[4,144,1024]{2,1,0:T(8,128)(2,1)S(1)}, bf16[4,144,1024]{2,1,0:T(8,128)(2,1)}, u32[]{:S(2)}, u32[]{:S(2)}) collective-permute-start(bf16[4,144,1024]{2,1,0:T(8,128)(2,1)S(1)} %constant_dynamic-update-slice_fusion.5.refs_0_), channel_id=1, source_target_pairs={{0,16},{4,20},{8,24},{12,28},{16,0},{20,4},{24,8},{28,12},{1,17},{... | collective-permute-start | bytes 3538952 | tf_op jit(solution)/shard_map/ppermute | solution.py:541
  62.8 52.4 %collective-permute-start.4 = (bf16[4,144,1024]{2,1,0:T(8,128)(2,1)S(1)}, bf16[4,144,1024]{2,1,0:T(8,128)(2,1)}, u32[]{:S(2)}, u32[]{:S(2)}) collective-permute-start(bf16[4,144,1024]{2,1,0:T(8,128)(2,1)S(1)} %constant_dynamic-update-slice_fusion.5.refs_0_), channel_id=1, source_target_pairs={{0,24},{4,28},{8,16},{12,20},{16,8},{20,12},{24,0},{28,4},{1,25},{... | collective-permute-start | bytes 3538952 | tf_op jit(solution)/shard_map/ppermute | solution.py:541
  63.9 59.2 %collective-permute-start.5 = (bf16[4,144,1024]{2,1,0:T(8,128)(2,1)S(1)}, bf16[4,144,1024]{2,1,0:T(8,128)(2,1)}, u32[]{:S(2)}, u32[]{:S(2)}) collective-permute-start(bf16[4,144,1024]{2,1,0:T(8,128)(2,1)S(1)} %constant_dynamic-update-slice_fusion.5.refs_0_), channel_id=1, source_target_pairs={{0,4},{4,0},{8,12},{12,8},{16,20},{20,16},{24,28},{28,24},{1,5},{5... | collective-permute-start | bytes 3538952 | tf_op jit(solution)/shard_map/ppermute | solution.py:542
  89.3 33.8 %collective-permute-start.6 = (bf16[4,144,1024]{2,1,0:T(8,128)(2,1)}, bf16[4,144,1024]{2,1,0:T(8,128)(2,1)}, u32[]{:S(2)}, u32[]{:S(2)}) collective-permute-start(bf16[4,144,1024]{2,1,0:T(8,128)(2,1)} %collective-permute-done.2.refs_1_), channel_id=1, source_target_pairs={{0,4},{4,0},{8,12},{12,8},{16,20},{20,16},{24,28},{28,24},{1,5},{5... | collective-permute-start | bytes 3538952 | tf_op jit(solution)/shard_map/ppermute | solution.py:542
  115.1 8.0 collective-permute-start.7
  115.1 8.0 collective-permute-start.8
  117.0 47.0 %all-to-all-start.2 = ((bf16[2,8,48,1024]{3,2,0,1:T(8,128)(2,1)}), bf16[2,8,48,1024]{3,2,0,1:T(8,128)(2,1)}, u32[]{:S(2)}, u32[]{:S(2)}) async-start(bf16[2,8,48,1024]{3,2,0,1:T(8,128)(2,1)} %bitcast.222), calls=%async_computation.2 | async-start | bytes 3145728 | tf_op jit(solution)/shard_map/all_to_all | solution.py:626
  122.3 56.5 %copy-start.15 = (s32[1,512]{1,0:T(1,128)}, s32[1,512]{1,0:T(1,128)S(1)}, u32[]{:S(2)}) copy-start(s32[1,512]{1,0:T(1,128)S(1)} %get-tuple-element.209.row) | copy-start | bytes 6148
  132.7 46.0 %copy-start.12 = (f32[8,1024]{1,0:T(8,128)}, f32[8,1024]{1,0:T(8,128)S(1)}, u32[]{:S(2)}) copy-start(f32[8,1024]{1,0:T(8,128)S(1)} %stack.30.small) | copy-start | bytes 98308
  164.0 45.9 %all-to-all-start.1 = ((bf16[16,48,1024]{2,1,0:T(8,128)(2,1)}), bf16[16,48,1024]{2,1,0:T(8,128)(2,1)S(1)}, u32[]{:S(2)}, u32[]{:S(2)}) async-start(bf16[16,48,1024]{2,1,0:T(8,128)(2,1)} %bitcast.238), calls=%async_computation.1 | async-start | bytes 3145728 | tf_op jit(solution)/shard_map/all_to_all | solution.py:661
  168.5 139.0 %collective-permute-start.10 = (bf16[2,2,384,1024]{3,2,1,0:T(8,128)(2,1)}, bf16[2,2,384,1024]{3,2,1,0:T(8,128)(2,1)}, u32[]{:S(2)}, u32[]{:S(2)}) collective-permute-start(bf16[2,2,384,1024]{3,2,1,0:T(8,128)(2,1)} %bitcast.233), channel_id=1, source_target_pairs={{0,2},{1,3},{2,0},{3,1},{4,6},{5,7},{6,4},{7,5},{8,10},{9,11},{10,... | collective-permute-start | bytes 9437192 | tf_op jit(solution)/shard_map/ppermute | solution.py:632
  209.9 25.4 %all-to-all-start.3 = ((bf16[16,48,1024]{2,1,0:T(8,128)(2,1)}), bf16[16,48,1024]{2,1,0:T(8,128)(2,1)}, u32[]{:S(2)}, u32[]{:S(2)}) async-start(bf16[16,48,1024]{2,1,0:T(8,128)(2,1)} %bitcast.237), calls=%async_computation.3 | async-start | bytes 3145728 | tf_op jit(solution)/shard_map/all_to_all | solution.py:661
  221.0 188.7 %collective-permute-start.9 = (bf16[2,384,1024]{2,1,0:T(8,128)(2,1)}, bf16[2,384,1024]{2,1,0:T(8,128)(2,1)S(1)}, u32[]{:S(2)}, u32[]{:S(2)}) collective-permute-start(bf16[2,384,1024]{2,1,0:T(8,128)(2,1)} %shard_map.316.refs_0_), channel_id=1, source_target_pairs={{0,2},{1,3},{2,0},{3,1},{4,6},{5,7},{6,4},{7,5},{8,10},{9,11},{10,... | collective-permute-start | bytes 4718600 | tf_op jit(solution)/shard_map/ppermute | solution.py:666
  307.5 172.2 %collective-permute-start.17 = (bf16[2,384,1024]{2,1,0:T(8,128)(2,1)}, bf16[2,384,1024]{2,1,0:T(8,128)(2,1)S(1)}, u32[]{:S(2)}, u32[]{:S(2)}) collective-permute-start(bf16[2,384,1024]{2,1,0:T(8,128)(2,1)} %shard_map.318.refs_0_), channel_id=1, source_target_pairs={{0,2},{1,3},{2,0},{3,1},{4,6},{5,7},{6,4},{7,5},{8,10},{9,11},{10,... | collective-permute-start | bytes 4718600 | tf_op jit(solution)/shard_map/ppermute | solution.py:669
  477.8 71.8 %collective-permute-start.12 = (bf16[2,384,1024]{2,1,0:T(8,128)(2,1)}, bf16[2,384,1024]{2,1,0:T(8,128)(2,1)S(1)}, u32[]{:S(2)}, u32[]{:S(2)}) collective-permute-start(bf16[2,384,1024]{2,1,0:T(8,128)(2,1)} %get-tuple-element.101), channel_id=1, source_target_pairs={{0,2},{1,3},{2,0},{3,1},{4,6},{5,7},{6,4},{7,5},{8,10},{9,11},{10,... | collective-permute-start | bytes 4718600 | tf_op jit(solution)/shard_map/ppermute | solution.py:680
  549.6 71.0 %copy-start.31 = (bf16[2,384,1024]{2,1,0:T(8,128)(2,1)}, bf16[2,384,1024]{2,1,0:T(8,128)(2,1)S(1)}, u32[]{:S(2)}) copy-start(bf16[2,384,1024]{2,1,0:T(8,128)(2,1)S(1)} %collective-permute-done.12.gx_far) | copy-start | bytes 4718596
  549.6 71.0 %collective-permute-start.18 = (bf16[2,384,1024]{2,1,0:T(8,128)(2,1)}, bf16[2,384,1024]{2,1,0:T(8,128)(2,1)}, u32[]{:S(2)}, u32[]{:S(2)}) collective-permute-start(bf16[2,384,1024]{2,1,0:T(8,128)(2,1)} %get-tuple-element.125), channel_id=1, source_target_pairs={{0,2},{1,3},{2,0},{3,1},{4,6},{5,7},{6,4},{7,5},{8,10},{9,11},{10,... | collective-permute-start | bytes 4718600 | tf_op jit(solution)/shard_map/ppermute | solution.py:682
  620.6 248.9 %collective-permute-start.24 = (bf16[2,2,1024,1024]{3,2,1,0:T(8,128)(2,1)}, bf16[2,2,1024,1024]{3,2,1,0:T(8,128)(2,1)}, u32[]{:S(2)}, u32[]{:S(2)}) collective-permute-start(bf16[2,2,1024,1024]{3,2,1,0:T(8,128)(2,1)} %get-tuple-element.148), channel_id=1, source_target_pairs={{0,1},{1,0},{2,3},{3,2},{4,5},{5,4},{6,7},{7,6},{8,9},{9,8},{10,11... | collective-permute-start | bytes 25165832 | tf_op jit(solution)/shard_map/ppermute | solution.py:684
  631.4 24.6 %all-to-all-start.4 = ((bf16[2,8,48,1024]{3,2,0,1:T(8,128)(2,1)}), bf16[2,8,48,1024]{3,2,0,1:T(8,128)(2,1)S(1)}, u32[]{:S(2)}, u32[]{:S(2)}) async-start(bf16[2,8,48,1024]{3,2,0,1:T(8,128)(2,1)} %copy.131), calls=%async_computation.4 | async-start | bytes 3145728 | tf_op jit(solution)/shard_map/all_to_all | solution.py:694
  657.1 58.0 %all-to-all-start.5 = ((bf16[2,8,48,1024]{3,2,0,1:T(8,128)(2,1)}), bf16[2,8,48,1024]{3,2,0,1:T(8,128)(2,1)S(1)}, u32[]{:S(2)}, u32[]{:S(2)}) async-start(bf16[2,8,48,1024]{3,2,0,1:T(8,128)(2,1)} %copy.136), calls=%async_computation.5 | async-start | bytes 3145728 | tf_op jit(solution)/shard_map/all_to_all | solution.py:694
  660.9 46.6 %copy-start.32 = (bf16[2,384,1024]{2,1,0:T(8,128)(2,1)S(1)}, bf16[2,384,1024]{2,1,0:T(8,128)(2,1)}, u32[]{:S(2)}) copy-start(bf16[2,384,1024]{2,1,0:T(8,128)(2,1)} %get-tuple-element.151) | copy-start | bytes 4718596
  706.9 6.7 collective-permute-start.13
  707.3 54.8 %collective-permute-start.14 = (bf16[16,32,1024]{2,1,0:T(8,128)(2,1)}, bf16[16,32,1024]{2,1,0:T(8,128)(2,1)}, u32[]{:S(2)}, u32[]{:S(2)}) collective-permute-start(bf16[16,32,1024]{2,1,0:T(8,128)(2,1)} %get-tuple-element.114), channel_id=1, source_target_pairs={{0,4},{4,0},{8,12},{12,8},{16,20},{20,16},{24,28},{28,24},{1,5},{5... | collective-permute-start | bytes 3145736 | tf_op jit(solution)/shard_map/ppermute | solution.py:707
  710.8 174.2 %collective-permute-start.25 = (bf16[2,2,384,1024]{3,2,1,0:T(8,128)(2,1)}, bf16[2,2,384,1024]{3,2,1,0:T(8,128)(2,1)}, u32[]{:S(2)}, u32[]{:S(2)}) collective-permute-start(bf16[2,2,384,1024]{3,2,1,0:T(8,128)(2,1)} %pad_maximum_fusion.1), channel_id=1, source_target_pairs={{0,2},{1,3},{2,0},{3,1},{4,6},{5,7},{6,4},{7,5},{8,10},{9,11},{10,... | collective-permute-start | bytes 9437192 | tf_op jit(solution)/shard_map/ppermute | solution.py:685
  713.6 55.7 %collective-permute-start.15 = (bf16[16,32,1024]{2,1,0:T(8,128)(2,1)}, bf16[16,32,1024]{2,1,0:T(8,128)(2,1)S(1)}, u32[]{:S(2)}, u32[]{:S(2)}) collective-permute-start(bf16[16,32,1024]{2,1,0:T(8,128)(2,1)} %get-tuple-element.115), channel_id=1, source_target_pairs={{0,4},{4,0},{8,12},{12,8},{16,20},{20,16},{24,28},{28,24},{1,5},{5... | collective-permute-start | bytes 3145736 | tf_op jit(solution)/shard_map/ppermute | solution.py:707
  714.6 55.2 %collective-permute-start.16 = (bf16[16,32,1024]{2,1,0:T(8,128)(2,1)}, bf16[16,32,1024]{2,1,0:T(8,128)(2,1)}, u32[]{:S(2)}, u32[]{:S(2)}) collective-permute-start(bf16[16,32,1024]{2,1,0:T(8,128)(2,1)} %get-tuple-element.116), channel_id=1, source_target_pairs={{0,4},{4,0},{8,12},{12,8},{16,20},{20,16},{24,28},{28,24},{1,5},{5... | collective-permute-start | bytes 3145736 | tf_op jit(solution)/shard_map/ppermute | solution.py:707
  762.1 9.0 collective-permute-start.19
  762.2 122.8 %all-to-all-start.6 = ((bf16[16,48,1024]{2,1,0:T(8,128)(2,1)}), bf16[16,48,1024]{2,1,0:T(8,128)(2,1)S(1)}, u32[]{:S(2)}, u32[]{:S(2)}) async-start(bf16[16,48,1024]{2,1,0:T(8,128)(2,1)} %bitcast.60), calls=%async_computation.6 | async-start | bytes 3145728 | tf_op jit(solution)/shard_map/all_to_all | solution.py:700
  769.2 1.5 collective-permute-start.23
  769.8 3.0 collective-permute-start.20
  770.7 3.6 collective-permute-start.21
  771.1 4.7 collective-permute-start.22
  885.0 25.1 %all-to-all-start.7 = ((bf16[16,48,1024]{2,1,0:T(8,128)(2,1)}), bf16[16,48,1024]{2,1,0:T(8,128)(2,1)S(1)}, u32[]{:S(2)}, u32[]{:S(2)}) async-start(bf16[16,48,1024]{2,1,0:T(8,128)(2,1)} %bitcast.236), calls=%async_computation.7 | async-start | bytes 3145728 | tf_op jit(solution)/shard_map/all_to_all | solution.py:700
  892.5 42.0 %collective-permute-start.26 = (bf16[4,144,1024]{2,1,0:T(8,128)(2,1)}, bf16[4,144,1024]{2,1,0:T(8,128)(2,1)}, u32[]{:S(2)}, u32[]{:S(2)}) collective-permute-start(bf16[4,144,1024]{2,1,0:T(8,128)(2,1)} %get-tuple-element.165), channel_id=1, source_target_pairs={{0,8},{4,12},{8,0},{12,4},{16,24},{20,28},{24,16},{28,20},{1,9},{5... | collective-permute-start | bytes 3538952 | tf_op jit(solution)/shard_map/ppermute | solution.py:552
  894.4 40.1 %collective-permute-start.27 = (bf16[4,144,1024]{2,1,0:T(8,128)(2,1)}, bf16[4,144,1024]{2,1,0:T(8,128)(2,1)}, u32[]{:S(2)}, u32[]{:S(2)}) collective-permute-start(bf16[4,144,1024]{2,1,0:T(8,128)(2,1)} %get-tuple-element.167), channel_id=1, source_target_pairs={{0,16},{4,20},{8,24},{12,28},{16,0},{20,4},{24,8},{28,12},{1,17},{... | collective-permute-start | bytes 3538952 | tf_op jit(solution)/shard_map/ppermute | solution.py:552
  895.9 64.4 %collective-permute-start.28 = (bf16[4,144,1024]{2,1,0:T(8,128)(2,1)}, bf16[4,144,1024]{2,1,0:T(8,128)(2,1)}, u32[]{:S(2)}, u32[]{:S(2)}) collective-permute-start(bf16[4,144,1024]{2,1,0:T(8,128)(2,1)} %get-tuple-element.166), channel_id=1, source_target_pairs={{0,24},{4,28},{8,16},{12,20},{16,8},{20,12},{24,0},{28,4},{1,25},{... | collective-permute-start | bytes 3538952 | tf_op jit(solution)/shard_map/ppermute | solution.py:552
  896.0 3.8 collective-permute-start.31
  963.8 27.9 %collective-permute-start.29 = (bf16[2,144,1024]{2,1,0:T(8,128)(2,1)S(1)}, bf16[2,144,1024]{2,1,0:T(8,128)(2,1)S(1)}, u32[]{:S(2)}, u32[]{:S(2)}) collective-permute-start(bf16[2,144,1024]{2,1,0:T(8,128)(2,1)S(1)} %fusion.12), channel_id=1, source_target_pairs={{0,2},{1,3},{2,0},{3,1},{4,6},{5,7},{6,4},{7,5},{8,10},{9,11},{10,... | collective-permute-start | bytes 1769480 | tf_op jit(solution)/shard_map/ppermute | solution.py:561
  964.8 27.3 %copy-start.21 = (bf16[2,8,48,1024]{3,2,1,0:T(8,128)(2,1)S(1)}, bf16[2,8,48,1024]{3,2,1,0:T(8,128)(2,1)}, u32[]{:S(2)}) copy-start(bf16[2,8,48,1024]{3,2,1,0:T(8,128)(2,1)} %copy.121) | copy-start | bytes 4718596
  964.8 27.3 %copy-start.22 = (bf16[2,8,48,1024]{3,2,1,0:T(8,128)(2,1)S(1)}, bf16[2,8,48,1024]{3,2,1,0:T(8,128)(2,1)}, u32[]{:S(2)}) copy-start(bf16[2,8,48,1024]{3,2,1,0:T(8,128)(2,1)} %copy.126) | copy-start | bytes 4718596
  964.9 27.3 %copy-start.29 = (bf16[2,384,1024]{2,1,0:T(8,128)(2,1)S(1)}, bf16[2,384,1024]{2,1,0:T(8,128)(2,1)}, u32[]{:S(2)}) copy-start(bf16[2,384,1024]{2,1,0:T(8,128)(2,1)} %get-tuple-element.99) | copy-start | bytes 4718596
  992.0 9.0 collective-permute-start.30
  (49 other events, 300.9 us)

commit v3 on v2

--- a/solution.py
+++ b/solution.py
@@ -307,27 +307,72 @@
     )(jnp.stack([ex, fi]).astype(jnp.int32).reshape(1, 2), *pieces)
 
 
-def add_dense_kernel(*refs):
-    terms, vector, out = refs[:-2], refs[-2], refs[-1]
+def rows_of(blocks):
+    return blocks.reshape(-1, blocks.shape[-1])
+
+
+def add_dense_kernel(groups, place, *refs):
+    chips = refs[0].shape[0] // groups
+    outs, (sums, got), terms = refs[-chips:], refs[-chips - 2 : -chips], refs[: -chips - 2]
     share = terms[0].shape[1]
-    for m in range(4):
-        total = sum(ref[...].astype(F32) for ref in terms[m::4])
-        out[:, m * share : (m + 1) * share, :] = total.astype(BF)
-    out[:, 4 * share :, :] = vector[...].astype(BF)
-
-
-def add_dense(terms, vector):
+    small = sums[...] + got[...]
+    for k, out in enumerate(outs):
+        owner = jnp.bitwise_xor(place[0, 0], k) * groups
+        for f in range(groups):
+            for m in range(4):
+                total = sum(ref[owner + f].astype(F32) for ref in terms[m::4])
+                at = (f * 4 + m) * share
+                out[at : at + share, :] = total.astype(BF)
+        out[groups * 4 * share :, :] = jnp.concatenate([small, jnp.zeros_like(small)]).astype(BF)
+
+
+def add_dense(terms, sums, sums_got, chip, groups):
     count, share, width = terms[0].shape
-    lines = vector.shape[1]
-    block = pl.BlockSpec((2, share, width), lambda o: (o, 0, 0))
+    vm = pl.BlockSpec(memory_space=pltpu.VMEM)
+    out = jax.ShapeDtypeStruct((groups * 4 * share + 16, width), BF)
     return pl.pallas_call(
-        add_dense_kernel,
-        grid=(count // 2,),
-        in_specs=[block] * len(terms) + [pl.BlockSpec((2, lines, width), lambda o: (o, 0, 0))],
-        out_specs=pl.BlockSpec((2, 4 * share + lines, width), lambda o: (o, 0, 0)),
-        out_shape=jax.ShapeDtypeStruct((count, 4 * share + lines, width), BF),
+        functools.partial(add_dense_kernel, groups),
+        in_specs=[pl.BlockSpec(memory_space=pltpu.SMEM)] + [vm] * (len(terms) + 2),
+        out_specs=[vm] * (count // groups),
+        out_shape=[out] * (count // groups),
+        compiler_params=pltpu.CompilerParams(vmem_limit_bytes=48 << 20),
         cost_estimate=LIGHT,
-    )(*terms, vector)
+    )(chip.reshape(1, 1), *terms, sums, sums_got)
+
+
+def add_plane_kernel(side, first, *refs):
+    got, (keep, give, sums) = refs[:-3], refs[-3:]
+    half = keep.shape[0]
+
+    def total(at, n):
+        at = at if isinstance(at, int) else pl.multiple_of(at, 16)
+        return sum((ref[pl.ds(at, n), :].astype(F32) for ref in got), first[pl.ds(at, n), :].astype(F32))
+
+    step = 128 if half % 128 == 0 else half
+    for at in range(0, half, step):
+        keep[at : at + step, :] = total(side[0, 0] * half + at, step)
+        give[at : at + step, :] = total((1 - side[0, 0]) * half + at, step).astype(BF)
+    small = total(2 * half, 16)
+    sums[...] = small
+    give[half:, :] = small.astype(BF)
+
+
+def add_plane(side, first, got):
+    lines, width = first.shape
+    half = (lines - 16) // 2
+    vm = pl.BlockSpec(memory_space=pltpu.VMEM)
+    return pl.pallas_call(
+        add_plane_kernel,
+        in_specs=[pl.BlockSpec(memory_space=pltpu.SMEM)] + [vm] * (1 + len(got)),
+        out_specs=[vm] * 3,
+        out_shape=[
+            jax.ShapeDtypeStruct((half, width), F32),
+            jax.ShapeDtypeStruct((half + 16, width), BF),
+            jax.ShapeDtypeStruct((16, width), F32),
+        ],
+        compiler_params=pltpu.CompilerParams(vmem_limit_bytes=48 << 20),
+        cost_estimate=LIGHT,
+    )(side.reshape(1, 1), first, *got)
 
 
 def add_near_kernel(a, c, got, out_in, out_out):
@@ -352,58 +397,71 @@
     )(dwi_own, dwo_own, got)
 
 
+def side_of(array, place):
+    return place[0] if array.shape[0] > 1 else 0
+
+
 def mixed_norm_kernel(rows, back, gain, shift, out):
-    normal, _ = normal_of(rows[0].astype(F32) + back[0].astype(F32))
+    normal, _ = normal_of(rows[0, 0].astype(F32) + back[0].astype(F32))
     out[0] = (normal * gain[...] + shift[...]).astype(BF)
 
 
-def mixed_norm(rows, back, gain, shift):
-    le, n, width = rows.shape
+def mixed_norm(t, rows, back, gain, shift):
+    le, n, width = back.shape
     block = pl.BlockSpec((1, 128, width), lambda j, c: (j, c, 0))
     line = pl.BlockSpec((1, width), lambda j, c: (0, 0))
     return pl.pallas_call(
         mixed_norm_kernel,
         grid=(le, n // 128),
-        in_specs=[block, block, line, line],
+        in_specs=[pl.BlockSpec((1, 1, 128, width), lambda j, c: (t, j, c, 0)), block, line, line],
         out_specs=block,
         out_shape=jax.ShapeDtypeStruct((le, n, width), BF),
         cost_estimate=LIGHT,
     )(rows, back, gain, shift)
 
 
-def mixed_back_kernel(rows, back, gx, gx_far, cot, fill, gain, exact, low, sums):
+def mixed_back_kernel(_, rows, back, gx, gx_far, cot, fill, gain, exact, low, sums):
     @pl.when((pl.program_id(0) == 0) & (pl.program_id(1) == 0))
     def _():
         sums[...] = jnp.zeros_like(sums)
 
-    normal, inverse = normal_of(rows[0].astype(F32) + back[0].astype(F32))
-    g = gx[0].astype(F32) + gx_far[0].astype(F32)
+    normal, inverse = normal_of(rows[0, 0].astype(F32) + back[0].astype(F32))
+    g = gx[0].astype(F32) + gx_far[0, 0].astype(F32)
     sums[0:1, :] += jnp.sum(g * normal, axis=0, keepdims=True)
     sums[1:2, :] += jnp.sum(g, axis=0, keepdims=True)
     u = g * gain[...]
-    total = cot[0].astype(F32) * fill[0] + inverse * (
+    total = cot[0, 0].astype(F32) * fill[0] + inverse * (
         u - jnp.mean(u, axis=-1, keepdims=True) - normal * jnp.mean(u * normal, axis=-1, keepdims=True)
     )
     exact[0] = total
     low[0] = total.astype(BF)
 
 
-def mixed_back(rows, back, gx, gx_far, cot, fill, gain):
-    le, n, width = rows.shape
-    block = pl.BlockSpec((1, 128, width), lambda j, c: (j, c, 0))
-    mark = pl.BlockSpec((1, 128, 1), lambda j, c: (j, c, 0))
+def mixed_back(t, other, rows, back, gx, gx_far, cot, fill, gain):
+    le, n, width = back.shape
+    block = pl.BlockSpec((1, 128, width), lambda j, c, s: (j, c, 0))
+    whole = pl.BlockSpec((1, 1, 128, width), lambda j, c, s: (t, j, c, 0))
     return pl.pallas_call(
         mixed_back_kernel,
-        grid=(le, n // 128),
-        in_specs=[block] * 5 + [mark, pl.BlockSpec((1, width), lambda j, c: (0, 0))],
-        out_specs=[block, block, pl.BlockSpec((8, width), lambda j, c: (0, 0))],
+        grid_spec=pltpu.PrefetchScalarGridSpec(
+            num_scalar_prefetch=1,
+            grid=(le, n // 128),
+            in_specs=[
+                whole, block, block,
+                pl.BlockSpec((1, 1, 128, width), lambda j, c, s: (side_of(gx_far, s), j, c, 0)),
+                whole,
+                pl.BlockSpec((1, 128, 1), lambda j, c, s: (j, c, 0)),
+                pl.BlockSpec((1, width), lambda j, c, s: (0, 0)),
+            ],
+            out_specs=[block, block, pl.BlockSpec((8, width), lambda j, c, s: (0, 0))],
+        ),
         out_shape=[
             jax.ShapeDtypeStruct((le, n, width), F32),
             jax.ShapeDtypeStruct((le, n, width), BF),
             jax.ShapeDtypeStruct((8, width), F32),
         ],
         cost_estimate=LIGHT,
-    )(rows, back, gx, gx_far, cot, fill, gain)
+    )(other, rows, back, gx, gx_far, cot, fill, gain)
 
 
 def gelu_parts(v):
@@ -415,7 +473,7 @@
     return v * half, slope
 
 
-def expert_kernel(first, tiles, *refs):
+def expert_kernel(first, tiles, _, *refs):
     (x_own, x_far, g_own, g_far, fill_own, fill_far, wi_own, wi_near, wo_own, wo_near, bias) = refs[:11]
     before = [None] * 5 if first else refs[11:16]
     (out_own, out_far, gx_own, gx_far, dwi_own, dwo_own, dw_near, db, dbo,
@@ -426,13 +484,15 @@
     @pl.when(h == 0)
     def _():
         xs[:rows, :] = x_own[0]
-        xs[rows:, :] = x_far[0]
+        xs[rows:, :] = x_far[0, 0]
         total = None
-        for start, ref, fill in ((0, g_own, fill_own), (rows, g_far, fill_far)):
-            g = ref[0].astype(F32) * fill[0]
+        for start, ref, fill in ((0, g_own[0, 0], fill_own), (rows, g_far[0, 0, 0], fill_far)):
+            g = ref.astype(F32) * fill[0]
             gs[start : start + rows, :] = g.astype(BF)
             part = jnp.sum(g, axis=0, keepdims=True)
             total = part if total is None else total + part
+        out_sum[...] = jnp.zeros_like(out_sum)
+        gx_sum[...] = jnp.zeros_like(gx_sum)
         dbo[0] = total if first else total + before[4][0]
 
     def tile_step(wi, wo, mine):
@@ -441,8 +501,8 @@
         act, slope = gelu_parts(inner)
         act = act.astype(BF)
         grad_inner = (dot(g, wo, NT) * slope).astype(BF)
-        out = dot(act, wo, NN)
-        gx = dot(grad_inner, wi, NT)
+        out_sum[...] += dot(act, wo, NN)
+        gx_sum[...] += dot(grad_inner, wi, NT)
         dwi = dot(x, grad_inner, TN) if mine else dot(grad_inner, x, TN)
         dwo = dot(act, g, TN)
         column = jnp.sum(grad_inner.astype(F32), axis=0, keepdims=True)
@@ -450,19 +510,9 @@
             dwi_own[0] = dwi if first else dwi + before[0][0]
             dwo_own[0] = dwo if first else dwo + before[1][0]
         else:
-            dw_near[0, 0] = (dwi if first else dwi + before[2][0, 0]).astype(dw_near.dtype)
-            dw_near[0, 1] = (dwo if first else dwo + before[2][0, 1]).astype(dw_near.dtype)
+            dw_near[0, 0] = (dwi if first else dwi + before[2][0, 0].astype(F32)).astype(dw_near.dtype)
+            dw_near[0, 1] = (dwo if first else dwo + before[2][0, 1].astype(F32)).astype(dw_near.dtype)
         db[0] = column if first else column + before[3][0]
-
-        @pl.when(h == 0)
-        def _():
-            out_sum[...] = out
-            gx_sum[...] = gx
-
-        @pl.when(h != 0)
-        def _():
-            out_sum[...] += out
-            gx_sum[...] += gx
 
     @pl.when(h < tiles)
     def _():
@@ -480,43 +530,64 @@
         gx_far[0] = gx_sum[rows:, :].astype(BF)
 
 
-def expert_step(x_own, x_far, g_own, g_far, fills, wi_own, wo_own, w_near, bias, before, tile=256):
+def expert_step(t, other, x_own, x_far, g_own, g_far, fills, wi_own, wo_own, w_near, bias, before, tile=512):
     le, rows, width = x_own.shape
     hidden = wi_own.shape[2]
     tiles = hidden // tile
     first = before is None
-    row = pl.BlockSpec((1, rows, width), lambda j, h: (j, 0, 0))
-    mark = pl.BlockSpec((1, rows, 1), lambda j, h: (j, 0, 0))
-    own_in = pl.BlockSpec((1, width, tile), lambda j, h: (j, 0, jnp.minimum(h, tiles - 1)))
-    near_in = pl.BlockSpec((1, width, tile), lambda j, h: (j, 0, jnp.maximum(h - tiles, 0)))
-    own_out = pl.BlockSpec((1, tile, width), lambda j, h: (j, jnp.minimum(h, tiles - 1), 0))
-    near_out = pl.BlockSpec((1, tile, width), lambda j, h: (le + j, jnp.maximum(h - tiles, 0), 0))
-    near_grads = pl.BlockSpec((1, 2, tile, width), lambda j, h: (j, 0, jnp.maximum(h - tiles, 0), 0))
-    column = pl.BlockSpec((1, 1, tile), lambda j, h: (j, 0, h))
-    line = pl.BlockSpec((1, 1, width), lambda j, h: (j, 0, 0))
+    mode = None if first else pl.Buffered(1)
+    out_row = pl.BlockSpec((1, rows, width), lambda j, h, s: (j, 0, 0))
+    mark = pl.BlockSpec((1, rows, 1), lambda j, h, s: (j, 0, 0), pipeline_mode=mode)
+    own = lambda h: jnp.minimum(h, tiles - 1)
+    near = lambda h: jnp.maximum(h - tiles, 0)
     shapes = [jax.ShapeDtypeStruct((le, rows, width), BF)] * 4 + [
         jax.ShapeDtypeStruct((le, width, hidden), F32),
         jax.ShapeDtypeStruct((le, hidden, width), F32),
-        jax.ShapeDtypeStruct((le, 2, hidden, width), F32 if first else BF),
+        jax.ShapeDtypeStruct((le, 2, hidden, width), BF),
         jax.ShapeDtypeStruct((le, 1, 2 * hidden), F32),
         jax.ShapeDtypeStruct((le, 1, width), F32),
     ]
-    grads = [own_in, own_out, near_grads, column, line]
+    own_in = pl.BlockSpec((1, width, tile), lambda j, h, s: (j, 0, own(h)))
+    own_out = pl.BlockSpec((1, tile, width), lambda j, h, s: (j, own(h), 0))
+    column = pl.BlockSpec((1, 1, tile), lambda j, h, s: (j, 0, h))
+    grads = [
+        own_in,
+        own_out,
+        pl.BlockSpec((1, 2, tile, width), lambda j, h, s: (j, 0, near(h), 0)),
+        column,
+        pl.BlockSpec((1, 1, width), lambda j, h, s: (j, 0, 0)),
+    ]
     operands = [x_own, x_far, g_own, g_far, *fills, wi_own, w_near, wo_own, w_near, bias]
-    in_specs = [row] * 4 + [mark] * 2 + [own_in, near_in, own_out, near_out, column]
+    in_specs = [
+        pl.BlockSpec((1, rows, width), lambda j, h, s: (j, 0, 0), pipeline_mode=mode),
+        pl.BlockSpec((1, 1, rows, width), lambda j, h, s: (side_of(x_far, s), j, 0, 0), pipeline_mode=mode),
+        pl.BlockSpec((1, 1, rows, width), lambda j, h, s: (t, j, 0, 0), pipeline_mode=mode),
+        pl.BlockSpec((1, 1, 1, rows, width), lambda j, h, s: (side_of(g_far, s), t, j, 0, 0), pipeline_mode=mode),
+        mark,
+        mark,
+        own_in,
+        pl.BlockSpec((1, width, tile), lambda j, h, s: (j, 0, near(h))),
+        own_out,
+        pl.BlockSpec((1, tile, width), lambda j, h, s: (le + j, near(h), 0)),
+        column,
+    ]
     if not first:
         operands += list(before)
-        in_specs += grads
+        near_before = pl.BlockSpec((1, 2, tile, width), lambda j, h, s: (j, 0, near(h), 0), pipeline_mode=mode)
+        in_specs += grads[:2] + [near_before] + grads[3:]
     return pl.pallas_call(
         functools.partial(expert_kernel, first, tiles),
-        grid=(le, 2 * tiles),
-        in_specs=in_specs,
-        out_specs=[row] * 4 + grads,
+        grid_spec=pltpu.PrefetchScalarGridSpec(
+            num_scalar_prefetch=1,
+            grid=(le, 2 * tiles),
+            in_specs=in_specs,
+            out_specs=[out_row] * 4 + grads,
+            scratch_shapes=[pltpu.VMEM((2 * rows, width), BF)] * 2 + [pltpu.VMEM((2 * rows, width), F32)] * 2,
+        ),
         out_shape=shapes,
-        scratch_shapes=[pltpu.VMEM((2 * rows, width), BF)] * 2 + [pltpu.VMEM((2 * rows, width), F32)] * 2,
         compiler_params=pltpu.CompilerParams(vmem_limit_bytes=60 << 20),
         cost_estimate=LIGHT,
-    )(*operands)
+    )(other, *operands)
 
 
 def pick(array, index, dim):
@@ -529,6 +600,11 @@
 
 def crossed(n, step):
     return [(i, i ^ step) for i in range(n)]
+
+
+def both_groups(array, n_f):
+    pairs = [[i, i ^ 2] for i in range(n_f) if not i & 2]
+    return lax.all_gather(array, "fsdp", axis_index_groups=pairs)
 
 
 def gather_all(shard, first, n_exp, n_f, ex, fi, share):
@@ -541,27 +617,6 @@
     pieces = [block] + [lax.ppermute(block, "exp", crossed(n_exp, 2 * k)) for k in range(1, n_exp // 2)]
     pieces += [lax.ppermute(piece, "exp", crossed(n_exp, 1)) for piece in pieces]
     return block, place_rows(pieces, ex, fi, share)
-
-
-def reduce_plane(low, n_exp, chip):
-    chips = n_exp // 2
-    view = low.reshape(chips, -1, low.shape[1], low.shape[2])
-    total = pick(view, chip, 0).astype(F32)
-    for step in range(1, chips):
-        block = pick(view, chip ^ step, 0)
-        total = total + lax.ppermute(block, "exp", crossed(n_exp, 2 * step)).astype(F32)
-    return total
-
-
-def reduce_groups(total, n_f, fi):
-    half = n_f // 2
-    while half >= 1:
-        pairs = total.reshape(2, half, *total.shape[1:])
-        side = (fi // half) % 2
-        got = lax.ppermute(pick(pairs, 1 - side, 0).astype(BF), "fsdp", crossed(n_f, half))
-        total = pick(pairs, side, 0) + got.astype(F32)
-        half //= 2
-    return total[0]
 
 
 def body(
@@ -629,7 +684,8 @@
     ready, (dense_full, table) = gather_all(shipped, arrived_all[0], n_exp, n_f, ex, fi, share)
     table = table.reshape(owners, -1).astype(F32)
     cot = out_cotangent[:, :, 0].reshape(mb, le, rows, width)
-    cot_far = lax.ppermute(after(cot, ready), "fsdp", far)
+    other = (1 - (fi // 2) % 2).astype(jnp.int32).reshape(1)
+    cot_far = both_groups(after(cot, ready), n_f)
     w_near = lax.ppermute(after(jnp.concatenate([expert_in, expert_out]), ready), "fsdp", near)
     block_rows = block_input[:, :, 0].reshape(mb, le, rows, width)
 
@@ -662,34 +718,38 @@
                 placed.reshape(experts, cap, width), "exp", split_axis=0, concat_axis=1, tiled=True
             ).reshape(le, rows, width)
         )
-        normed_two.append(mixed_norm(block_rows[t], back_rows[t], small[5:6], small[6:7]))
-    normed_far = [lax.ppermute(normed_two[0], "fsdp", far)]
+        normed_two.append(mixed_norm(t, block_rows, back_rows[t], small[5:6], small[6:7]))
+    normed_far = [lax.ppermute(normed_two[0], "fsdp", far)[None]]
     for t in range(1, mb):
         rows_sent, cot_far = lax.optimization_barrier((normed_two[t], cot_far))
-        normed_far.append(lax.ppermute(rows_sent, "fsdp", far))
+        normed_far.append(lax.ppermute(rows_sent, "fsdp", far)[None])
 
     ffn, before = [], None
     for t in range(mb):
         ffn.append(
             expert_step(
-                normed_two[t], normed_far[t], cot[t], cot_far[t], (fill_own[t], fill_far[t]),
+                t, other, normed_two[t], normed_far[t], cot, cot_far, (fill_own[t], fill_far[t]),
                 expert_in, expert_out, w_near, bias_in, before,
             )
         )
         before = ffn[t][4:]
-    gx_far = [lax.ppermute(ffn[0][3], "fsdp", far)]
+    gx_far = [lax.ppermute(ffn[0][3], "fsdp", far)[None]]
     for t in range(1, mb):
-        gx_far.append(lax.ppermute(after(ffn[t][3], gx_far[t - 1]), "fsdp", far))
+        gx_far.append(both_groups(after(ffn[t][3], gx_far[t - 1]), n_f))
     dwi_own, dwo_own, dw_near, db, dbo = before
-    dw_got = lax.ppermute(after(dw_near, gx_far[mb - 1]), "fsdp", near)
-    out_far = lax.ppermute(after(jnp.stack([ffn[t][1] for t in range(mb)]), gx_far[mb - 1]), "fsdp", far)
     dbo = dbo[:, 0]
-    vectors = lax.ppermute(jnp.concatenate([db[:, 0, hidden:], dbo], axis=1), "fsdp", near)
-
+    vectors = jnp.concatenate([db[:, 0, hidden:], dbo], axis=1)
+
+    dw_got = lax.ppermute(dw_near, "fsdp", near)
     input_grads, terms, small_total = [], [], None
     for t in range(mb):
+        got = gx_far[t]
+        if t == mb - 1:
+            outs = jnp.stack([ffn[i][1] for i in range(mb)])
+            got, outs, placed_back = lax.optimization_barrier((got, outs, placed_back))
+            out_far = both_groups(outs, n_f)
         grad_mixed, to_send, norm_sums = mixed_back(
-            block_rows[t], back_rows[t], ffn[t][2], gx_far[t], cot[t], fill_own[t], small[5:6]
+            t, other, block_rows, back_rows[t], ffn[t][2], got, cot, fill_own[t], small[5:6]
         )
         grad_arrived = lax.all_to_all(
             to_send.reshape(le, sources, cap, width), "exp", split_axis=1, concat_axis=0, tiled=True
@@ -703,34 +763,45 @@
         input_grads.append(
             (grad_mixed + returned.astype(F32)).astype(BF).reshape(le, 1, sources, cap, width)
         )
-        sums = jnp.concatenate([sums[:5], norm_sums[:2]])
+        sums = jnp.concatenate([sums[:5], norm_sums[:2], norm_sums[7:]])
         terms += list(keep) + [lax.ppermute(part, "exp", crossed(n_exp, 1)) for part in give]
         small_total = sums if t == 0 else small_total + sums
 
-    vector = small_total.reshape(7, owners, share).transpose(1, 0, 2).reshape(owners, 7 * share)
-    vector = jnp.pad(vector, ((0, 0), (0, width - 7 * share)))[:, None, :]
-    vector = vector.reshape(n_exp // 2, 2, n_f, 1, width)
-    vector = pick(vector, core, 1) + lax.ppermute(pick(vector, 1 - core, 1), "exp", crossed(n_exp, 1))
-    vector = jnp.pad(vector.reshape(owners // 2, 1, width), ((0, 0), (0, 15), (0, 0)))
-    grad_in, grad_out = add_near(dwi_own, dwo_own, dw_got)
-    low, grad_in, grad_out, out_far = lax.optimization_barrier((add_dense(terms, vector), grad_in, grad_out, out_far))
-    total = reduce_groups(reduce_plane(low, n_exp, chip), n_f, fi)
-    dense = total[: 4 * share].reshape(4, share, width)
-    smalls = total[4 * share, : 7 * share].reshape(7, share)
-
+    sums_got = lax.ppermute(small_total, "exp", crossed(n_exp, 1))
+    blocks = add_dense(terms, small_total, sums_got, chip, n_f)
+    got = [lax.ppermute(blocks[k], "exp", crossed(n_exp, 2 * k)) for k in range(1, n_exp // 2)]
+    keep, give, sums = add_plane((fi // 2) % 2, blocks[0], got)
+    far_got = lax.ppermute(give, "fsdp", far)
     outputs = []
+    far_outs = pick(out_far, other[0], 0)
     for t in range(mb):
         mixed = block_rows[t].astype(F32) + back_rows[t].astype(F32)
-        ffn_out = ffn[t][0].astype(F32) + out_far[t].astype(F32) + bias_out[:, None, :]
+        ffn_out = ffn[t][0].astype(F32) + far_outs[t].astype(F32) + bias_out[:, None, :]
         outputs.append(
             ((mixed + ffn_out) * fill_own[t]).astype(BF).reshape(le, 1, sources, cap, width)
         )
-    grad_in_bias = db[:, 0, :hidden] + vectors[:, :hidden]
+    outputs = jnp.stack(outputs)
+    half = keep.shape[0]
+    keep = keep + far_got[:half].astype(F32)
+    sums = sums + far_got[half:].astype(F32)
+    pairs = keep.reshape(2, 4 * share, width)
+    ride = jnp.pad(vectors, ((0, 0), (0, -vectors.shape[1] % width))).reshape(-1, width)
+    give = jnp.concatenate([pick(pairs, 1 - fi % 2, 0), sums, ride]).astype(BF)
+    give, outputs = lax.optimization_barrier((give, outputs))
+    near_got = lax.ppermute(give, "fsdp", near).astype(F32)
+    total = pick(pairs, fi % 2, 0) + near_got[: 4 * share]
+    sums = sums + near_got[4 * share : 4 * share + 16]
+    vectors_got = near_got[4 * share + 16 :].reshape(le, -1)[:, : vectors.shape[1]]
+    grad_in, grad_out = add_near(dwi_own, dwo_own, dw_got)
+    dense = total.reshape(4, share, width)
+    smalls = lax.dynamic_slice_in_dim(sums, (ex * n_f + fi) * share, share, 1)
+
+    grad_in_bias = db[:, 0, :hidden] + vectors_got[:, :hidden]
     grad_out_bias = lax.dynamic_slice_in_dim(
-        dbo + vectors[:, hidden:], fi * (width // n_f), width // n_f, 1
+        dbo + vectors_got[:, hidden:], fi * (width // n_f), width // n_f, 1
     )
     return (
-        jnp.stack(outputs),
+        outputs,
         jnp.stack(input_grads),
         smalls[0],
         smalls[1],

time: 1010 us -> 874 us (0.87)
  waiting for transfers between devices: 508 us -> 346 us
  between operations: 1.98 us -> 15.2 us
  other arithmetic: 26.1 us -> 36.3 us
    ppermute x14 -> x10, waiting for transfers between devices: 393 us -> 172 us  [the longest x1 99 us: body(): normed_far = [lax.ppermute(normed_two[0], 'fsdp', far)[None]]]
    ppermute x1, waiting for transfers between devices: 0.01 us -> 33.5 us  [body(): lax.ppermute(after(jnp.concatenate([expert_in, expert_out]), ready), 'fsd...]
    all_to_all x2, waiting for transfers between devices: 10.2 us -> 31.9 us  [body(): lax.all_to_all(to_send.reshape(le, sources, cap, width), 'exp', split_axi...]
    pallas_call x7 -> x8, Pallas kernels: 173 us -> 168 us  [the longest x2 129 us: expert_step(): pl.pallas_call(functools.partial(expert_kernel, first, tiles), grid_spec=...]
    ppermute x14 -> x10, starting transfers between devices: 17.2 us -> 20.4 us  [the longest x1 4.59 us: body(): near_got = lax.ppermute(give, 'fsdp', near).astype(F32)]
    unnamed x127 -> x130, local copies, waits for them, and re-layouts: 22.9 us -> 21.4 us
  transfers between devices with their start and end apart: 40 -> 39, of which waited for: 21 -> 18; matrix products, arithmetic and copies ran while one was open for 6% -> 8% of each run, Pallas kernels for 34% -> 39%
where the time goes in v3:
time: 874 us; the launch traced here: 864 us
  waiting for transfers between devices  346 us (40%)
  Pallas kernels  334 us (38%)
  starting transfers between devices  69.5 us (8%)
  local copies, waits for them, and re-layouts  63.6 us (7%)
  other arithmetic  36.3 us (4%)
  between operations  15.2 us (2%)
    pallas_call x2, Pallas kernels, expert_step(): pl.pallas_call(functools.partial(expert_kernel, first, tiles), grid_spec=...  129 us
    ppermute x1, waiting for transfers between devices, body(): normed_far = [lax.ppermute(normed_two[0], 'fsdp', far)[None]]  99 us
    pallas_call x2, Pallas kernels, attention_backward(): pl.pallas_call(functools.partial(backward_kernel, groups), in_specs=[sm,...  92.4 us
    ppermute x3, waiting for transfers between devices, gather_all(): lax.ppermute(block, 'exp', crossed(n_exp, 2 * k))  51.2 us
    pallas_call x2, Pallas kernels, attention_forward(): pl.pallas_call(forward_kernel, in_specs=[pl.BlockSpec(memory_space=pltpu....  51 us
    ppermute x1, waiting for transfers between devices, body(): far_got = lax.ppermute(give, 'fsdp', far)  39.4 us
    ppermute x1, waiting for transfers between devices, body(): lax.ppermute(after(jnp.concatenate([expert_in, expert_out]), ready), 'fsd...  33.5 us
    ppermute x3, waiting for transfers between devices, body(): lax.ppermute(blocks[k], 'exp', crossed(n_exp, 2 * k))  33 us
  transfers between devices with their start and end apart: 39, of which 18 were waited for; matrix products, arithmetic and copies ran while one was open for 8% of the time, Pallas kernels for 39%

profile of v3, /device:TPU:0, one launch (start us, length us, event | category | flops | bytes accessed | tf_op | source)
XLA Modules:
  0.0 864.3 jit_solution(11455522412394703305)
XLA Ops:
  7.2 3.4 fusion.19
  13.5 5.3 all-to-all-start
  21.0 7.8 collective-permute-done
  28.9 10.9 %all-to-all-done = bf16[2,8,48,1024]{3,2,0,1:T(8,128)(2,1)S(1)} async-done(((bf16[2,8,48,1024]{3,2,0,1:T(8,128)(2,1)}), bf16[2,8,48,1024]{3,2,0,1:T(8,128)(2,1)S(1)}, u32[]{:S(2)}, u32[]{:S(2)}) %all-to-all-start) | async-done | bytes 1572896 | tf_op jit(solution)/shard_map/all_to_all | solution.py:681
  42.4 7.6 pad_maximum_fusion
  50.0 15.6 %collective-permute-done.1 = bf16[2,144,1024]{2,1,0:T(8,128)(2,1)S(1)} collective-permute-done((bf16[2,144,1024]{2,1,0:T(8,128)(2,1)S(1)}, bf16[2,144,1024]{2,1,0:T(8,128)(2,1)S(1)}, u32[]{:S(2)}, u32[]{:S(2)}) %collective-permute-start.1) | collective-permute-done | bytes 589856 | tf_op jit(solution)/shard_map/ppermute | solution.py:613
  66.4 3.5 collective-permute-start.2
  71.5 25.3 %collective-permute-done.2.refs_1_ = bf16[4,144,1024]{2,1,0:T(8,128)(2,1)} collective-permute-done((bf16[4,144,1024]{2,1,0:T(8,128)(2,1)S(1)}, bf16[4,144,1024]{2,1,0:T(8,128)(2,1)}, u32[]{:S(2)}, u32[]{:S(2)}) %collective-permute-start.2) | collective-permute-done | bytes 1179680 | tf_op jit(solution)/shard_map/ppermute | solution.py:617
  96.9 25.8 %collective-permute-done.3.refs_2_ = bf16[4,144,1024]{2,1,0:T(8,128)(2,1)} collective-permute-done((bf16[4,144,1024]{2,1,0:T(8,128)(2,1)S(1)}, bf16[4,144,1024]{2,1,0:T(8,128)(2,1)}, u32[]{:S(2)}, u32[]{:S(2)}) %collective-permute-start.3) | collective-permute-done | bytes 1179680 | tf_op jit(solution)/shard_map/ppermute | solution.py:617
  123.2 4.1 copy_convert_fusion
  127.4 4.4 all-to-all-start.2
  133.5 7.3 shard_map.314
  143.1 25.5 %shard_map.315 = (bf16[768,1024]{1,0:T(8,128)(2,1)}, bf16[512,1024]{1,0:T(8,128)(2,1)S(1)}, bf16[512,1024]{1,0:T(8,128)(2,1)S(1)}, bf16[512,1024]{1,0:T(8,128)(2...) custom-call(s32[1,1]{1,0:T(1,128)} %bitcast.112.length, ...), custom_call_target="tpu_custom_call" | custom-call | flops 1000000 | bytes 100000 | tf_op jit(solution)/shard_map/pallas_call | solution.py:122
  174.3 4.4 all-to-all-start.1
  181.5 25.5 %shard_map.317 = (bf16[768,1024]{1,0:T(8,128)(2,1)}, bf16[512,1024]{1,0:T(8,128)(2,1)S(1)}, bf16[512,1024]{1,0:T(8,128)(2,1)S(1)}, bf16[512,1024]{1,0:T(8,128)(2...) custom-call(s32[1,1]{1,0:T(1,128)} %bitcast.111.length, ...), custom_call_target="tpu_custom_call" | custom-call | flops 1000000 | bytes 100000 | tf_op jit(solution)/shard_map/pallas_call | solution.py:122
  212.8 4.3 all-to-all-start.3
  218.4 5.5 shard_map.316.refs_0_
  223.9 3.4 collective-permute-start.9
  231.9 6.2 all-to-all-done.3
  240.9 5.5 shard_map.318.refs_0_
  246.3 3.4 collective-permute-start.16
  249.7 99.0 %collective-permute-done.9 = bf16[2,384,1024]{2,1,0:T(8,128)(2,1)S(1)} collective-permute-done((bf16[2,384,1024]{2,1,0:T(8,128)(2,1)}, bf16[2,384,1024]{2,1,0:T(8,128)(2,1)S(1)}, u32[]{:S(2)}, u32[]{:S(2)}) %collective-permute-start.9) | collective-permute-done | bytes 1572896 | tf_op jit(solution)/shard_map/ppermute | solution.py:722
  348.7 33.5 %collective-permute-done.10.refs_7_.refs_9_ = bf16[4,1024,1024]{2,1,0:T(8,128)(2,1)} collective-permute-done((bf16[4,1024,1024]{2,1,0:T(8,128)(2,1)}, bf16[4,1024,1024]{2,1,0:T(8,128)(2,1)}, u32[]{:S(2)}, u32[]{:S(2)}) %collective-permute-start.10) | collective-permute-done | bytes 8388640 | tf_op jit(solution)/shard_map/ppermute | solution.py:689
  382.2 54.3 %shard_map.319 = (bf16[2,384,1024]{2,1,0:T(8,128)(2,1)}, bf16[2,384,1024]{2,1,0:T(8,128)(2,1)}, bf16[2,384,1024]{2,1,0:T(8,128)(2,1)}, bf16[2,384,1024]{2,1,0:T(...) custom-call(s32[1]{0:T(128)} %bitcast.4._, ...), custom_call_target="tpu_custom_call" | custom-call | flops 1000000 | bytes 100000 | tf_op jit(solution)/shard_map/pallas_call | solution.py:578
  442.2 75.0 %shard_map.322 = (bf16[2,384,1024]{2,1,0:T(8,128)(2,1)}, bf16[2,384,1024]{2,1,0:T(8,128)(2,1)}, bf16[2,384,1024]{2,1,0:T(8,128)(2,1)}, bf16[2,384,1024]{2,1,0:T(...) custom-call(s32[1]{0:T(128)} %bitcast.4._, ...), custom_call_target="tpu_custom_call" | custom-call | flops 1000000 | bytes 100000 | tf_op jit(solution)/shard_map/pallas_call | solution.py:578
  518.3 8.2 shard_map.320
  529.3 5.1 all-to-all-start.4
  537.1 3.3 pad_maximum_fusion.1
  540.4 15.1 %all-to-all-done.4 = bf16[2,8,48,1024]{3,2,0,1:T(8,128)(2,1)S(1)} async-done(((bf16[2,8,48,1024]{3,2,0,1:T(8,128)(2,1)}), bf16[2,8,48,1024]{3,2,0,1:T(8,128)(2,1)S(1)}, u32[]{:S(2)}, u32[]{:S(2)}) %all-to-all-start.4) | async-done | bytes 1572896 | tf_op jit(solution)/shard_map/all_to_all | solution.py:754
  556.6 46.1 %shard_map.321 = (bf16[768,1024]{1,0:T(8,128)(2,1)}, bf16[16,32,1024]{2,1,0:T(8,128)(2,1)}, bf16[16,32,1024]{2,1,0:T(8,128)(2,1)}, bf16[16,32,1024]{2,1,0:T(8,12...) custom-call(s32[1,1]{1,0:T(1,128)} %bitcast.112.length, ...), custom_call_target="tpu_custom_call" | custom-call | flops 1000000 | bytes 100000 | tf_op jit(solution)/shard_map/pallas_call | solution.py:261
  602.8 8.3 shard_map.323
  611.1 3.0 copy.126
  614.1 3.9 all-to-all-start.5
  622.1 16.8 %all-to-all-done.5 = bf16[2,8,48,1024]{3,2,0,1:T(8,128)(2,1)S(1)} async-done(((bf16[2,8,48,1024]{3,2,0,1:T(8,128)(2,1)}), bf16[2,8,48,1024]{3,2,0,1:T(8,128)(2,1)S(1)}, u32[]{:S(2)}, u32[]{:S(2)}) %all-to-all-start.5) | async-done | bytes 1572896 | tf_op jit(solution)/shard_map/all_to_all | solution.py:754
  640.0 46.3 %shard_map.324 = (bf16[768,1024]{1,0:T(8,128)(2,1)}, bf16[16,32,1024]{2,1,0:T(8,128)(2,1)}, bf16[16,32,1024]{2,1,0:T(8,128)(2,1)}, bf16[16,32,1024]{2,1,0:T(8,12...) custom-call(s32[1,1]{1,0:T(1,128)} %bitcast.111.length, ...), custom_call_target="tpu_custom_call" | custom-call | flops 1000000 | bytes 100000 | tf_op jit(solution)/shard_map/pallas_call | solution.py:261
  688.8 4.3 all-to-all-start.6
  696.3 8.5 shard_map.325
  708.3 6.3 all-to-all-done.6
  714.6 4.6 all-to-all-start.7
  719.2 4.1 copy.129
  728.0 8.7 %collective-permute-done.22.refs_0_ = bf16[528,1024]{1,0:T(8,128)(2,1)S(1)} collective-permute-done((bf16[528,1024]{1,0:T(8,128)(2,1)}, bf16[528,1024]{1,0:T(8,128)(2,1)S(1)}, u32[]{:S(2)}, u32[]{:S(2)}) %collective-permute-start.22) | collective-permute-done | bytes 1081376 | tf_op jit(solution)/shard_map/ppermute | solution.py:772
  736.8 24.2 %collective-permute-done.24.refs_2_ = bf16[528,1024]{1,0:T(8,128)(2,1)} collective-permute-done((bf16[528,1024]{1,0:T(8,128)(2,1)}, bf16[528,1024]{1,0:T(8,128)(2,1)}, u32[]{:S(2)}, u32[]{:S(2)}) %collective-permute-start.24) | collective-permute-done | bytes 1081376 | tf_op jit(solution)/shard_map/ppermute | solution.py:772
  768.9 8.5 all-to-all-done.7
  777.4 3.5 copy.134
  781.0 39.4 %collective-permute-done.25 = bf16[272,1024]{1,0:T(8,128)(2,1)} collective-permute-done((bf16[272,1024]{1,0:T(8,128)(2,1)}, bf16[272,1024]{1,0:T(8,128)(2,1)}, u32[]{:S(2)}, u32[]{:S(2)}) %collective-permute-start.25) | collective-permute-done | bytes 557088 | tf_op jit(solution)/shard_map/ppermute | solution.py:774
  822.7 5.6 fusion.9
  830.3 4.6 collective-permute-start.26
  838.2 15.6 %shard_map.327 = (f32[2,1024,1024]{2,1,0:T(8,128)}, f32[2,1024,1024]{2,1,0:T(8,128)}) custom-call(f32[2,1024,1024]{2,1,0:T(8,128)} %get-tuple-element.170.a, f32[2,1024,1024]{2,1,0:T(8,128)} %get-tuple-element.171.c, bf16[2,2,1024,1024]{3,2,1,0:T(8,128)(2,1)} %collective-permute-done.27.got), custom_call_target="tpu_custom_call", output_to_operand_aliasing={{0}: (0, {}), {1}: (1, {})} | custom-call | flops 1000000 | bytes 100000 | tf_op jit(solution)/shard_map/pallas_call | solution.py:389
  (265 shorter events, 88.3 us)
Async XLA Ops:
  13.5 26.3 %all-to-all-start = ((bf16[2,8,48,1024]{3,2,0,1:T(8,128)(2,1)}), bf16[2,8,48,1024]{3,2,0,1:T(8,128)(2,1)S(1)}, u32[]{:S(2)}, u32[]{:S(2)}) async-start(bf16[2,8,48,1024]{3,2,0,1:T(8,128)(2,1)} %get-tuple-element.189), calls=%async_computation | async-start | bytes 3145728 | tf_op jit(solution)/shard_map/all_to_all | solution.py:681
  18.8 227.5 %all-gather.7.cloned.1.call-start = ((), (), s32[]{:S(2)}) async-start(), calls=%async_computation.8 | async-start | bytes 9437184 | tf_op jit(solution)/shard_map/all_gather | solution.py:607
  19.4 9.4 %collective-permute-start = (bf16[1,144,1024]{2,1,0:T(8,128)(2,1)S(1)}, bf16[1,144,1024]{2,1,0:T(8,128)(2,1)S(1)}, u32[]{:S(2)}, u32[]{:S(2)}) collective-permute-start(bf16[1,144,1024]{2,1,0:T(8,128)(2,1)S(1)} %bitcast.225), channel_id=1, source_target_pairs={{0,1},{1,0},{2,3},{3,2},{4,5},{5,4},{6,7},{7,6},{8,9},{9,8},{10,11... | collective-permute-start | bytes 884744 | tf_op jit(solution)/shard_map/ppermute | solution.py:613
  39.8 25.8 %collective-permute-start.1 = (bf16[2,144,1024]{2,1,0:T(8,128)(2,1)S(1)}, bf16[2,144,1024]{2,1,0:T(8,128)(2,1)S(1)}, u32[]{:S(2)}, u32[]{:S(2)}) collective-permute-start(bf16[2,144,1024]{2,1,0:T(8,128)(2,1)S(1)} %pad_maximum_fusion.4), channel_id=1, source_target_pairs={{0,2},{1,3},{2,0},{3,1},{4,6},{5,7},{6,4},{7,5},{8,10},{9,11},{10,... | collective-permute-start | bytes 1769480 | tf_op jit(solution)/shard_map/ppermute | solution.py:613
  65.7 316.5 %collective-permute-start.10 = (bf16[4,1024,1024]{2,1,0:T(8,128)(2,1)}, bf16[4,1024,1024]{2,1,0:T(8,128)(2,1)}, u32[]{:S(2)}, u32[]{:S(2)}) collective-permute-start(bf16[4,1024,1024]{2,1,0:T(8,128)(2,1)} %pad_maximum_fusion), channel_id=1, source_target_pairs={{0,1},{1,0},{2,3},{3,2},{4,5},{5,4},{6,7},{7,6},{8,9},{9,8},{10,11... | collective-permute-start | bytes 25165832 | tf_op jit(solution)/shard_map/ppermute | solution.py:689
  66.4 30.4 %collective-permute-start.2 = (bf16[4,144,1024]{2,1,0:T(8,128)(2,1)S(1)}, bf16[4,144,1024]{2,1,0:T(8,128)(2,1)}, u32[]{:S(2)}, u32[]{:S(2)}) collective-permute-start(bf16[4,144,1024]{2,1,0:T(8,128)(2,1)S(1)} %constant_dynamic-update-slice_fusion.5.refs_0_), channel_id=1, source_target_pairs={{0,8},{4,12},{8,0},{12,4},{16,24},{20,28},{24,16},{28,20},{1,9},{5... | collective-permute-start | bytes 3538952 | tf_op jit(solution)/shard_map/ppermute | solution.py:617
  70.0 52.7 %collective-permute-start.3 = (bf16[4,144,1024]{2,1,0:T(8,128)(2,1)S(1)}, bf16[4,144,1024]{2,1,0:T(8,128)(2,1)}, u32[]{:S(2)}, u32[]{:S(2)}) collective-permute-start(bf16[4,144,1024]{2,1,0:T(8,128)(2,1)S(1)} %constant_dynamic-update-slice_fusion.5.refs_0_), channel_id=1, source_target_pairs={{0,16},{4,20},{8,24},{12,28},{16,0},{20,4},{24,8},{28,12},{1,17},{... | collective-permute-start | bytes 3538952 | tf_op jit(solution)/shard_map/ppermute | solution.py:617
  70.3 52.4 %collective-permute-start.4 = (bf16[4,144,1024]{2,1,0:T(8,128)(2,1)S(1)}, bf16[4,144,1024]{2,1,0:T(8,128)(2,1)}, u32[]{:S(2)}, u32[]{:S(2)}) collective-permute-start(bf16[4,144,1024]{2,1,0:T(8,128)(2,1)S(1)} %constant_dynamic-update-slice_fusion.5.refs_0_), channel_id=1, source_target_pairs={{0,24},{4,28},{8,16},{12,20},{16,8},{20,12},{24,0},{28,4},{1,25},{... | collective-permute-start | bytes 3538952 | tf_op jit(solution)/shard_map/ppermute | solution.py:617
  71.5 62.0 %collective-permute-start.5 = (bf16[4,144,1024]{2,1,0:T(8,128)(2,1)S(1)}, bf16[4,144,1024]{2,1,0:T(8,128)(2,1)}, u32[]{:S(2)}, u32[]{:S(2)}) collective-permute-start(bf16[4,144,1024]{2,1,0:T(8,128)(2,1)S(1)} %constant_dynamic-update-slice_fusion.5.refs_0_), channel_id=1, source_target_pairs={{0,4},{4,0},{8,12},{12,8},{16,20},{20,16},{24,28},{28,24},{1,5},{5... | collective-permute-start | bytes 3538952 | tf_op jit(solution)/shard_map/ppermute | solution.py:618
  96.9 36.6 %collective-permute-start.6 = (bf16[4,144,1024]{2,1,0:T(8,128)(2,1)}, bf16[4,144,1024]{2,1,0:T(8,128)(2,1)}, u32[]{:S(2)}, u32[]{:S(2)}) collective-permute-start(bf16[4,144,1024]{2,1,0:T(8,128)(2,1)} %collective-permute-done.2.refs_1_), channel_id=1, source_target_pairs={{0,4},{4,0},{8,12},{12,8},{16,20},{20,16},{24,28},{28,24},{1,5},{5... | collective-permute-start | bytes 3538952 | tf_op jit(solution)/shard_map/ppermute | solution.py:618
  122.7 10.8 %collective-permute-start.7 = (bf16[4,144,1024]{2,1,0:T(8,128)(2,1)}, bf16[4,144,1024]{2,1,0:T(8,128)(2,1)}, u32[]{:S(2)}, u32[]{:S(2)}) collective-permute-start(bf16[4,144,1024]{2,1,0:T(8,128)(2,1)} %collective-permute-done.3.refs_2_), channel_id=1, source_target_pairs={{0,4},{4,0},{8,12},{12,8},{16,20},{20,16},{24,28},{28,24},{1,5},{5... | collective-permute-start | bytes 3538952 | tf_op jit(solution)/shard_map/ppermute | solution.py:618
  122.7 10.8 %collective-permute-start.8 = (bf16[4,144,1024]{2,1,0:T(8,128)(2,1)}, bf16[4,144,1024]{2,1,0:T(8,128)(2,1)}, u32[]{:S(2)}, u32[]{:S(2)}) collective-permute-start(bf16[4,144,1024]{2,1,0:T(8,128)(2,1)} %collective-permute-done.4.refs_3_), channel_id=1, source_target_pairs={{0,4},{4,0},{8,12},{12,8},{16,20},{20,16},{24,28},{28,24},{1,5},{5... | collective-permute-start | bytes 3538952 | tf_op jit(solution)/shard_map/ppermute | solution.py:618
  127.4 46.9 %all-to-all-start.2 = ((bf16[2,8,48,1024]{3,2,0,1:T(8,128)(2,1)}), bf16[2,8,48,1024]{3,2,0,1:T(8,128)(2,1)}, u32[]{:S(2)}, u32[]{:S(2)}) async-start(bf16[2,8,48,1024]{3,2,0,1:T(8,128)(2,1)} %get-tuple-element.191), calls=%async_computation.2 | async-start | bytes 3145728 | tf_op jit(solution)/shard_map/all_to_all | solution.py:681
  132.6 48.9 %copy-start.22 = (s32[1,512]{1,0:T(1,128)}, s32[1,512]{1,0:T(1,128)S(1)}, u32[]{:S(2)}) copy-start(s32[1,512]{1,0:T(1,128)S(1)} %get-tuple-element.216.row) | copy-start | bytes 6148
  143.0 38.5 %copy-start.19 = (f32[8,1024]{1,0:T(8,128)}, f32[8,1024]{1,0:T(8,128)S(1)}, u32[]{:S(2)}) copy-start(f32[8,1024]{1,0:T(8,128)S(1)} %stack.30.small) | copy-start | bytes 98308
  174.3 38.5 %all-to-all-start.1 = ((bf16[16,48,1024]{2,1,0:T(8,128)(2,1)}), bf16[16,48,1024]{2,1,0:T(8,128)(2,1)S(1)}, u32[]{:S(2)}, u32[]{:S(2)}) async-start(bf16[16,48,1024]{2,1,0:T(8,128)(2,1)} %bitcast.216), calls=%async_computation.1 | async-start | bytes 3145728 | tf_op jit(solution)/shard_map/all_to_all | solution.py:717
  178.8 28.2 %copy-start.1 = (s32[512,1]{1,0:T(8,128)}, s32[512,1]{1,0:T(8,128)S(1)}, u32[]{:S(2)}) copy-start(s32[512,1]{1,0:T(8,128)S(1)} %copy.115.column) | copy-start | bytes 6148
  212.8 25.3 %all-to-all-start.3 = ((bf16[16,48,1024]{2,1,0:T(8,128)(2,1)}), bf16[16,48,1024]{2,1,0:T(8,128)(2,1)}, u32[]{:S(2)}, u32[]{:S(2)}) async-start(bf16[16,48,1024]{2,1,0:T(8,128)(2,1)} %bitcast.217), calls=%async_computation.3 | async-start | bytes 3145728 | tf_op jit(solution)/shard_map/all_to_all | solution.py:717
  217.1 385.7 %all-gather.9.cloned.1.call-start = ((), (), s32[]{:S(2)}) async-start(), calls=%async_computation.9 | async-start | bytes 4718592 | tf_op jit(solution)/shard_map/all_gather | solution.py:607
  223.9 124.8 %collective-permute-start.9 = (bf16[2,384,1024]{2,1,0:T(8,128)(2,1)}, bf16[2,384,1024]{2,1,0:T(8,128)(2,1)S(1)}, u32[]{:S(2)}, u32[]{:S(2)}) collective-permute-start(bf16[2,384,1024]{2,1,0:T(8,128)(2,1)} %shard_map.316.refs_0_), channel_id=1, source_target_pairs={{0,2},{1,3},{2,0},{3,1},{4,6},{5,7},{6,4},{7,5},{8,10},{9,11},{10,... | collective-permute-start | bytes 4718600 | tf_op jit(solution)/shard_map/ppermute | solution.py:722
  246.3 194.7 %collective-permute-start.16 = (bf16[2,384,1024]{2,1,0:T(8,128)(2,1)}, bf16[2,384,1024]{2,1,0:T(8,128)(2,1)S(1)}, u32[]{:S(2)}, u32[]{:S(2)}) collective-permute-start(bf16[2,384,1024]{2,1,0:T(8,128)(2,1)} %shard_map.318.refs_0_), channel_id=1, source_target_pairs={{0,2},{1,3},{2,0},{3,1},{4,6},{5,7},{6,4},{7,5},{8,10},{9,11},{10,... | collective-permute-start | bytes 4718600 | tf_op jit(solution)/shard_map/ppermute | solution.py:725
  348.7 33.5 %copy-start.36 = (bf16[2,384,1024]{2,1,0:T(8,128)(2,1)}, bf16[2,384,1024]{2,1,0:T(8,128)(2,1)S(1)}, u32[]{:S(2)}) copy-start(bf16[2,384,1024]{2,1,0:T(8,128)(2,1)S(1)} %collective-permute-done.9) | copy-start | bytes 4718596
  436.5 80.7 %collective-permute-start.11 = (bf16[2,384,1024]{2,1,0:T(8,128)(2,1)}, bf16[2,384,1024]{2,1,0:T(8,128)(2,1)S(1)}, u32[]{:S(2)}, u32[]{:S(2)}) collective-permute-start(bf16[2,384,1024]{2,1,0:T(8,128)(2,1)} %get-tuple-element.105), channel_id=1, source_target_pairs={{0,2},{1,3},{2,0},{3,1},{4,6},{5,7},{6,4},{7,5},{8,10},{9,11},{10,... | collective-permute-start | bytes 4718600 | tf_op jit(solution)/shard_map/ppermute | solution.py:736
  529.3 26.1 %all-to-all-start.4 = ((bf16[2,8,48,1024]{3,2,0,1:T(8,128)(2,1)}), bf16[2,8,48,1024]{3,2,0,1:T(8,128)(2,1)S(1)}, u32[]{:S(2)}, u32[]{:S(2)}) async-start(bf16[2,8,48,1024]{3,2,0,1:T(8,128)(2,1)} %copy.121), calls=%async_computation.4 | async-start | bytes 3145728 | tf_op jit(solution)/shard_map/all_to_all | solution.py:754
  534.5 288.2 %all-gather.11.cloned.1.call-start = ((), (), s32[]{:S(2)}) async-start(), calls=%async_computation.10 | async-start | bytes 9437184 | tf_op jit(solution)/shard_map/all_gather | solution.py:607
  534.5 303.7 %collective-permute-start.27 = (bf16[2,2,1024,1024]{3,2,1,0:T(8,128)(2,1)}, bf16[2,2,1024,1024]{3,2,1,0:T(8,128)(2,1)}, u32[]{:S(2)}, u32[]{:S(2)}) collective-permute-start(bf16[2,2,1024,1024]{3,2,1,0:T(8,128)(2,1)} %get-tuple-element.172), channel_id=1, source_target_pairs={{0,1},{1,0},{2,3},{3,2},{4,5},{5,4},{6,7},{7,6},{8,9},{9,8},{10,11... | collective-permute-start | bytes 25165832 | tf_op jit(solution)/shard_map/ppermute | solution.py:743
  614.1 24.8 %all-to-all-start.5 = ((bf16[2,8,48,1024]{3,2,0,1:T(8,128)(2,1)}), bf16[2,8,48,1024]{3,2,0,1:T(8,128)(2,1)S(1)}, u32[]{:S(2)}, u32[]{:S(2)}) async-start(bf16[2,8,48,1024]{3,2,0,1:T(8,128)(2,1)} %copy.126), calls=%async_computation.5 | async-start | bytes 3145728 | tf_op jit(solution)/shard_map/all_to_all | solution.py:754
  617.9 69.4 %collective-permute-start.12 = (bf16[16,32,1024]{2,1,0:T(8,128)(2,1)}, bf16[16,32,1024]{2,1,0:T(8,128)(2,1)}, u32[]{:S(2)}, u32[]{:S(2)}) collective-permute-start(bf16[16,32,1024]{2,1,0:T(8,128)(2,1)} %get-tuple-element.117), channel_id=1, source_target_pairs={{0,4},{4,0},{8,12},{12,8},{16,20},{20,16},{24,28},{28,24},{1,5},{5... | collective-permute-start | bytes 3145736 | tf_op jit(solution)/shard_map/ppermute | solution.py:767
  618.4 69.0 %collective-permute-start.13 = (bf16[16,32,1024]{2,1,0:T(8,128)(2,1)}, bf16[16,32,1024]{2,1,0:T(8,128)(2,1)}, u32[]{:S(2)}, u32[]{:S(2)}) collective-permute-start(bf16[16,32,1024]{2,1,0:T(8,128)(2,1)} %get-tuple-element.118), channel_id=1, source_target_pairs={{0,4},{4,0},{8,12},{12,8},{16,20},{20,16},{24,28},{28,24},{1,5},{5... | collective-permute-start | bytes 3145736 | tf_op jit(solution)/shard_map/ppermute | solution.py:767
  618.5 69.4 %collective-permute-start.14 = (bf16[16,32,1024]{2,1,0:T(8,128)(2,1)}, bf16[16,32,1024]{2,1,0:T(8,128)(2,1)}, u32[]{:S(2)}, u32[]{:S(2)}) collective-permute-start(bf16[16,32,1024]{2,1,0:T(8,128)(2,1)} %get-tuple-element.119), channel_id=1, source_target_pairs={{0,4},{4,0},{8,12},{12,8},{16,20},{20,16},{24,28},{28,24},{1,5},{5... | collective-permute-start | bytes 3145736 | tf_op jit(solution)/shard_map/ppermute | solution.py:767
  618.9 69.0 %collective-permute-start.15 = (bf16[16,32,1024]{2,1,0:T(8,128)(2,1)}, bf16[16,32,1024]{2,1,0:T(8,128)(2,1)}, u32[]{:S(2)}, u32[]{:S(2)}) collective-permute-start(bf16[16,32,1024]{2,1,0:T(8,128)(2,1)} %get-tuple-element.120), channel_id=1, source_target_pairs={{0,4},{4,0},{8,12},{12,8},{16,20},{20,16},{24,28},{28,24},{1,5},{5... | collective-permute-start | bytes 3145736 | tf_op jit(solution)/shard_map/ppermute | solution.py:767
  640.0 46.3 %copy-start.47 = (f32[8,1024]{1,0:T(8,128)S(1)}, f32[8,1024]{1,0:T(8,128)}, u32[]{:S(2)}) copy-start(f32[8,1024]{1,0:T(8,128)} %get-tuple-element.149) | copy-start | bytes 98308
  687.3 1.3 collective-permute-start.21
  687.4 5.7 collective-permute-start.17
  687.9 5.2 collective-permute-start.18
  688.0 5.5 collective-permute-start.19
  688.6 6.4 collective-permute-start.20
  688.8 25.9 %all-to-all-start.6 = ((bf16[16,48,1024]{2,1,0:T(8,128)(2,1)}), bf16[16,48,1024]{2,1,0:T(8,128)(2,1)}, u32[]{:S(2)}, u32[]{:S(2)}) async-start(bf16[16,48,1024]{2,1,0:T(8,128)(2,1)} %bitcast.215), calls=%async_computation.6 | async-start | bytes 3145728 | tf_op jit(solution)/shard_map/all_to_all | solution.py:760
  704.8 32.0 %collective-permute-start.22 = (bf16[528,1024]{1,0:T(8,128)(2,1)}, bf16[528,1024]{1,0:T(8,128)(2,1)S(1)}, u32[]{:S(2)}, u32[]{:S(2)}) collective-permute-start(bf16[528,1024]{1,0:T(8,128)(2,1)} %get-tuple-element.154), channel_id=1, source_target_pairs={{0,8},{4,12},{8,0},{12,4},{16,24},{20,28},{24,16},{28,20},{1,9},{5... | collective-permute-start | bytes 3244040 | tf_op jit(solution)/shard_map/ppermute | solution.py:772
  705.3 31.4 %collective-permute-start.23 = (bf16[528,1024]{1,0:T(8,128)(2,1)}, bf16[528,1024]{1,0:T(8,128)(2,1)S(1)}, u32[]{:S(2)}, u32[]{:S(2)}) collective-permute-start(bf16[528,1024]{1,0:T(8,128)(2,1)} %get-tuple-element.155), channel_id=1, source_target_pairs={{0,16},{4,20},{8,24},{12,28},{16,0},{20,4},{24,8},{28,12},{1,17},{... | collective-permute-start | bytes 3244040 | tf_op jit(solution)/shard_map/ppermute | solution.py:772
  706.3 54.7 %collective-permute-start.24 = (bf16[528,1024]{1,0:T(8,128)(2,1)}, bf16[528,1024]{1,0:T(8,128)(2,1)}, u32[]{:S(2)}, u32[]{:S(2)}) collective-permute-start(bf16[528,1024]{1,0:T(8,128)(2,1)} %get-tuple-element.156), channel_id=1, source_target_pairs={{0,24},{4,28},{8,16},{12,20},{16,8},{20,12},{24,0},{28,4},{1,25},{... | collective-permute-start | bytes 3244040 | tf_op jit(solution)/shard_map/ppermute | solution.py:772
  714.6 62.8 %all-to-all-start.7 = ((bf16[16,48,1024]{2,1,0:T(8,128)(2,1)}), bf16[16,48,1024]{2,1,0:T(8,128)(2,1)}, u32[]{:S(2)}, u32[]{:S(2)}) async-start(bf16[16,48,1024]{2,1,0:T(8,128)(2,1)} %bitcast.214), calls=%async_computation.7 | async-start | bytes 3145728 | tf_op jit(solution)/shard_map/all_to_all | solution.py:760
  723.4 37.6 %copy-start.2 = (bf16[528,1024]{1,0:T(8,128)(2,1)S(1)}, bf16[528,1024]{1,0:T(8,128)(2,1)}, u32[]{:S(2)}) copy-start(bf16[528,1024]{1,0:T(8,128)(2,1)} %get-tuple-element.153.first) | copy-start | bytes 3244036
  764.5 55.9 %collective-permute-start.25 = (bf16[272,1024]{1,0:T(8,128)(2,1)}, bf16[272,1024]{1,0:T(8,128)(2,1)}, u32[]{:S(2)}, u32[]{:S(2)}) collective-permute-start(bf16[272,1024]{1,0:T(8,128)(2,1)} %get-tuple-element.158), channel_id=1, source_target_pairs={{0,2},{1,3},{2,0},{3,1},{4,6},{5,7},{6,4},{7,5},{8,10},{9,11},{10,... | collective-permute-start | bytes 1671176 | tf_op jit(solution)/shard_map/ppermute | solution.py:774
  777.4 43.0 %copy-start.18 = (f32[256,1024]{1,0:T(8,128)S(1)}, f32[256,1024]{1,0:T(8,128)}, u32[]{:S(2)}) copy-start(f32[256,1024]{1,0:T(8,128)} %copy-done.17) | copy-start | bytes 3145732
  781.0 41.7 %copy-start.24 = (bf16[2,8,48,1024]{3,2,1,0:T(8,128)(2,1)S(1)}, bf16[2,8,48,1024]{3,2,1,0:T(8,128)(2,1)}, u32[]{:S(2)}) copy-start(bf16[2,8,48,1024]{3,2,1,0:T(8,128)(2,1)} %copy.116) | copy-start | bytes 4718596
  781.0 41.7 %copy-start.25 = (bf16[2,8,48,1024]{3,2,1,0:T(8,128)(2,1)S(1)}, bf16[2,8,48,1024]{3,2,1,0:T(8,128)(2,1)}, u32[]{:S(2)}) copy-start(bf16[2,8,48,1024]{3,2,1,0:T(8,128)(2,1)} %copy.112) | copy-start | bytes 4718596
  830.3 23.5 %collective-permute-start.26 = (bf16[148,1024]{1,0:T(8,128)(2,1)S(1)}, bf16[148,1024]{1,0:T(8,128)(2,1)S(1)}, u32[]{:S(2)}, u32[]{:S(2)}) collective-permute-start(bf16[148,1024]{1,0:T(8,128)(2,1)S(1)} %pad_maximum_fusion.5), channel_id=1, source_target_pairs={{0,1},{1,0},{2,3},{3,2},{4,5},{5,4},{6,7},{7,6},{8,9},{9,8},{10,11... | collective-permute-start | bytes 909320 | tf_op jit(solution)/shard_map/ppermute | solution.py:791
  (50 other events, 254.9 us)
Sparse Core Ops, SparseCore 0:
  71.6 148.3 all-gather.6
  517.3 80.8 all-gather.8
  602.9 146.0 all-gather.10

commit v4 on v3

--- a/solution.py
+++ b/solution.py
@@ -507,8 +507,8 @@
         dwo = dot(act, g, TN)
         column = jnp.sum(grad_inner.astype(F32), axis=0, keepdims=True)
         if mine:
-            dwi_own[0] = dwi if first else dwi + before[0][0]
-            dwo_own[0] = dwo if first else dwo + before[1][0]
+            dwi_own[0] = dwi.astype(BF) if first else dwi + before[0][0].astype(F32)
+            dwo_own[0] = dwo.astype(BF) if first else dwo + before[1][0].astype(F32)
         else:
             dw_near[0, 0] = (dwi if first else dwi + before[2][0, 0].astype(F32)).astype(dw_near.dtype)
             dw_near[0, 1] = (dwo if first else dwo + before[2][0, 1].astype(F32)).astype(dw_near.dtype)
@@ -535,14 +535,13 @@
     hidden = wi_own.shape[2]
     tiles = hidden // tile
     first = before is None
-    mode = None if first else pl.Buffered(1)
     out_row = pl.BlockSpec((1, rows, width), lambda j, h, s: (j, 0, 0))
-    mark = pl.BlockSpec((1, rows, 1), lambda j, h, s: (j, 0, 0), pipeline_mode=mode)
+    mark = pl.BlockSpec((1, rows, 1), lambda j, h, s: (j, 0, 0))
     own = lambda h: jnp.minimum(h, tiles - 1)
     near = lambda h: jnp.maximum(h - tiles, 0)
     shapes = [jax.ShapeDtypeStruct((le, rows, width), BF)] * 4 + [
-        jax.ShapeDtypeStruct((le, width, hidden), F32),
-        jax.ShapeDtypeStruct((le, hidden, width), F32),
+        jax.ShapeDtypeStruct((le, width, hidden), BF if first else F32),
+        jax.ShapeDtypeStruct((le, hidden, width), BF if first else F32),
         jax.ShapeDtypeStruct((le, 2, hidden, width), BF),
         jax.ShapeDtypeStruct((le, 1, 2 * hidden), F32),
         jax.ShapeDtypeStruct((le, 1, width), F32),
@@ -559,10 +558,10 @@
     ]
     operands = [x_own, x_far, g_own, g_far, *fills, wi_own, w_near, wo_own, w_near, bias]
     in_specs = [
-        pl.BlockSpec((1, rows, width), lambda j, h, s: (j, 0, 0), pipeline_mode=mode),
-        pl.BlockSpec((1, 1, rows, width), lambda j, h, s: (side_of(x_far, s), j, 0, 0), pipeline_mode=mode),
-        pl.BlockSpec((1, 1, rows, width), lambda j, h, s: (t, j, 0, 0), pipeline_mode=mode),
-        pl.BlockSpec((1, 1, 1, rows, width), lambda j, h, s: (side_of(g_far, s), t, j, 0, 0), pipeline_mode=mode),
+        pl.BlockSpec((1, rows, width), lambda j, h, s: (j, 0, 0)),
+        pl.BlockSpec((1, 1, rows, width), lambda j, h, s: (side_of(x_far, s), j, 0, 0)),
+        pl.BlockSpec((1, 1, rows, width), lambda j, h, s: (t, j, 0, 0)),
+        pl.BlockSpec((1, 1, 1, rows, width), lambda j, h, s: (side_of(g_far, s), t, j, 0, 0)),
         mark,
         mark,
         own_in,
@@ -573,8 +572,7 @@
     ]
     if not first:
         operands += list(before)
-        near_before = pl.BlockSpec((1, 2, tile, width), lambda j, h, s: (j, 0, near(h), 0), pipeline_mode=mode)
-        in_specs += grads[:2] + [near_before] + grads[3:]
+        in_specs += grads
     return pl.pallas_call(
         functools.partial(expert_kernel, first, tiles),
         grid_spec=pltpu.PrefetchScalarGridSpec(

time: 874 us -> 864 us (0.989)
  Pallas kernels: 334 us -> 322 us
    pallas_call x2, Pallas kernels: 129 us -> 118 us  [expert_step(): pl.pallas_call(functools.partial(expert_kernel, first, tiles), grid_spec=...]
  transfers between devices with their start and end apart: 39 -> 39, of which waited for: 18 -> 19; matrix products, arithmetic and copies ran while one was open for 8% -> 8% of each run, Pallas kernels for 39% -> 38%
where the time goes in v4:
time: 864 us; the launch traced here: 854 us
  waiting for transfers between devices  348 us (40%)
  Pallas kernels  322 us (37%)
  starting transfers between devices  69 us (8%)
  local copies, waits for them, and re-layouts  63.7 us (7%)
  other arithmetic  36.4 us (4%)
  between operations  15.2 us (2%)
    pallas_call x2, Pallas kernels, expert_step(): pl.pallas_call(functools.partial(expert_kernel, first, tiles), grid_spec=...  118 us
    ppermute x1, waiting for transfers between devices, body(): normed_far = [lax.ppermute(normed_two[0], 'fsdp', far)[None]]  99.1 us
    pallas_call x2, Pallas kernels, attention_backward(): pl.pallas_call(functools.partial(backward_kernel, groups), in_specs=[sm,...  92 us
    ppermute x3, waiting for transfers between devices, gather_all(): lax.ppermute(block, 'exp', crossed(n_exp, 2 * k))  51.2 us
    pallas_call x2, Pallas kernels, attention_forward(): pl.pallas_call(forward_kernel, in_specs=[pl.BlockSpec(memory_space=pltpu....  51 us
    ppermute x1, waiting for transfers between devices, body(): far_got = lax.ppermute(give, 'fsdp', far)  41 us
    ppermute x1, waiting for transfers between devices, body(): lax.ppermute(after(jnp.concatenate([expert_in, expert_out]), ready), 'fsd...  33.5 us
    ppermute x3, waiting for transfers between devices, body(): lax.ppermute(blocks[k], 'exp', crossed(n_exp, 2 * k))  33 us
  transfers between devices with their start and end apart: 39, of which 19 were waited for; matrix products, arithmetic and copies ran while one was open for 8% of the time, Pallas kernels for 38%

profile of v4, /device:TPU:0, one launch (start us, length us, event | category | flops | bytes accessed | tf_op | source)
XLA Modules:
  0.0 854.4 jit_solution(10402340021010875491)
XLA Ops:
  7.2 3.4 fusion.19
  13.5 5.3 all-to-all-start
  21.0 7.8 collective-permute-done
  28.9 10.9 %all-to-all-done = bf16[2,8,48,1024]{3,2,0,1:T(8,128)(2,1)S(1)} async-done(((bf16[2,8,48,1024]{3,2,0,1:T(8,128)(2,1)}), bf16[2,8,48,1024]{3,2,0,1:T(8,128)(2,1)S(1)}, u32[]{:S(2)}, u32[]{:S(2)}) %all-to-all-start) | async-done | bytes 1572896 | tf_op jit(solution)/shard_map/all_to_all | solution.py:679
  42.4 7.6 pad_maximum_fusion
  50.0 15.6 %collective-permute-done.1 = bf16[2,144,1024]{2,1,0:T(8,128)(2,1)S(1)} collective-permute-done((bf16[2,144,1024]{2,1,0:T(8,128)(2,1)S(1)}, bf16[2,144,1024]{2,1,0:T(8,128)(2,1)S(1)}, u32[]{:S(2)}, u32[]{:S(2)}) %collective-permute-start.1) | collective-permute-done | bytes 589856 | tf_op jit(solution)/shard_map/ppermute | solution.py:611
  66.4 3.5 collective-permute-start.2
  71.5 25.3 %collective-permute-done.2.refs_1_ = bf16[4,144,1024]{2,1,0:T(8,128)(2,1)} collective-permute-done((bf16[4,144,1024]{2,1,0:T(8,128)(2,1)S(1)}, bf16[4,144,1024]{2,1,0:T(8,128)(2,1)}, u32[]{:S(2)}, u32[]{:S(2)}) %collective-permute-start.2) | collective-permute-done | bytes 1179680 | tf_op jit(solution)/shard_map/ppermute | solution.py:615
  96.9 25.8 %collective-permute-done.3.refs_2_ = bf16[4,144,1024]{2,1,0:T(8,128)(2,1)} collective-permute-done((bf16[4,144,1024]{2,1,0:T(8,128)(2,1)S(1)}, bf16[4,144,1024]{2,1,0:T(8,128)(2,1)}, u32[]{:S(2)}, u32[]{:S(2)}) %collective-permute-start.3) | collective-permute-done | bytes 1179680 | tf_op jit(solution)/shard_map/ppermute | solution.py:615
  123.2 4.1 copy_convert_fusion
  127.4 4.4 all-to-all-start.2
  133.5 7.3 shard_map.314
  143.0 25.6 %shard_map.315 = (bf16[768,1024]{1,0:T(8,128)(2,1)}, bf16[512,1024]{1,0:T(8,128)(2,1)S(1)}, bf16[512,1024]{1,0:T(8,128)(2,1)S(1)}, bf16[512,1024]{1,0:T(8,128)(2...) custom-call(s32[1,1]{1,0:T(1,128)} %bitcast.112.length, ...), custom_call_target="tpu_custom_call" | custom-call | flops 1000000 | bytes 100000 | tf_op jit(solution)/shard_map/pallas_call | solution.py:122
  174.3 4.4 all-to-all-start.1
  181.6 25.5 %shard_map.317 = (bf16[768,1024]{1,0:T(8,128)(2,1)}, bf16[512,1024]{1,0:T(8,128)(2,1)S(1)}, bf16[512,1024]{1,0:T(8,128)(2,1)S(1)}, bf16[512,1024]{1,0:T(8,128)(2...) custom-call(s32[1,1]{1,0:T(1,128)} %bitcast.111.length, ...), custom_call_target="tpu_custom_call" | custom-call | flops 1000000 | bytes 100000 | tf_op jit(solution)/shard_map/pallas_call | solution.py:122
  212.7 4.3 all-to-all-start.3
  218.4 5.5 shard_map.316.refs_0_
  223.9 3.4 collective-permute-start.9
  231.9 6.2 all-to-all-done.3
  240.8 5.4 shard_map.318.refs_0_
  246.2 3.4 collective-permute-start.16
  249.6 99.1 %collective-permute-done.9 = bf16[2,384,1024]{2,1,0:T(8,128)(2,1)S(1)} collective-permute-done((bf16[2,384,1024]{2,1,0:T(8,128)(2,1)}, bf16[2,384,1024]{2,1,0:T(8,128)(2,1)S(1)}, u32[]{:S(2)}, u32[]{:S(2)}) %collective-permute-start.9) | collective-permute-done | bytes 1572896 | tf_op jit(solution)/shard_map/ppermute | solution.py:720
  348.7 33.5 %collective-permute-done.10.refs_7_.refs_9_ = bf16[4,1024,1024]{2,1,0:T(8,128)(2,1)} collective-permute-done((bf16[4,1024,1024]{2,1,0:T(8,128)(2,1)}, bf16[4,1024,1024]{2,1,0:T(8,128)(2,1)}, u32[]{:S(2)}, u32[]{:S(2)}) %collective-permute-start.10) | collective-permute-done | bytes 8388640 | tf_op jit(solution)/shard_map/ppermute | solution.py:687
  382.2 53.6 %shard_map.319 = (bf16[2,384,1024]{2,1,0:T(8,128)(2,1)}, bf16[2,384,1024]{2,1,0:T(8,128)(2,1)}, bf16[2,384,1024]{2,1,0:T(8,128)(2,1)}, bf16[2,384,1024]{2,1,0:T(...) custom-call(s32[1]{0:T(128)} %bitcast.4._, ...), custom_call_target="tpu_custom_call" | custom-call | flops 1000000 | bytes 100000 | tf_op jit(solution)/shard_map/pallas_call | solution.py:576
  441.6 64.3 %shard_map.322 = (bf16[2,384,1024]{2,1,0:T(8,128)(2,1)}, bf16[2,384,1024]{2,1,0:T(8,128)(2,1)}, bf16[2,384,1024]{2,1,0:T(8,128)(2,1)}, bf16[2,384,1024]{2,1,0:T(...) custom-call(s32[1]{0:T(128)} %bitcast.4._, ...), custom_call_target="tpu_custom_call" | custom-call | flops 1000000 | bytes 100000 | tf_op jit(solution)/shard_map/pallas_call | solution.py:576
  507.4 8.0 shard_map.320
  518.3 5.0 all-to-all-start.4
  525.7 3.3 pad_maximum_fusion.1
  529.0 15.3 %all-to-all-done.4 = bf16[2,8,48,1024]{3,2,0,1:T(8,128)(2,1)S(1)} async-done(((bf16[2,8,48,1024]{3,2,0,1:T(8,128)(2,1)}), bf16[2,8,48,1024]{3,2,0,1:T(8,128)(2,1)S(1)}, u32[]{:S(2)}, u32[]{:S(2)}) %all-to-all-start.4) | async-done | bytes 1572896 | tf_op jit(solution)/shard_map/all_to_all | solution.py:752
  545.4 46.2 %shard_map.321 = (bf16[768,1024]{1,0:T(8,128)(2,1)}, bf16[16,32,1024]{2,1,0:T(8,128)(2,1)}, bf16[16,32,1024]{2,1,0:T(8,128)(2,1)}, bf16[16,32,1024]{2,1,0:T(8,12...) custom-call(s32[1,1]{1,0:T(1,128)} %bitcast.112.length, ...), custom_call_target="tpu_custom_call" | custom-call | flops 1000000 | bytes 100000 | tf_op jit(solution)/shard_map/pallas_call | solution.py:261
  591.7 8.3 shard_map.323
  600.0 3.1 copy.126
  603.1 3.9 all-to-all-start.5
  611.1 16.8 %all-to-all-done.5 = bf16[2,8,48,1024]{3,2,0,1:T(8,128)(2,1)S(1)} async-done(((bf16[2,8,48,1024]{3,2,0,1:T(8,128)(2,1)}), bf16[2,8,48,1024]{3,2,0,1:T(8,128)(2,1)S(1)}, u32[]{:S(2)}, u32[]{:S(2)}) %all-to-all-start.5) | async-done | bytes 1572896 | tf_op jit(solution)/shard_map/all_to_all | solution.py:752
  629.0 45.8 %shard_map.324 = (bf16[768,1024]{1,0:T(8,128)(2,1)}, bf16[16,32,1024]{2,1,0:T(8,128)(2,1)}, bf16[16,32,1024]{2,1,0:T(8,128)(2,1)}, bf16[16,32,1024]{2,1,0:T(8,12...) custom-call(s32[1,1]{1,0:T(1,128)} %bitcast.111.length, ...), custom_call_target="tpu_custom_call" | custom-call | flops 1000000 | bytes 100000 | tf_op jit(solution)/shard_map/pallas_call | solution.py:261
  677.3 4.3 all-to-all-start.6
  684.8 8.6 %shard_map.325 = (bf16[528,1024]{1,0:T(8,128)(2,1)}, bf16[528,1024]{1,0:T(8,128)(2,1)}, bf16[528,1024]{1,0:T(8,128)(2,1)}, bf16[528,1024]{1,0:T(8,128)(2,1)}) custom-call(s32[1,1]{1,0:T(1,128)} %bitcast.1.place, bf16[16,32,1024]{2,1,0:T(8,128)(2,1)S(1)} %copy-done.13, bf16[16,32,1024]{2,1,0:T(8,128)(2,1)S(1)} %copy-done.14, ...), custom_call_target="tpu_custom_call" | custom-call | flops 1000000 | bytes 100000 | tf_op jit(solution)/shard_map/pallas_call | solution.py:333
  696.9 6.3 all-to-all-done.6
  703.2 4.6 all-to-all-start.7
  707.8 4.1 copy.129
  716.6 8.7 %collective-permute-done.22.refs_0_ = bf16[528,1024]{1,0:T(8,128)(2,1)S(1)} collective-permute-done((bf16[528,1024]{1,0:T(8,128)(2,1)}, bf16[528,1024]{1,0:T(8,128)(2,1)S(1)}, u32[]{:S(2)}, u32[]{:S(2)}) %collective-permute-start.22) | collective-permute-done | bytes 1081376 | tf_op jit(solution)/shard_map/ppermute | solution.py:770
  725.3 24.2 %collective-permute-done.24.refs_2_ = bf16[528,1024]{1,0:T(8,128)(2,1)} collective-permute-done((bf16[528,1024]{1,0:T(8,128)(2,1)}, bf16[528,1024]{1,0:T(8,128)(2,1)}, u32[]{:S(2)}, u32[]{:S(2)}) %collective-permute-start.24) | collective-permute-done | bytes 1081376 | tf_op jit(solution)/shard_map/ppermute | solution.py:770
  757.4 8.6 %all-to-all-done.7 = bf16[16,48,1024]{2,1,0:T(8,128)(2,1)} async-done(((bf16[16,48,1024]{2,1,0:T(8,128)(2,1)}), bf16[16,48,1024]{2,1,0:T(8,128)(2,1)}, u32[]{:S(2)}, u32[]{:S(2)}) %all-to-all-start.7) | async-done | bytes 1572896 | tf_op jit(solution)/shard_map/all_to_all | solution.py:758
  766.0 3.5 copy.134
  769.5 41.0 %collective-permute-done.25 = bf16[272,1024]{1,0:T(8,128)(2,1)} collective-permute-done((bf16[272,1024]{1,0:T(8,128)(2,1)}, bf16[272,1024]{1,0:T(8,128)(2,1)}, u32[]{:S(2)}, u32[]{:S(2)}) %collective-permute-start.25) | collective-permute-done | bytes 557088 | tf_op jit(solution)/shard_map/ppermute | solution.py:772
  812.8 5.6 fusion.9
  820.4 4.6 collective-permute-start.26
  828.3 15.6 %shard_map.327 = (f32[2,1024,1024]{2,1,0:T(8,128)}, f32[2,1024,1024]{2,1,0:T(8,128)}) custom-call(f32[2,1024,1024]{2,1,0:T(8,128)} %get-tuple-element.170.a, f32[2,1024,1024]{2,1,0:T(8,128)} %get-tuple-element.171.c, bf16[2,2,1024,1024]{3,2,1,0:T(8,128)(2,1)} %collective-permute-done.27.got), custom_call_target="tpu_custom_call", output_to_operand_aliasing={{0}: (0, {}), {1}: (1, {})} | custom-call | flops 1000000 | bytes 100000 | tf_op jit(solution)/shard_map/pallas_call | solution.py:389
  (265 shorter events, 88.4 us)
Async XLA Ops:
  13.5 26.3 %all-to-all-start = ((bf16[2,8,48,1024]{3,2,0,1:T(8,128)(2,1)}), bf16[2,8,48,1024]{3,2,0,1:T(8,128)(2,1)S(1)}, u32[]{:S(2)}, u32[]{:S(2)}) async-start(bf16[2,8,48,1024]{3,2,0,1:T(8,128)(2,1)} %get-tuple-element.189), calls=%async_computation | async-start | bytes 3145728 | tf_op jit(solution)/shard_map/all_to_all | solution.py:679
  18.8 227.4 %all-gather.7.cloned.1.call-start = ((), (), s32[]{:S(2)}) async-start(), calls=%async_computation.8 | async-start | bytes 9437184 | tf_op jit(solution)/shard_map/all_gather | solution.py:605
  19.4 9.4 %collective-permute-start = (bf16[1,144,1024]{2,1,0:T(8,128)(2,1)S(1)}, bf16[1,144,1024]{2,1,0:T(8,128)(2,1)S(1)}, u32[]{:S(2)}, u32[]{:S(2)}) collective-permute-start(bf16[1,144,1024]{2,1,0:T(8,128)(2,1)S(1)} %bitcast.225), channel_id=1, source_target_pairs={{0,1},{1,0},{2,3},{3,2},{4,5},{5,4},{6,7},{7,6},{8,9},{9,8},{10,11... | collective-permute-start | bytes 884744 | tf_op jit(solution)/shard_map/ppermute | solution.py:611
  39.8 25.8 %collective-permute-start.1 = (bf16[2,144,1024]{2,1,0:T(8,128)(2,1)S(1)}, bf16[2,144,1024]{2,1,0:T(8,128)(2,1)S(1)}, u32[]{:S(2)}, u32[]{:S(2)}) collective-permute-start(bf16[2,144,1024]{2,1,0:T(8,128)(2,1)S(1)} %pad_maximum_fusion.4), channel_id=1, source_target_pairs={{0,2},{1,3},{2,0},{3,1},{4,6},{5,7},{6,4},{7,5},{8,10},{9,11},{10,... | collective-permute-start | bytes 1769480 | tf_op jit(solution)/shard_map/ppermute | solution.py:611
  65.7 316.5 %collective-permute-start.10 = (bf16[4,1024,1024]{2,1,0:T(8,128)(2,1)}, bf16[4,1024,1024]{2,1,0:T(8,128)(2,1)}, u32[]{:S(2)}, u32[]{:S(2)}) collective-permute-start(bf16[4,1024,1024]{2,1,0:T(8,128)(2,1)} %pad_maximum_fusion), channel_id=1, source_target_pairs={{0,1},{1,0},{2,3},{3,2},{4,5},{5,4},{6,7},{7,6},{8,9},{9,8},{10,11... | collective-permute-start | bytes 25165832 | tf_op jit(solution)/shard_map/ppermute | solution.py:687
  66.4 30.4 %collective-permute-start.2 = (bf16[4,144,1024]{2,1,0:T(8,128)(2,1)S(1)}, bf16[4,144,1024]{2,1,0:T(8,128)(2,1)}, u32[]{:S(2)}, u32[]{:S(2)}) collective-permute-start(bf16[4,144,1024]{2,1,0:T(8,128)(2,1)S(1)} %constant_dynamic-update-slice_fusion.5.refs_0_), channel_id=1, source_target_pairs={{0,8},{4,12},{8,0},{12,4},{16,24},{20,28},{24,16},{28,20},{1,9},{5... | collective-permute-start | bytes 3538952 | tf_op jit(solution)/shard_map/ppermute | solution.py:615
  70.0 52.7 %collective-permute-start.3 = (bf16[4,144,1024]{2,1,0:T(8,128)(2,1)S(1)}, bf16[4,144,1024]{2,1,0:T(8,128)(2,1)}, u32[]{:S(2)}, u32[]{:S(2)}) collective-permute-start(bf16[4,144,1024]{2,1,0:T(8,128)(2,1)S(1)} %constant_dynamic-update-slice_fusion.5.refs_0_), channel_id=1, source_target_pairs={{0,16},{4,20},{8,24},{12,28},{16,0},{20,4},{24,8},{28,12},{1,17},{... | collective-permute-start | bytes 3538952 | tf_op jit(solution)/shard_map/ppermute | solution.py:615
  70.3 52.4 %collective-permute-start.4 = (bf16[4,144,1024]{2,1,0:T(8,128)(2,1)S(1)}, bf16[4,144,1024]{2,1,0:T(8,128)(2,1)}, u32[]{:S(2)}, u32[]{:S(2)}) collective-permute-start(bf16[4,144,1024]{2,1,0:T(8,128)(2,1)S(1)} %constant_dynamic-update-slice_fusion.5.refs_0_), channel_id=1, source_target_pairs={{0,24},{4,28},{8,16},{12,20},{16,8},{20,12},{24,0},{28,4},{1,25},{... | collective-permute-start | bytes 3538952 | tf_op jit(solution)/shard_map/ppermute | solution.py:615
  71.5 62.0 %collective-permute-start.5 = (bf16[4,144,1024]{2,1,0:T(8,128)(2,1)S(1)}, bf16[4,144,1024]{2,1,0:T(8,128)(2,1)}, u32[]{:S(2)}, u32[]{:S(2)}) collective-permute-start(bf16[4,144,1024]{2,1,0:T(8,128)(2,1)S(1)} %constant_dynamic-update-slice_fusion.5.refs_0_), channel_id=1, source_target_pairs={{0,4},{4,0},{8,12},{12,8},{16,20},{20,16},{24,28},{28,24},{1,5},{5... | collective-permute-start | bytes 3538952 | tf_op jit(solution)/shard_map/ppermute | solution.py:616
  96.9 36.6 %collective-permute-start.6 = (bf16[4,144,1024]{2,1,0:T(8,128)(2,1)}, bf16[4,144,1024]{2,1,0:T(8,128)(2,1)}, u32[]{:S(2)}, u32[]{:S(2)}) collective-permute-start(bf16[4,144,1024]{2,1,0:T(8,128)(2,1)} %collective-permute-done.2.refs_1_), channel_id=1, source_target_pairs={{0,4},{4,0},{8,12},{12,8},{16,20},{20,16},{24,28},{28,24},{1,5},{5... | collective-permute-start | bytes 3538952 | tf_op jit(solution)/shard_map/ppermute | solution.py:616
  122.7 10.8 %collective-permute-start.7 = (bf16[4,144,1024]{2,1,0:T(8,128)(2,1)}, bf16[4,144,1024]{2,1,0:T(8,128)(2,1)}, u32[]{:S(2)}, u32[]{:S(2)}) collective-permute-start(bf16[4,144,1024]{2,1,0:T(8,128)(2,1)} %collective-permute-done.3.refs_2_), channel_id=1, source_target_pairs={{0,4},{4,0},{8,12},{12,8},{16,20},{20,16},{24,28},{28,24},{1,5},{5... | collective-permute-start | bytes 3538952 | tf_op jit(solution)/shard_map/ppermute | solution.py:616
  122.7 10.8 %collective-permute-start.8 = (bf16[4,144,1024]{2,1,0:T(8,128)(2,1)}, bf16[4,144,1024]{2,1,0:T(8,128)(2,1)}, u32[]{:S(2)}, u32[]{:S(2)}) collective-permute-start(bf16[4,144,1024]{2,1,0:T(8,128)(2,1)} %collective-permute-done.4.refs_3_), channel_id=1, source_target_pairs={{0,4},{4,0},{8,12},{12,8},{16,20},{20,16},{24,28},{28,24},{1,5},{5... | collective-permute-start | bytes 3538952 | tf_op jit(solution)/shard_map/ppermute | solution.py:616
  127.4 46.9 %all-to-all-start.2 = ((bf16[2,8,48,1024]{3,2,0,1:T(8,128)(2,1)}), bf16[2,8,48,1024]{3,2,0,1:T(8,128)(2,1)}, u32[]{:S(2)}, u32[]{:S(2)}) async-start(bf16[2,8,48,1024]{3,2,0,1:T(8,128)(2,1)} %get-tuple-element.191), calls=%async_computation.2 | async-start | bytes 3145728 | tf_op jit(solution)/shard_map/all_to_all | solution.py:679
  132.6 48.9 %copy-start.22 = (s32[1,512]{1,0:T(1,128)}, s32[1,512]{1,0:T(1,128)S(1)}, u32[]{:S(2)}) copy-start(s32[1,512]{1,0:T(1,128)S(1)} %get-tuple-element.216.row) | copy-start | bytes 6148
  143.0 38.5 %copy-start.19 = (f32[8,1024]{1,0:T(8,128)}, f32[8,1024]{1,0:T(8,128)S(1)}, u32[]{:S(2)}) copy-start(f32[8,1024]{1,0:T(8,128)S(1)} %stack.30.small) | copy-start | bytes 98308
  174.3 38.4 %all-to-all-start.1 = ((bf16[16,48,1024]{2,1,0:T(8,128)(2,1)}), bf16[16,48,1024]{2,1,0:T(8,128)(2,1)S(1)}, u32[]{:S(2)}, u32[]{:S(2)}) async-start(bf16[16,48,1024]{2,1,0:T(8,128)(2,1)} %bitcast.217), calls=%async_computation.1 | async-start | bytes 3145728 | tf_op jit(solution)/shard_map/all_to_all | solution.py:715
  178.9 28.2 %copy-start.1 = (s32[512,1]{1,0:T(8,128)}, s32[512,1]{1,0:T(8,128)S(1)}, u32[]{:S(2)}) copy-start(s32[512,1]{1,0:T(8,128)S(1)} %copy.115.column) | copy-start | bytes 6148
  212.7 25.3 %all-to-all-start.3 = ((bf16[16,48,1024]{2,1,0:T(8,128)(2,1)}), bf16[16,48,1024]{2,1,0:T(8,128)(2,1)}, u32[]{:S(2)}, u32[]{:S(2)}) async-start(bf16[16,48,1024]{2,1,0:T(8,128)(2,1)} %bitcast.218), calls=%async_computation.3 | async-start | bytes 3145728 | tf_op jit(solution)/shard_map/all_to_all | solution.py:715
  217.0 374.6 %all-gather.9.cloned.1.call-start = ((), (), s32[]{:S(2)}) async-start(), calls=%async_computation.9 | async-start | bytes 4718592 | tf_op jit(solution)/shard_map/all_gather | solution.py:605
  223.9 124.9 %collective-permute-start.9 = (bf16[2,384,1024]{2,1,0:T(8,128)(2,1)}, bf16[2,384,1024]{2,1,0:T(8,128)(2,1)S(1)}, u32[]{:S(2)}, u32[]{:S(2)}) collective-permute-start(bf16[2,384,1024]{2,1,0:T(8,128)(2,1)} %shard_map.316.refs_0_), channel_id=1, source_target_pairs={{0,2},{1,3},{2,0},{3,1},{4,6},{5,7},{6,4},{7,5},{8,10},{9,11},{10,... | collective-permute-start | bytes 4718600 | tf_op jit(solution)/shard_map/ppermute | solution.py:720
  246.2 194.2 %collective-permute-start.16 = (bf16[2,384,1024]{2,1,0:T(8,128)(2,1)}, bf16[2,384,1024]{2,1,0:T(8,128)(2,1)S(1)}, u32[]{:S(2)}, u32[]{:S(2)}) collective-permute-start(bf16[2,384,1024]{2,1,0:T(8,128)(2,1)} %shard_map.318.refs_0_), channel_id=1, source_target_pairs={{0,2},{1,3},{2,0},{3,1},{4,6},{5,7},{6,4},{7,5},{8,10},{9,11},{10,... | collective-permute-start | bytes 4718600 | tf_op jit(solution)/shard_map/ppermute | solution.py:723
  348.7 33.5 %copy-start.36 = (bf16[2,384,1024]{2,1,0:T(8,128)(2,1)}, bf16[2,384,1024]{2,1,0:T(8,128)(2,1)S(1)}, u32[]{:S(2)}) copy-start(bf16[2,384,1024]{2,1,0:T(8,128)(2,1)S(1)} %collective-permute-done.9) | copy-start | bytes 4718596
  435.8 70.4 %collective-permute-start.11 = (bf16[2,384,1024]{2,1,0:T(8,128)(2,1)}, bf16[2,384,1024]{2,1,0:T(8,128)(2,1)S(1)}, u32[]{:S(2)}, u32[]{:S(2)}) collective-permute-start(bf16[2,384,1024]{2,1,0:T(8,128)(2,1)} %get-tuple-element.105), channel_id=1, source_target_pairs={{0,2},{1,3},{2,0},{3,1},{4,6},{5,7},{6,4},{7,5},{8,10},{9,11},{10,... | collective-permute-start | bytes 4718600 | tf_op jit(solution)/shard_map/ppermute | solution.py:734
  518.3 26.0 %all-to-all-start.4 = ((bf16[2,8,48,1024]{3,2,0,1:T(8,128)(2,1)}), bf16[2,8,48,1024]{3,2,0,1:T(8,128)(2,1)S(1)}, u32[]{:S(2)}, u32[]{:S(2)}) async-start(bf16[2,8,48,1024]{3,2,0,1:T(8,128)(2,1)} %copy.121), calls=%async_computation.4 | async-start | bytes 3145728 | tf_op jit(solution)/shard_map/all_to_all | solution.py:752
  523.3 289.5 %all-gather.11.cloned.1.call-start = ((), (), s32[]{:S(2)}) async-start(), calls=%async_computation.10 | async-start | bytes 9437184 | tf_op jit(solution)/shard_map/all_gather | solution.py:605
  523.3 305.0 %collective-permute-start.27 = (bf16[2,2,1024,1024]{3,2,1,0:T(8,128)(2,1)}, bf16[2,2,1024,1024]{3,2,1,0:T(8,128)(2,1)}, u32[]{:S(2)}, u32[]{:S(2)}) collective-permute-start(bf16[2,2,1024,1024]{3,2,1,0:T(8,128)(2,1)} %get-tuple-element.172), channel_id=1, source_target_pairs={{0,1},{1,0},{2,3},{3,2},{4,5},{5,4},{6,7},{7,6},{8,9},{9,8},{10,11... | collective-permute-start | bytes 25165832 | tf_op jit(solution)/shard_map/ppermute | solution.py:741
  603.1 24.8 %all-to-all-start.5 = ((bf16[2,8,48,1024]{3,2,0,1:T(8,128)(2,1)}), bf16[2,8,48,1024]{3,2,0,1:T(8,128)(2,1)S(1)}, u32[]{:S(2)}, u32[]{:S(2)}) async-start(bf16[2,8,48,1024]{3,2,0,1:T(8,128)(2,1)} %copy.126), calls=%async_computation.5 | async-start | bytes 3145728 | tf_op jit(solution)/shard_map/all_to_all | solution.py:752
  606.9 68.9 %collective-permute-start.12 = (bf16[16,32,1024]{2,1,0:T(8,128)(2,1)}, bf16[16,32,1024]{2,1,0:T(8,128)(2,1)}, u32[]{:S(2)}, u32[]{:S(2)}) collective-permute-start(bf16[16,32,1024]{2,1,0:T(8,128)(2,1)} %get-tuple-element.117), channel_id=1, source_target_pairs={{0,4},{4,0},{8,12},{12,8},{16,20},{20,16},{24,28},{28,24},{1,5},{5... | collective-permute-start | bytes 3145736 | tf_op jit(solution)/shard_map/ppermute | solution.py:765
  607.4 68.5 %collective-permute-start.13 = (bf16[16,32,1024]{2,1,0:T(8,128)(2,1)}, bf16[16,32,1024]{2,1,0:T(8,128)(2,1)}, u32[]{:S(2)}, u32[]{:S(2)}) collective-permute-start(bf16[16,32,1024]{2,1,0:T(8,128)(2,1)} %get-tuple-element.118), channel_id=1, source_target_pairs={{0,4},{4,0},{8,12},{12,8},{16,20},{20,16},{24,28},{28,24},{1,5},{5... | collective-permute-start | bytes 3145736 | tf_op jit(solution)/shard_map/ppermute | solution.py:765
  607.5 68.9 %collective-permute-start.14 = (bf16[16,32,1024]{2,1,0:T(8,128)(2,1)}, bf16[16,32,1024]{2,1,0:T(8,128)(2,1)}, u32[]{:S(2)}, u32[]{:S(2)}) collective-permute-start(bf16[16,32,1024]{2,1,0:T(8,128)(2,1)} %get-tuple-element.119), channel_id=1, source_target_pairs={{0,4},{4,0},{8,12},{12,8},{16,20},{20,16},{24,28},{28,24},{1,5},{5... | collective-permute-start | bytes 3145736 | tf_op jit(solution)/shard_map/ppermute | solution.py:765
  608.0 68.6 %collective-permute-start.15 = (bf16[16,32,1024]{2,1,0:T(8,128)(2,1)}, bf16[16,32,1024]{2,1,0:T(8,128)(2,1)}, u32[]{:S(2)}, u32[]{:S(2)}) collective-permute-start(bf16[16,32,1024]{2,1,0:T(8,128)(2,1)} %get-tuple-element.120), channel_id=1, source_target_pairs={{0,4},{4,0},{8,12},{12,8},{16,20},{20,16},{24,28},{28,24},{1,5},{5... | collective-permute-start | bytes 3145736 | tf_op jit(solution)/shard_map/ppermute | solution.py:765
  629.0 45.9 %copy-start.47 = (f32[8,1024]{1,0:T(8,128)S(1)}, f32[8,1024]{1,0:T(8,128)}, u32[]{:S(2)}) copy-start(f32[8,1024]{1,0:T(8,128)} %get-tuple-element.149) | copy-start | bytes 98308
  675.9 1.3 collective-permute-start.21
  676.0 5.7 collective-permute-start.17
  676.5 5.2 collective-permute-start.18
  676.5 5.5 collective-permute-start.19
  677.1 6.4 collective-permute-start.20
  677.3 25.9 %all-to-all-start.6 = ((bf16[16,48,1024]{2,1,0:T(8,128)(2,1)}), bf16[16,48,1024]{2,1,0:T(8,128)(2,1)}, u32[]{:S(2)}, u32[]{:S(2)}) async-start(bf16[16,48,1024]{2,1,0:T(8,128)(2,1)} %bitcast.216), calls=%async_computation.6 | async-start | bytes 3145728 | tf_op jit(solution)/shard_map/all_to_all | solution.py:758
  693.4 31.9 %collective-permute-start.22 = (bf16[528,1024]{1,0:T(8,128)(2,1)}, bf16[528,1024]{1,0:T(8,128)(2,1)S(1)}, u32[]{:S(2)}, u32[]{:S(2)}) collective-permute-start(bf16[528,1024]{1,0:T(8,128)(2,1)} %get-tuple-element.154), channel_id=1, source_target_pairs={{0,8},{4,12},{8,0},{12,4},{16,24},{20,28},{24,16},{28,20},{1,9},{5... | collective-permute-start | bytes 3244040 | tf_op jit(solution)/shard_map/ppermute | solution.py:770
  693.9 31.4 %collective-permute-start.23 = (bf16[528,1024]{1,0:T(8,128)(2,1)}, bf16[528,1024]{1,0:T(8,128)(2,1)S(1)}, u32[]{:S(2)}, u32[]{:S(2)}) collective-permute-start(bf16[528,1024]{1,0:T(8,128)(2,1)} %get-tuple-element.155), channel_id=1, source_target_pairs={{0,16},{4,20},{8,24},{12,28},{16,0},{20,4},{24,8},{28,12},{1,17},{... | collective-permute-start | bytes 3244040 | tf_op jit(solution)/shard_map/ppermute | solution.py:770
  694.9 54.7 %collective-permute-start.24 = (bf16[528,1024]{1,0:T(8,128)(2,1)}, bf16[528,1024]{1,0:T(8,128)(2,1)}, u32[]{:S(2)}, u32[]{:S(2)}) collective-permute-start(bf16[528,1024]{1,0:T(8,128)(2,1)} %get-tuple-element.156), channel_id=1, source_target_pairs={{0,24},{4,28},{8,16},{12,20},{16,8},{20,12},{24,0},{28,4},{1,25},{... | collective-permute-start | bytes 3244040 | tf_op jit(solution)/shard_map/ppermute | solution.py:770
  703.2 62.8 %all-to-all-start.7 = ((bf16[16,48,1024]{2,1,0:T(8,128)(2,1)}), bf16[16,48,1024]{2,1,0:T(8,128)(2,1)}, u32[]{:S(2)}, u32[]{:S(2)}) async-start(bf16[16,48,1024]{2,1,0:T(8,128)(2,1)} %bitcast.215), calls=%async_computation.7 | async-start | bytes 3145728 | tf_op jit(solution)/shard_map/all_to_all | solution.py:758
  711.9 37.6 %copy-start.2 = (bf16[528,1024]{1,0:T(8,128)(2,1)S(1)}, bf16[528,1024]{1,0:T(8,128)(2,1)}, u32[]{:S(2)}) copy-start(bf16[528,1024]{1,0:T(8,128)(2,1)} %get-tuple-element.153.first) | copy-start | bytes 3244036
  753.0 57.5 %collective-permute-start.25 = (bf16[272,1024]{1,0:T(8,128)(2,1)}, bf16[272,1024]{1,0:T(8,128)(2,1)}, u32[]{:S(2)}, u32[]{:S(2)}) collective-permute-start(bf16[272,1024]{1,0:T(8,128)(2,1)} %get-tuple-element.158), channel_id=1, source_target_pairs={{0,2},{1,3},{2,0},{3,1},{4,6},{5,7},{6,4},{7,5},{8,10},{9,11},{10,... | collective-permute-start | bytes 1671176 | tf_op jit(solution)/shard_map/ppermute | solution.py:772
  766.0 44.5 %copy-start.18 = (f32[256,1024]{1,0:T(8,128)S(1)}, f32[256,1024]{1,0:T(8,128)}, u32[]{:S(2)}) copy-start(f32[256,1024]{1,0:T(8,128)} %copy-done.17) | copy-start | bytes 3145732
  769.5 43.3 %copy-start.24 = (bf16[2,8,48,1024]{3,2,1,0:T(8,128)(2,1)S(1)}, bf16[2,8,48,1024]{3,2,1,0:T(8,128)(2,1)}, u32[]{:S(2)}) copy-start(bf16[2,8,48,1024]{3,2,1,0:T(8,128)(2,1)} %copy.116) | copy-start | bytes 4718596
  769.5 43.3 %copy-start.25 = (bf16[2,8,48,1024]{3,2,1,0:T(8,128)(2,1)S(1)}, bf16[2,8,48,1024]{3,2,1,0:T(8,128)(2,1)}, u32[]{:S(2)}) copy-start(bf16[2,8,48,1024]{3,2,1,0:T(8,128)(2,1)} %copy.112) | copy-start | bytes 4718596
  820.4 23.5 %collective-permute-start.26 = (bf16[148,1024]{1,0:T(8,128)(2,1)S(1)}, bf16[148,1024]{1,0:T(8,128)(2,1)S(1)}, u32[]{:S(2)}, u32[]{:S(2)}) collective-permute-start(bf16[148,1024]{1,0:T(8,128)(2,1)S(1)} %pad_maximum_fusion.5), channel_id=1, source_target_pairs={{0,1},{1,0},{2,3},{3,2},{4,5},{5,4},{6,7},{7,6},{8,9},{9,8},{10,11... | collective-permute-start | bytes 909320 | tf_op jit(solution)/shard_map/ppermute | solution.py:789
  (50 other events, 254.5 us)
Sparse Core Ops, SparseCore 0:
  71.6 148.3 all-gather.6
  506.4 81.9 all-gather.8
  591.8 147.1 all-gather.10

commit v5 on v4

--- a/solution.py
+++ b/solution.py
@@ -732,6 +732,7 @@
         )
         before = ffn[t][4:]
     gx_far = [lax.ppermute(ffn[0][3], "fsdp", far)[None]]
+    out_far = [both_groups(ffn[t][1], n_f) for t in range(mb - 1)]
     for t in range(1, mb):
         gx_far.append(both_groups(after(ffn[t][3], gx_far[t - 1]), n_f))
     dwi_own, dwo_own, dw_near, db, dbo = before
@@ -743,9 +744,8 @@
     for t in range(mb):
         got = gx_far[t]
         if t == mb - 1:
-            outs = jnp.stack([ffn[i][1] for i in range(mb)])
-            got, outs, placed_back = lax.optimization_barrier((got, outs, placed_back))
-            out_far = both_groups(outs, n_f)
+            got, outs, placed_back = lax.optimization_barrier((got, ffn[t][1], placed_back))
+            out_far.append(both_groups(outs, n_f))
         grad_mixed, to_send, norm_sums = mixed_back(
             t, other, block_rows, back_rows[t], ffn[t][2], got, cot, fill_own[t], small[5:6]
         )
@@ -771,10 +771,9 @@
     keep, give, sums = add_plane((fi // 2) % 2, blocks[0], got)
     far_got = lax.ppermute(give, "fsdp", far)
     outputs = []
-    far_outs = pick(out_far, other[0], 0)
     for t in range(mb):
         mixed = block_rows[t].astype(F32) + back_rows[t].astype(F32)
-        ffn_out = ffn[t][0].astype(F32) + far_outs[t].astype(F32) + bias_out[:, None, :]
+        ffn_out = ffn[t][0].astype(F32) + pick(out_far[t], other[0], 0).astype(F32) + bias_out[:, None, :]
         outputs.append(
             ((mixed + ffn_out) * fill_own[t]).astype(BF).reshape(le, 1, sources, cap, width)
         )

time: 864 us -> 844 us (0.977)
  waiting for transfers between devices: 348 us -> 338 us
    all_to_all x2, waiting for transfers between devices: 14.9 us -> 0.01 us  [body(): lax.all_to_all(placed_back.reshape(experts, cap, width), 'exp', split_axi...]
    ppermute x1, waiting for transfers between devices: 41 us -> 31.7 us  [body(): far_got = lax.ppermute(give, 'fsdp', far)]
    unnamed x130 -> x122, local copies, waits for them, and re-layouts: 21.3 us -> 18.3 us
  transfers between devices with their start and end apart: 39 -> 40, of which waited for: 19 -> 17; matrix products, arithmetic and copies ran while one was open for 8% -> 8% of each run, Pallas kernels for 38% -> 38%
where the time goes in v5:
time: 844 us; the launch traced here: 834 us
  waiting for transfers between devices  338 us (40%)
  Pallas kernels  321 us (38%)
  starting transfers between devices  70.2 us (8%)
  local copies, waits for them, and re-layouts  58.3 us (7%)
  other arithmetic  31.3 us (4%)
  between operations  15.2 us (2%)
    pallas_call x2, Pallas kernels, expert_step(): pl.pallas_call(functools.partial(expert_kernel, first, tiles), grid_spec=...  118 us
    ppermute x1, waiting for transfers between devices, body(): normed_far = [lax.ppermute(normed_two[0], 'fsdp', far)[None]]  99.1 us
    pallas_call x2, Pallas kernels, attention_backward(): pl.pallas_call(functools.partial(backward_kernel, groups), in_specs=[sm,...  91.8 us
    ppermute x3, waiting for transfers between devices, gather_all(): lax.ppermute(block, 'exp', crossed(n_exp, 2 * k))  51.2 us
    pallas_call x2, Pallas kernels, attention_forward(): pl.pallas_call(forward_kernel, in_specs=[pl.BlockSpec(memory_space=pltpu....  51 us
    all_to_all x2, waiting for transfers between devices, body(): lax.all_to_all(to_send.reshape(le, sources, cap, width), 'exp', split_axi...  40.8 us
    ppermute x3, waiting for transfers between devices, body(): lax.ppermute(blocks[k], 'exp', crossed(n_exp, 2 * k))  38.1 us
    ppermute x1, waiting for transfers between devices, body(): lax.ppermute(after(jnp.concatenate([expert_in, expert_out]), ready), 'fsd...  33.5 us
  transfers between devices with their start and end apart: 40, of which 17 were waited for; matrix products, arithmetic and copies ran while one was open for 8% of the time, Pallas kernels for 38%

profile of v5, /device:TPU:0, one launch (start us, length us, event | category | flops | bytes accessed | tf_op | source)
XLA Modules:
  0.0 834.0 jit_solution(7129952798813810015)
XLA Ops:
  7.2 3.4 fusion.19
  10.6 2.7 copy_convert_fusion.1
  13.5 5.3 all-to-all-start
  21.0 7.8 collective-permute-done
  28.9 10.9 %all-to-all-done = bf16[2,8,48,1024]{3,2,0,1:T(8,128)(2,1)S(1)} async-done(((bf16[2,8,48,1024]{3,2,0,1:T(8,128)(2,1)}), bf16[2,8,48,1024]{3,2,0,1:T(8,128)(2,1)S(1)}, u32[]{:S(2)}, u32[]{:S(2)}) %all-to-all-start) | async-done | bytes 1572896 | tf_op jit(solution)/shard_map/all_to_all | solution.py:679
  42.4 7.6 pad_maximum_fusion
  50.0 15.6 %collective-permute-done.1 = bf16[2,144,1024]{2,1,0:T(8,128)(2,1)S(1)} collective-permute-done((bf16[2,144,1024]{2,1,0:T(8,128)(2,1)S(1)}, bf16[2,144,1024]{2,1,0:T(8,128)(2,1)S(1)}, u32[]{:S(2)}, u32[]{:S(2)}) %collective-permute-start.1) | collective-permute-done | bytes 589856 | tf_op jit(solution)/shard_map/ppermute | solution.py:611
  66.4 3.5 collective-permute-start.2
  71.5 25.3 %collective-permute-done.2.refs_1_ = bf16[4,144,1024]{2,1,0:T(8,128)(2,1)} collective-permute-done((bf16[4,144,1024]{2,1,0:T(8,128)(2,1)S(1)}, bf16[4,144,1024]{2,1,0:T(8,128)(2,1)}, u32[]{:S(2)}, u32[]{:S(2)}) %collective-permute-start.2) | collective-permute-done | bytes 1179680 | tf_op jit(solution)/shard_map/ppermute | solution.py:615
  96.9 25.8 %collective-permute-done.3.refs_2_ = bf16[4,144,1024]{2,1,0:T(8,128)(2,1)} collective-permute-done((bf16[4,144,1024]{2,1,0:T(8,128)(2,1)S(1)}, bf16[4,144,1024]{2,1,0:T(8,128)(2,1)}, u32[]{:S(2)}, u32[]{:S(2)}) %collective-permute-start.3) | collective-permute-done | bytes 1179680 | tf_op jit(solution)/shard_map/ppermute | solution.py:615
  123.2 4.1 copy_convert_fusion
  127.4 4.4 all-to-all-start.2
  133.5 7.3 shard_map.314
  143.1 25.5 %shard_map.315 = (bf16[768,1024]{1,0:T(8,128)(2,1)}, bf16[512,1024]{1,0:T(8,128)(2,1)S(1)}, bf16[512,1024]{1,0:T(8,128)(2,1)S(1)}, bf16[512,1024]{1,0:T(8,128)(2...) custom-call(s32[1,1]{1,0:T(1,128)} %bitcast.111.length, ...), custom_call_target="tpu_custom_call" | custom-call | flops 1000000 | bytes 100000 | tf_op jit(solution)/shard_map/pallas_call | solution.py:122
  174.3 4.4 all-to-all-start.1
  181.6 25.5 %shard_map.317 = (bf16[768,1024]{1,0:T(8,128)(2,1)}, bf16[512,1024]{1,0:T(8,128)(2,1)S(1)}, bf16[512,1024]{1,0:T(8,128)(2,1)S(1)}, bf16[512,1024]{1,0:T(8,128)(2...) custom-call(s32[1,1]{1,0:T(1,128)} %bitcast.110.length, ...), custom_call_target="tpu_custom_call" | custom-call | flops 1000000 | bytes 100000 | tf_op jit(solution)/shard_map/pallas_call | solution.py:122
  212.7 4.3 all-to-all-start.3
  218.4 5.5 shard_map.316.refs_0_
  223.9 3.4 collective-permute-start.9
  231.8 6.2 all-to-all-done.3
  238.1 2.7 copy.116
  240.8 5.4 shard_map.318.refs_0_
  246.2 3.4 collective-permute-start.16
  249.6 99.1 %collective-permute-done.9 = bf16[2,384,1024]{2,1,0:T(8,128)(2,1)S(1)} collective-permute-done((bf16[2,384,1024]{2,1,0:T(8,128)(2,1)}, bf16[2,384,1024]{2,1,0:T(8,128)(2,1)S(1)}, u32[]{:S(2)}, u32[]{:S(2)}) %collective-permute-start.9) | collective-permute-done | bytes 1572896 | tf_op jit(solution)/shard_map/ppermute | solution.py:720
  348.7 33.5 %collective-permute-done.10.refs_7_.refs_9_ = bf16[4,1024,1024]{2,1,0:T(8,128)(2,1)} collective-permute-done((bf16[4,1024,1024]{2,1,0:T(8,128)(2,1)}, bf16[4,1024,1024]{2,1,0:T(8,128)(2,1)}, u32[]{:S(2)}, u32[]{:S(2)}) %collective-permute-start.10) | collective-permute-done | bytes 8388640 | tf_op jit(solution)/shard_map/ppermute | solution.py:687
  382.2 53.6 %shard_map.319 = (bf16[2,384,1024]{2,1,0:T(8,128)(2,1)}, bf16[2,384,1024]{2,1,0:T(8,128)(2,1)}, bf16[2,384,1024]{2,1,0:T(8,128)(2,1)}, bf16[2,384,1024]{2,1,0:T(...) custom-call(s32[1]{0:T(128)} %bitcast.4._, ...), custom_call_target="tpu_custom_call" | custom-call | flops 1000000 | bytes 100000 | tf_op jit(solution)/shard_map/pallas_call | solution.py:576
  441.5 64.0 %shard_map.322 = (bf16[2,384,1024]{2,1,0:T(8,128)(2,1)}, bf16[2,384,1024]{2,1,0:T(8,128)(2,1)}, bf16[2,384,1024]{2,1,0:T(8,128)(2,1)}, bf16[2,384,1024]{2,1,0:T(...) custom-call(s32[1]{0:T(128)} %bitcast.4._, ...), custom_call_target="tpu_custom_call" | custom-call | flops 1000000 | bytes 100000 | tf_op jit(solution)/shard_map/pallas_call | solution.py:576
  508.9 8.2 shard_map.320
  517.1 2.8 copy.121
  519.9 5.2 all-to-all-start.4
  525.1 21.0 %all-to-all-done.4 = bf16[2,8,48,1024]{3,2,0,1:T(8,128)(2,1)S(1)} async-done(((bf16[2,8,48,1024]{3,2,0,1:T(8,128)(2,1)}), bf16[2,8,48,1024]{3,2,0,1:T(8,128)(2,1)S(1)}, u32[]{:S(2)}, u32[]{:S(2)}) %all-to-all-start.4) | async-done | bytes 1572896 | tf_op jit(solution)/shard_map/all_to_all | solution.py:752
  547.2 45.9 %shard_map.321 = (bf16[768,1024]{1,0:T(8,128)(2,1)}, bf16[16,32,1024]{2,1,0:T(8,128)(2,1)}, bf16[16,32,1024]{2,1,0:T(8,128)(2,1)}, bf16[16,32,1024]{2,1,0:T(8,12...) custom-call(s32[1,1]{1,0:T(1,128)} %bitcast.111.length, ...), custom_call_target="tpu_custom_call" | custom-call | flops 1000000 | bytes 100000 | tf_op jit(solution)/shard_map/pallas_call | solution.py:261
  593.2 8.6 %shard_map.323 = (f32[2,384,1024]{2,1,0:T(8,128)}, bf16[2,384,1024]{2,1,0:T(8,128)(2,1)}, f32[8,1024]{1,0:T(8,128)}) custom-call(s32[1]{0:T(128)} %bitcast.4._, bf16[2,2,384,1024]{3,2,1,0:T(8,128)(2,1)} %bitcast.181, bf16[2,384,1024]{2,1,0:T(8,128)(2,1)} %bitcast.188, bf16[2,384,1024]{2,1,0:T(8,128)(2,1)} %get-tuple-element.127.gx, ...), custom_call_target="tpu_custom_call" | custom-call | flops 1000000 | bytes 100000 | tf_op jit(solution)/shard_map/pallas_call | solution.py:444
  601.8 2.7 copy.126
  604.5 3.6 all-to-all-start.5
  609.3 19.8 %all-to-all-done.5 = bf16[2,8,48,1024]{3,2,0,1:T(8,128)(2,1)S(1)} async-done(((bf16[2,8,48,1024]{3,2,0,1:T(8,128)(2,1)}), bf16[2,8,48,1024]{3,2,0,1:T(8,128)(2,1)S(1)}, u32[]{:S(2)}, u32[]{:S(2)}) %all-to-all-start.5) | async-done | bytes 1572896 | tf_op jit(solution)/shard_map/all_to_all | solution.py:752
  629.1 4.3 all-to-all-start.6
  636.4 45.9 %shard_map.324 = (bf16[768,1024]{1,0:T(8,128)(2,1)}, bf16[16,32,1024]{2,1,0:T(8,128)(2,1)}, bf16[16,32,1024]{2,1,0:T(8,128)(2,1)}, bf16[16,32,1024]{2,1,0:T(8,12...) custom-call(s32[1,1]{1,0:T(1,128)} %bitcast.110.length, ...), custom_call_target="tpu_custom_call" | custom-call | flops 1000000 | bytes 100000 | tf_op jit(solution)/shard_map/pallas_call | solution.py:261
  684.8 4.5 all-to-all-start.7
  692.4 8.6 %shard_map.325 = (bf16[528,1024]{1,0:T(8,128)(2,1)}, bf16[528,1024]{1,0:T(8,128)(2,1)}, bf16[528,1024]{1,0:T(8,128)(2,1)}, bf16[528,1024]{1,0:T(8,128)(2,1)}) custom-call(s32[1,1]{1,0:T(1,128)} %bitcast.1.place, bf16[16,32,1024]{2,1,0:T(8,128)(2,1)S(1)} %copy-done.13, bf16[16,32,1024]{2,1,0:T(8,128)(2,1)S(1)} %copy-done.14, ...), custom_call_target="tpu_custom_call" | custom-call | flops 1000000 | bytes 100000 | tf_op jit(solution)/shard_map/pallas_call | solution.py:333
  704.5 4.1 copy.129
  715.1 3.5 copy.134
  718.7 14.4 %collective-permute-done.22.refs_0_ = bf16[528,1024]{1,0:T(8,128)(2,1)S(1)} collective-permute-done((bf16[528,1024]{1,0:T(8,128)(2,1)}, bf16[528,1024]{1,0:T(8,128)(2,1)S(1)}, u32[]{:S(2)}, u32[]{:S(2)}) %collective-permute-start.22) | collective-permute-done | bytes 1081376 | tf_op jit(solution)/shard_map/ppermute | solution.py:770
  733.1 23.6 %collective-permute-done.24.refs_2_ = bf16[528,1024]{1,0:T(8,128)(2,1)S(1)} collective-permute-done((bf16[528,1024]{1,0:T(8,128)(2,1)}, bf16[528,1024]{1,0:T(8,128)(2,1)S(1)}, u32[]{:S(2)}, u32[]{:S(2)}) %collective-permute-start.24) | collective-permute-done | bytes 1081376 | tf_op jit(solution)/shard_map/ppermute | solution.py:770
  761.1 6.4 fusion.9
  769.5 31.7 %collective-permute-done.25 = bf16[272,1024]{1,0:T(8,128)(2,1)S(1)} collective-permute-done((bf16[272,1024]{1,0:T(8,128)(2,1)}, bf16[272,1024]{1,0:T(8,128)(2,1)S(1)}, u32[]{:S(2)}, u32[]{:S(2)}) %collective-permute-start.25) | collective-permute-done | bytes 557088 | tf_op jit(solution)/shard_map/ppermute | solution.py:772
  801.4 4.0 collective-permute-start.26
  808.7 15.5 %shard_map.327 = (f32[2,1024,1024]{2,1,0:T(8,128)}, f32[2,1024,1024]{2,1,0:T(8,128)}) custom-call(f32[2,1024,1024]{2,1,0:T(8,128)} %get-tuple-element.170.a, f32[2,1024,1024]{2,1,0:T(8,128)} %get-tuple-element.171.c, bf16[2,2,1024,1024]{3,2,1,0:T(8,128)(2,1)} %collective-permute-done.27.got), custom_call_target="tpu_custom_call", output_to_operand_aliasing={{0}: (0, {}), {1}: (1, {})} | custom-call | flops 1000000 | bytes 100000 | tf_op jit(solution)/shard_map/pallas_call | solution.py:389
  (259 shorter events, 73.8 us)
Async XLA Ops:
  13.5 26.3 %all-to-all-start = ((bf16[2,8,48,1024]{3,2,0,1:T(8,128)(2,1)}), bf16[2,8,48,1024]{3,2,0,1:T(8,128)(2,1)S(1)}, u32[]{:S(2)}, u32[]{:S(2)}) async-start(bf16[2,8,48,1024]{3,2,0,1:T(8,128)(2,1)} %get-tuple-element.187), calls=%async_computation | async-start | bytes 3145728 | tf_op jit(solution)/shard_map/all_to_all | solution.py:679
  18.8 227.4 %all-gather.9.cloned.1.call-start = ((), (), s32[]{:S(2)}) async-start(), calls=%async_computation.8 | async-start | bytes 9437184 | tf_op jit(solution)/shard_map/all_gather | solution.py:605
  19.4 9.4 %collective-permute-start = (bf16[1,144,1024]{2,1,0:T(8,128)(2,1)S(1)}, bf16[1,144,1024]{2,1,0:T(8,128)(2,1)S(1)}, u32[]{:S(2)}, u32[]{:S(2)}) collective-permute-start(bf16[1,144,1024]{2,1,0:T(8,128)(2,1)S(1)} %bitcast.218), channel_id=1, source_target_pairs={{0,1},{1,0},{2,3},{3,2},{4,5},{5,4},{6,7},{7,6},{8,9},{9,8},{10,11... | collective-permute-start | bytes 884744 | tf_op jit(solution)/shard_map/ppermute | solution.py:611
  39.8 25.8 %collective-permute-start.1 = (bf16[2,144,1024]{2,1,0:T(8,128)(2,1)S(1)}, bf16[2,144,1024]{2,1,0:T(8,128)(2,1)S(1)}, u32[]{:S(2)}, u32[]{:S(2)}) collective-permute-start(bf16[2,144,1024]{2,1,0:T(8,128)(2,1)S(1)} %pad_maximum_fusion.3), channel_id=1, source_target_pairs={{0,2},{1,3},{2,0},{3,1},{4,6},{5,7},{6,4},{7,5},{8,10},{9,11},{10,... | collective-permute-start | bytes 1769480 | tf_op jit(solution)/shard_map/ppermute | solution.py:611
  65.7 316.5 %collective-permute-start.10 = (bf16[4,1024,1024]{2,1,0:T(8,128)(2,1)}, bf16[4,1024,1024]{2,1,0:T(8,128)(2,1)}, u32[]{:S(2)}, u32[]{:S(2)}) collective-permute-start(bf16[4,1024,1024]{2,1,0:T(8,128)(2,1)} %pad_maximum_fusion), channel_id=1, source_target_pairs={{0,1},{1,0},{2,3},{3,2},{4,5},{5,4},{6,7},{7,6},{8,9},{9,8},{10,11... | collective-permute-start | bytes 25165832 | tf_op jit(solution)/shard_map/ppermute | solution.py:687
  66.4 30.4 %collective-permute-start.2 = (bf16[4,144,1024]{2,1,0:T(8,128)(2,1)S(1)}, bf16[4,144,1024]{2,1,0:T(8,128)(2,1)}, u32[]{:S(2)}, u32[]{:S(2)}) collective-permute-start(bf16[4,144,1024]{2,1,0:T(8,128)(2,1)S(1)} %constant_dynamic-update-slice_fusion.5.refs_0_), channel_id=1, source_target_pairs={{0,8},{4,12},{8,0},{12,4},{16,24},{20,28},{24,16},{28,20},{1,9},{5... | collective-permute-start | bytes 3538952 | tf_op jit(solution)/shard_map/ppermute | solution.py:615
  70.0 52.7 %collective-permute-start.3 = (bf16[4,144,1024]{2,1,0:T(8,128)(2,1)S(1)}, bf16[4,144,1024]{2,1,0:T(8,128)(2,1)}, u32[]{:S(2)}, u32[]{:S(2)}) collective-permute-start(bf16[4,144,1024]{2,1,0:T(8,128)(2,1)S(1)} %constant_dynamic-update-slice_fusion.5.refs_0_), channel_id=1, source_target_pairs={{0,16},{4,20},{8,24},{12,28},{16,0},{20,4},{24,8},{28,12},{1,17},{... | collective-permute-start | bytes 3538952 | tf_op jit(solution)/shard_map/ppermute | solution.py:615
  70.3 52.4 %collective-permute-start.4 = (bf16[4,144,1024]{2,1,0:T(8,128)(2,1)S(1)}, bf16[4,144,1024]{2,1,0:T(8,128)(2,1)}, u32[]{:S(2)}, u32[]{:S(2)}) collective-permute-start(bf16[4,144,1024]{2,1,0:T(8,128)(2,1)S(1)} %constant_dynamic-update-slice_fusion.5.refs_0_), channel_id=1, source_target_pairs={{0,24},{4,28},{8,16},{12,20},{16,8},{20,12},{24,0},{28,4},{1,25},{... | collective-permute-start | bytes 3538952 | tf_op jit(solution)/shard_map/ppermute | solution.py:615
  71.5 62.0 %collective-permute-start.5 = (bf16[4,144,1024]{2,1,0:T(8,128)(2,1)S(1)}, bf16[4,144,1024]{2,1,0:T(8,128)(2,1)}, u32[]{:S(2)}, u32[]{:S(2)}) collective-permute-start(bf16[4,144,1024]{2,1,0:T(8,128)(2,1)S(1)} %constant_dynamic-update-slice_fusion.5.refs_0_), channel_id=1, source_target_pairs={{0,4},{4,0},{8,12},{12,8},{16,20},{20,16},{24,28},{28,24},{1,5},{5... | collective-permute-start | bytes 3538952 | tf_op jit(solution)/shard_map/ppermute | solution.py:616
  96.9 36.6 %collective-permute-start.6 = (bf16[4,144,1024]{2,1,0:T(8,128)(2,1)}, bf16[4,144,1024]{2,1,0:T(8,128)(2,1)}, u32[]{:S(2)}, u32[]{:S(2)}) collective-permute-start(bf16[4,144,1024]{2,1,0:T(8,128)(2,1)} %collective-permute-done.2.refs_1_), channel_id=1, source_target_pairs={{0,4},{4,0},{8,12},{12,8},{16,20},{20,16},{24,28},{28,24},{1,5},{5... | collective-permute-start | bytes 3538952 | tf_op jit(solution)/shard_map/ppermute | solution.py:616
  122.7 10.8 %collective-permute-start.7 = (bf16[4,144,1024]{2,1,0:T(8,128)(2,1)}, bf16[4,144,1024]{2,1,0:T(8,128)(2,1)}, u32[]{:S(2)}, u32[]{:S(2)}) collective-permute-start(bf16[4,144,1024]{2,1,0:T(8,128)(2,1)} %collective-permute-done.3.refs_2_), channel_id=1, source_target_pairs={{0,4},{4,0},{8,12},{12,8},{16,20},{20,16},{24,28},{28,24},{1,5},{5... | collective-permute-start | bytes 3538952 | tf_op jit(solution)/shard_map/ppermute | solution.py:616
  122.7 10.8 %collective-permute-start.8 = (bf16[4,144,1024]{2,1,0:T(8,128)(2,1)}, bf16[4,144,1024]{2,1,0:T(8,128)(2,1)}, u32[]{:S(2)}, u32[]{:S(2)}) collective-permute-start(bf16[4,144,1024]{2,1,0:T(8,128)(2,1)} %collective-permute-done.4.refs_3_), channel_id=1, source_target_pairs={{0,4},{4,0},{8,12},{12,8},{16,20},{20,16},{24,28},{28,24},{1,5},{5... | collective-permute-start | bytes 3538952 | tf_op jit(solution)/shard_map/ppermute | solution.py:616
  127.4 46.9 %all-to-all-start.2 = ((bf16[2,8,48,1024]{3,2,0,1:T(8,128)(2,1)}), bf16[2,8,48,1024]{3,2,0,1:T(8,128)(2,1)}, u32[]{:S(2)}, u32[]{:S(2)}) async-start(bf16[2,8,48,1024]{3,2,0,1:T(8,128)(2,1)} %get-tuple-element.189), calls=%async_computation.2 | async-start | bytes 3145728 | tf_op jit(solution)/shard_map/all_to_all | solution.py:679
  132.6 49.0 %copy-start.22 = (s32[1,512]{1,0:T(1,128)}, s32[1,512]{1,0:T(1,128)S(1)}, u32[]{:S(2)}) copy-start(s32[1,512]{1,0:T(1,128)S(1)} %get-tuple-element.216.row) | copy-start | bytes 6148
  143.0 38.6 %copy-start.19 = (f32[8,1024]{1,0:T(8,128)}, f32[8,1024]{1,0:T(8,128)S(1)}, u32[]{:S(2)}) copy-start(f32[8,1024]{1,0:T(8,128)S(1)} %stack.21.small) | copy-start | bytes 98308
  174.3 38.4 %all-to-all-start.1 = ((bf16[16,48,1024]{2,1,0:T(8,128)(2,1)}), bf16[16,48,1024]{2,1,0:T(8,128)(2,1)S(1)}, u32[]{:S(2)}, u32[]{:S(2)}) async-start(bf16[16,48,1024]{2,1,0:T(8,128)(2,1)} %bitcast.211), calls=%async_computation.1 | async-start | bytes 3145728 | tf_op jit(solution)/shard_map/all_to_all | solution.py:715
  212.7 25.4 %all-to-all-start.3 = ((bf16[16,48,1024]{2,1,0:T(8,128)(2,1)}), bf16[16,48,1024]{2,1,0:T(8,128)(2,1)}, u32[]{:S(2)}, u32[]{:S(2)}) async-start(bf16[16,48,1024]{2,1,0:T(8,128)(2,1)} %bitcast.212), calls=%async_computation.3 | async-start | bytes 3145728 | tf_op jit(solution)/shard_map/all_to_all | solution.py:715
  217.0 376.2 %all-gather.11.cloned.1.call-start = ((), (), s32[]{:S(2)}) async-start(), calls=%async_computation.9 | async-start | bytes 4718592 | tf_op jit(solution)/shard_map/all_gather | solution.py:605
  223.9 124.8 %collective-permute-start.9 = (bf16[2,384,1024]{2,1,0:T(8,128)(2,1)}, bf16[2,384,1024]{2,1,0:T(8,128)(2,1)S(1)}, u32[]{:S(2)}, u32[]{:S(2)}) collective-permute-start(bf16[2,384,1024]{2,1,0:T(8,128)(2,1)} %shard_map.316.refs_0_), channel_id=1, source_target_pairs={{0,2},{1,3},{2,0},{3,1},{4,6},{5,7},{6,4},{7,5},{8,10},{9,11},{10,... | collective-permute-start | bytes 4718600 | tf_op jit(solution)/shard_map/ppermute | solution.py:720
  246.2 194.1 %collective-permute-start.16 = (bf16[2,384,1024]{2,1,0:T(8,128)(2,1)}, bf16[2,384,1024]{2,1,0:T(8,128)(2,1)S(1)}, u32[]{:S(2)}, u32[]{:S(2)}) collective-permute-start(bf16[2,384,1024]{2,1,0:T(8,128)(2,1)} %shard_map.318.refs_0_), channel_id=1, source_target_pairs={{0,2},{1,3},{2,0},{3,1},{4,6},{5,7},{6,4},{7,5},{8,10},{9,11},{10,... | collective-permute-start | bytes 4718600 | tf_op jit(solution)/shard_map/ppermute | solution.py:723
  348.7 33.5 %copy-start.32 = (bf16[2,384,1024]{2,1,0:T(8,128)(2,1)}, bf16[2,384,1024]{2,1,0:T(8,128)(2,1)S(1)}, u32[]{:S(2)}) copy-start(bf16[2,384,1024]{2,1,0:T(8,128)(2,1)S(1)} %collective-permute-done.9) | copy-start | bytes 4718596
  435.9 70.4 %collective-permute-start.11 = (bf16[2,384,1024]{2,1,0:T(8,128)(2,1)}, bf16[2,384,1024]{2,1,0:T(8,128)(2,1)S(1)}, u32[]{:S(2)}, u32[]{:S(2)}) collective-permute-start(bf16[2,384,1024]{2,1,0:T(8,128)(2,1)} %get-tuple-element.105), channel_id=1, source_target_pairs={{0,2},{1,3},{2,0},{3,1},{4,6},{5,7},{6,4},{7,5},{8,10},{9,11},{10,... | collective-permute-start | bytes 4718600 | tf_op jit(solution)/shard_map/ppermute | solution.py:734
  506.2 254.9 %all-gather.13.cloned.1.call-start = ((), (), s32[]{:S(2)}) async-start(), calls=%async_computation.10 | async-start | bytes 4718592 | tf_op jit(solution)/shard_map/all_gather | solution.py:605
  507.0 301.7 %collective-permute-start.27 = (bf16[2,2,1024,1024]{3,2,1,0:T(8,128)(2,1)}, bf16[2,2,1024,1024]{3,2,1,0:T(8,128)(2,1)}, u32[]{:S(2)}, u32[]{:S(2)}) collective-permute-start(bf16[2,2,1024,1024]{3,2,1,0:T(8,128)(2,1)} %get-tuple-element.172), channel_id=1, source_target_pairs={{0,1},{1,0},{2,3},{3,2},{4,5},{5,4},{6,7},{7,6},{8,9},{9,8},{10,11... | collective-permute-start | bytes 25165832 | tf_op jit(solution)/shard_map/ppermute | solution.py:742
  519.9 26.2 %all-to-all-start.4 = ((bf16[2,8,48,1024]{3,2,0,1:T(8,128)(2,1)}), bf16[2,8,48,1024]{3,2,0,1:T(8,128)(2,1)S(1)}, u32[]{:S(2)}, u32[]{:S(2)}) async-start(bf16[2,8,48,1024]{3,2,0,1:T(8,128)(2,1)} %copy.121), calls=%async_computation.4 | async-start | bytes 3145728 | tf_op jit(solution)/shard_map/all_to_all | solution.py:752
  604.5 24.5 %all-to-all-start.5 = ((bf16[2,8,48,1024]{3,2,0,1:T(8,128)(2,1)}), bf16[2,8,48,1024]{3,2,0,1:T(8,128)(2,1)S(1)}, u32[]{:S(2)}, u32[]{:S(2)}) async-start(bf16[2,8,48,1024]{3,2,0,1:T(8,128)(2,1)} %copy.126), calls=%async_computation.5 | async-start | bytes 3145728 | tf_op jit(solution)/shard_map/all_to_all | solution.py:752
  608.1 153.0 %all-gather.15.cloned.1.call-start = ((), (), s32[]{:S(2)}) async-start(), calls=%async_computation.11 | async-start | bytes 4718592 | tf_op jit(solution)/shard_map/all_gather | solution.py:605
  608.2 75.1 %collective-permute-start.12 = (bf16[16,32,1024]{2,1,0:T(8,128)(2,1)}, bf16[16,32,1024]{2,1,0:T(8,128)(2,1)}, u32[]{:S(2)}, u32[]{:S(2)}) collective-permute-start(bf16[16,32,1024]{2,1,0:T(8,128)(2,1)} %get-tuple-element.117), channel_id=1, source_target_pairs={{0,4},{4,0},{8,12},{12,8},{16,20},{20,16},{24,28},{28,24},{1,5},{5... | collective-permute-start | bytes 3145736 | tf_op jit(solution)/shard_map/ppermute | solution.py:765
  608.5 75.1 %collective-permute-start.13 = (bf16[16,32,1024]{2,1,0:T(8,128)(2,1)}, bf16[16,32,1024]{2,1,0:T(8,128)(2,1)}, u32[]{:S(2)}, u32[]{:S(2)}) collective-permute-start(bf16[16,32,1024]{2,1,0:T(8,128)(2,1)} %get-tuple-element.118), channel_id=1, source_target_pairs={{0,4},{4,0},{8,12},{12,8},{16,20},{20,16},{24,28},{28,24},{1,5},{5... | collective-permute-start | bytes 3145736 | tf_op jit(solution)/shard_map/ppermute | solution.py:765
  608.7 75.1 %collective-permute-start.14 = (bf16[16,32,1024]{2,1,0:T(8,128)(2,1)}, bf16[16,32,1024]{2,1,0:T(8,128)(2,1)}, u32[]{:S(2)}, u32[]{:S(2)}) collective-permute-start(bf16[16,32,1024]{2,1,0:T(8,128)(2,1)} %get-tuple-element.119), channel_id=1, source_target_pairs={{0,4},{4,0},{8,12},{12,8},{16,20},{20,16},{24,28},{28,24},{1,5},{5... | collective-permute-start | bytes 3145736 | tf_op jit(solution)/shard_map/ppermute | solution.py:765
  609.0 75.1 %collective-permute-start.15 = (bf16[16,32,1024]{2,1,0:T(8,128)(2,1)}, bf16[16,32,1024]{2,1,0:T(8,128)(2,1)}, u32[]{:S(2)}, u32[]{:S(2)}) collective-permute-start(bf16[16,32,1024]{2,1,0:T(8,128)(2,1)} %get-tuple-element.120), channel_id=1, source_target_pairs={{0,4},{4,0},{8,12},{12,8},{16,20},{20,16},{24,28},{28,24},{1,5},{5... | collective-permute-start | bytes 3145736 | tf_op jit(solution)/shard_map/ppermute | solution.py:765
  629.1 55.8 %all-to-all-start.6 = ((bf16[16,48,1024]{2,1,0:T(8,128)(2,1)}), bf16[16,48,1024]{2,1,0:T(8,128)(2,1)}, u32[]{:S(2)}, u32[]{:S(2)}) async-start(bf16[16,48,1024]{2,1,0:T(8,128)(2,1)} %bitcast.66), calls=%async_computation.6 | async-start | bytes 3145728 | tf_op jit(solution)/shard_map/all_to_all | solution.py:758
  636.4 45.9 %copy-start.42 = (f32[8,1024]{1,0:T(8,128)S(1)}, f32[8,1024]{1,0:T(8,128)}, u32[]{:S(2)}) copy-start(f32[8,1024]{1,0:T(8,128)} %get-tuple-element.148) | copy-start | bytes 98308
  683.3 1.3 collective-permute-start.21
  683.6 5.8 collective-permute-start.17
  683.9 5.5 collective-permute-start.18
  684.2 5.5 collective-permute-start.19
  684.6 6.6 collective-permute-start.20
  684.8 30.3 %all-to-all-start.7 = ((bf16[16,48,1024]{2,1,0:T(8,128)(2,1)}), bf16[16,48,1024]{2,1,0:T(8,128)(2,1)}, u32[]{:S(2)}, u32[]{:S(2)}) async-start(bf16[16,48,1024]{2,1,0:T(8,128)(2,1)} %bitcast.210), calls=%async_computation.7 | async-start | bytes 3145728 | tf_op jit(solution)/shard_map/all_to_all | solution.py:758
  701.0 32.1 %collective-permute-start.22 = (bf16[528,1024]{1,0:T(8,128)(2,1)}, bf16[528,1024]{1,0:T(8,128)(2,1)S(1)}, u32[]{:S(2)}, u32[]{:S(2)}) collective-permute-start(bf16[528,1024]{1,0:T(8,128)(2,1)} %get-tuple-element.153), channel_id=1, source_target_pairs={{0,8},{4,12},{8,0},{12,4},{16,24},{20,28},{24,16},{28,20},{1,9},{5... | collective-permute-start | bytes 3244040 | tf_op jit(solution)/shard_map/ppermute | solution.py:770
  702.8 30.3 %collective-permute-start.23 = (bf16[528,1024]{1,0:T(8,128)(2,1)}, bf16[528,1024]{1,0:T(8,128)(2,1)S(1)}, u32[]{:S(2)}, u32[]{:S(2)}) collective-permute-start(bf16[528,1024]{1,0:T(8,128)(2,1)} %get-tuple-element.154), channel_id=1, source_target_pairs={{0,16},{4,20},{8,24},{12,28},{16,0},{20,4},{24,8},{28,12},{1,17},{... | collective-permute-start | bytes 3244040 | tf_op jit(solution)/shard_map/ppermute | solution.py:770
  704.2 52.5 %collective-permute-start.24 = (bf16[528,1024]{1,0:T(8,128)(2,1)}, bf16[528,1024]{1,0:T(8,128)(2,1)S(1)}, u32[]{:S(2)}, u32[]{:S(2)}) collective-permute-start(bf16[528,1024]{1,0:T(8,128)(2,1)} %get-tuple-element.155), channel_id=1, source_target_pairs={{0,24},{4,28},{8,16},{12,20},{16,8},{20,12},{24,0},{28,4},{1,25},{... | collective-permute-start | bytes 3244040 | tf_op jit(solution)/shard_map/ppermute | solution.py:770
  715.1 41.6 %copy-start.2 = (bf16[528,1024]{1,0:T(8,128)(2,1)S(1)}, bf16[528,1024]{1,0:T(8,128)(2,1)}, u32[]{:S(2)}) copy-start(bf16[528,1024]{1,0:T(8,128)(2,1)} %get-tuple-element.152.first) | copy-start | bytes 3244036
  759.0 42.2 %collective-permute-start.25 = (bf16[272,1024]{1,0:T(8,128)(2,1)}, bf16[272,1024]{1,0:T(8,128)(2,1)S(1)}, u32[]{:S(2)}, u32[]{:S(2)}) collective-permute-start(bf16[272,1024]{1,0:T(8,128)(2,1)} %get-tuple-element.157), channel_id=1, source_target_pairs={{0,2},{1,3},{2,0},{3,1},{4,6},{5,7},{6,4},{7,5},{8,10},{9,11},{10,... | collective-permute-start | bytes 1671176 | tf_op jit(solution)/shard_map/ppermute | solution.py:772
  767.5 33.6 %copy-start.18 = (f32[256,1024]{1,0:T(8,128)S(1)}, f32[256,1024]{1,0:T(8,128)}, u32[]{:S(2)}) copy-start(f32[256,1024]{1,0:T(8,128)} %copy-done.17) | copy-start | bytes 3145732
  767.5 37.8 %copy-start.30 = (f32[2,384,1024]{2,1,0:T(8,128)S(1)}, f32[2,384,1024]{2,1,0:T(8,128)}, u32[]{:S(2)}) copy-start(f32[2,384,1024]{2,1,0:T(8,128)} %get-tuple-element.167) | copy-start | bytes 9437188
  769.5 35.9 %copy-start.25 = (f32[8,2,48,1024]{3,2,0,1:T(8,128)S(1)}, f32[8,2,48,1024]{3,2,0,1:T(8,128)}, u32[]{:S(2)}) copy-start(f32[8,2,48,1024]{3,2,0,1:T(8,128)} %copy.134) | copy-start | bytes 9437188
  801.4 22.8 %collective-permute-start.26 = (bf16[148,1024]{1,0:T(8,128)(2,1)S(1)}, bf16[148,1024]{1,0:T(8,128)(2,1)S(1)}, u32[]{:S(2)}, u32[]{:S(2)}) collective-permute-start(bf16[148,1024]{1,0:T(8,128)(2,1)S(1)} %pad_maximum_fusion.4), channel_id=1, source_target_pairs={{0,1},{1,0},{2,3},{3,2},{4,5},{5,4},{6,7},{7,6},{8,9},{9,8},{10,11... | collective-permute-start | bytes 909320 | tf_op jit(solution)/shard_map/ppermute | solution.py:788
  (47 other events, 254.0 us)
Sparse Core Ops, SparseCore 0:
  71.6 148.3 all-gather.8
  506.4 80.8 all-gather.10
  588.8 78.7 all-gather.12
  669.0 78.7 all-gather.14
